TPU v7x, 32 devices: a whole 2x2x4 slice. The times are simulated.
32 devices in a mesh: dom: 4 (over x, core), mem: 8 (over z, y).
Axes of the slice: x: 2, y: 2, z: 4, core: 2. Of those that a mesh axis runs over, the one named last changes fastest.
Arguments:
- state: float32 [1024, 32768], P('mem', 'dom'), may hold values from -14 to 14, as said below
- obs_ensemble: float32 [1024, 2048], P('mem', 'dom'), may hold values from -14 to 14, as said below
- innovations: float32 [1024, 2048], P('mem', 'dom'), may hold values from -6 to 6
- obs_coords: float32 [2, 2048], P(None, 'dom'), may hold values from 0 to 4, as said below
- tile_list: int32 [4, 8, 2, 48], P('dom', 'mem'), may hold values from 0 to 11, as said below
- tile_counts: int32 [4, 8], P('dom', 'mem'), may hold values from 24 to 48, as said below
Outputs:
- analysis: float32 [1024, 32768], P(None, ('dom', 'mem'))
Inputs may be any that keep to these rules, and one draw needn't show every extreme that they name: `state`: forecast values of each gridpoint: an offset plus a spread of its own times a bounded noise. `obs_ensemble`: Observation-space values of each observation: an offset plus a spread of its own times a bounded noise. `obs_coords`: the observations of domain d have a first coordinate within [d, d + 1) and a second within [0, 1). `tile_list`: slots k * 6 to (k + 1) * 6 - 1 name point block k (of 8) and 6 distinct observation blocks of the window of 12 blocks: the left neighbour domain's, the own domain's, the right neighbour domain's, domains on a cycle. `tile_counts`: slots below the count are live. Some group has all 48 live, some other group half of them.
All inputs are finite; a program needn't handle non-finite values.
Results may differ from a plain program's by a relative error of at most 0.0002.
Values sent between devices are 32-bit elements; how exact they have to be, the bound alone decides.
No kernel may reach another device: no remote copies, remote signals or barrier semaphores. Data moves between devices by JAX's collectives and lax.ppermute only.
A program may use at most 192 MiB of HBM per device.

v0:
```python
import jax
import jax.numpy as jnp
from jax import lax
from jax.sharding import PartitionSpec as P

taper_reach = 0.6
highest = lax.Precision.HIGHEST


def padded(block, sides, width):
    for axis, dim in sides:
        count = lax.axis_size(axis)
        forward = [(i, i + 1) for i in range(count - 1)]
        forward.append((count - 1, 0))
        backward = [(target, source) for source, target in forward]
        low = lax.ppermute(
            lax.slice_in_dim(block, block.shape[dim] - width, None, axis=dim), axis, forward
        )
        high = lax.ppermute(lax.slice_in_dim(block, 0, width, axis=dim), axis, backward)
        block = jnp.concatenate([low, block, high], axis=dim)
    return block


def taper_of(point_x, point_y, obs_x, obs_y, cycle_size):
    gap_x = jnp.abs(point_x[:, :, None] - obs_x[:, None, :])
    gap_x = jnp.minimum(gap_x, cycle_size - gap_x)
    gap_y = point_y[:, :, None] - obs_y[:, None, :]
    return jnp.exp(-(gap_x * gap_x + gap_y * gap_y) / (2.0 * taper_reach * taper_reach))


def shards(state, obs_ensemble, innovations, obs_coords, tile_list, tile_counts):
    members_local = state.shape[0]
    groups = lax.axis_size("mem")
    per_domain = state.shape[1]
    per_device = per_domain // groups
    obs_local = obs_ensemble.shape[1]
    members = members_local * groups
    full_ens, full_innov = (
        lax.all_gather(obs_ensemble, "mem", axis=0, tiled=True),
        lax.all_gather(innovations, "mem", axis=0, tiled=True),
    )
    anomalies = full_ens - jnp.mean(full_ens, axis=0, keepdims=True)
    stacked = jnp.concatenate([anomalies, full_innov, obs_coords], axis=0)
    window = padded(stacked, (("dom", 1),), obs_local)
    anom_win = window[:members]
    innov_win = window[members : 2 * members]
    coord_win = window[2 * members :]
    states = lax.all_to_all(state, "mem", split_axis=1, concat_axis=0, tiled=True)
    tile_side = 128
    nblocks = per_device // tile_side
    wblocks = 3 * obs_local // tile_side
    point_grid = states.reshape(members, nblocks, tile_side)
    anom_grid = anom_win.reshape(members, wblocks, tile_side)
    innov_grid = innov_win.reshape(members, wblocks, tile_side)
    obs_x = coord_win[0].reshape(wblocks, tile_side)
    obs_y = coord_win[1].reshape(wblocks, tile_side)
    domain = lax.axis_index("dom")
    start_index = lax.axis_index("mem") * per_device
    within = start_index + jnp.arange(per_device, dtype=jnp.int32)
    pts_x = (domain.astype(jnp.float32) + ((within % 32).astype(jnp.float32) + 0.5) / 32.0).reshape(
        nblocks, tile_side
    )
    pts_y = (((within // 32).astype(jnp.float32) + 0.5) / float(per_domain // 32)).reshape(
        nblocks, tile_side
    )
    cycle_size = float(lax.axis_size("dom"))
    pblocks = tile_list[0, 0, 0]
    oblocks = tile_list[0, 0, 1]
    tiles_total = pblocks.shape[0]
    live_mask = (jnp.arange(tiles_total, dtype=jnp.int32) < tile_counts[0, 0]).astype(jnp.float32)
    batch_size = min(tiles_total, 24)
    batches = tiles_total // batch_size
    block_ids = jnp.arange(nblocks, dtype=jnp.int32)

    def tile_batch(change, batch):
        point_ids, obs_ids, alive = batch
        x_blocks = jnp.take(point_grid, point_ids, axis=1)
        y_blocks = jnp.take(anom_grid, obs_ids, axis=1)
        w_blocks = jnp.take(innov_grid, obs_ids, axis=1)
        covariance = jnp.einsum("mti,mtj->tij", x_blocks, y_blocks, precision=highest) / (
            members - 1
        )
        taper = taper_of(
            jnp.take(pts_x, point_ids, axis=0),
            jnp.take(pts_y, point_ids, axis=0),
            jnp.take(obs_x, obs_ids, axis=0),
            jnp.take(obs_y, obs_ids, axis=0),
            cycle_size,
        )
        weights = taper * covariance * alive[:, None, None]
        increment = jnp.einsum("mtj,tij->mti", w_blocks, weights, precision=highest)
        onehot = (point_ids[:, None] == block_ids[None, :]).astype(jnp.float32)
        change = change + jnp.einsum("mti,tp->mpi", increment, onehot, precision=highest)
        return (change, None)

    change, _ = lax.scan(
        tile_batch,
        jnp.zeros((members, nblocks, tile_side), jnp.float32),
        (
            pblocks.reshape(batches, batch_size),
            oblocks.reshape(batches, batch_size),
            live_mask.reshape(batches, batch_size),
        ),
    )
    return states + change.reshape(members, per_device)


def solution(mesh):
    return jax.shard_map(
        shards,
        mesh=mesh,
        in_specs=(
            P("mem", "dom"),
            P("mem", "dom"),
            P("mem", "dom"),
            P(None, "dom"),
            P("dom", "mem", None, None),
            P("dom", "mem"),
        ),
        out_specs=P(None, ("dom", "mem")),
        check_vma=False,
    )
```

profile of v0, /device:TPU:0, one launch (start us, length us, event | category | flops | bytes accessed | tf_op | source)
XLA Modules:
  0.0 524.2 jit_solution(14135043123592323151)
XLA Ops:
  8.4 1.8 copy.27
  10.3 4.8 copy.42
  15.1 7.4 %all-to-all-start = ((f32[128,8,1024]{2,0,1:T(8,128)}), f32[128,8,1024]{2,0,1:T(8,128)}, u32[]{:S(2)}, u32[]{:S(2)}) async-start(f32[128,8,1024]{2,0,1:T(8,128)} %bitcast.78), calls=%async_computation | async-start | bytes 8388608 | tf_op jit(solution)/shard_map/all_to_all | solution.py:48
  22.6 103.9 %all-gather.3.cloned.1.call-done = f32[1024,512]{0,1:T(8,128)} async-done(((f32[128,512]{0,1:T(8,128)}), f32[1024,512]{0,1:T(8,128)}) %all-gather.3.cloned.1.call-update) | async-done | bytes 2097168 | tf_op jit(solution)/shard_map/all_gather | solution.py:39
  130.1 51.9 %all-gather.5.cloned.1.call-done = f32[1024,512]{0,1:T(8,128)} async-done(((f32[128,512]{0,1:T(8,128)}), f32[1024,512]{0,1:T(8,128)}) %all-gather.5.cloned.1.call-update) | async-done | bytes 2097168 | tf_op jit(solution)/shard_map/all_gather | solution.py:40
  182.0 4.0 pad_maximum_fusion.5
  186.0 5.7 %copy.29 = f32[2050,512]{1,0:T(8,128)} copy(f32[2050,512]{0,1:T(8,128)} %pad_maximum_fusion.5) | data formatting | bytes 8396800 | tf_op jit(solution)/shard_map/concatenate | solution.py:43
  194.3 3.2 copy.38
  197.5 2.8 copy.33
  200.3 83.1 %collective-permute-done = f32[2050,512]{1,0:T(8,128)} collective-permute-done((f32[2050,512]{1,0:T(8,128)}, f32[2050,512]{1,0:T(8,128)}, u32[]{:S(2)}, u32[]{:S(2)}) %collective-permute-start) | collective-permute-done | bytes 4198432 | tf_op jit(solution)/shard_map/ppermute | solution.py:16
  283.4 5.5 %copy.31 = f32[2050,512]{0,1:T(8,128)} copy(f32[2050,512]{1,0:T(8,128)} %collective-permute-done) | data formatting | bytes 8396800 | tf_op jit(solution)/shard_map/ppermute | solution.py:16
  288.9 5.5 %copy.32 = f32[2050,512]{0,1:T(8,128)} copy(f32[2050,512]{1,0:T(8,128)} %collective-permute-done.1) | data formatting | bytes 8396800 | tf_op jit(solution)/shard_map/ppermute | solution.py:19
  294.3 8.6 %pad_maximum_fusion = (f32[1024,1536]{0,1:T(8,128)}, f32[1024,1536]{0,1:T(8,128)}) fusion(f32[2050,512]{0,1:T(8,128)} %copy.32, f32[2050,512]{0,1:T(8,128)} %copy.31, f32[2,512]{0,1:T(8,128)S(1)} %copy.28, f32[1024,512]{0,1:T(8,128)} %all-gather.5.cloned.1.call-done, f32[1024,512]{0,1:T(8,128)S(1)} %broadcast_subtract_fusion), kind=kLoop, calls=%fused_computation.90 | loop fusion | flops 12582912 | bytes 25178112 | tf_op jit(solution)/shard_map/concatenate | solution.py:20
  302.9 6.6 %copy.34 = f32[1024,12,128]{2,0,1:T(8,128)} copy(f32[1024,12,128]{0,2,1:T(8,128)} %bitcast.77) | data formatting | bytes 12582912
  309.6 6.6 %copy.35 = f32[1024,12,128]{2,0,1:T(8,128)} copy(f32[1024,12,128]{0,2,1:T(8,128)} %bitcast.76) | data formatting | bytes 12582912
  316.2 1.9 maximum_reduce_fusion
  318.1 192.2 %while.13 = (s32[]{:T(128)}, f32[1024,8,128]{2,1,0:T(8,128)}, s32[2,24]{1,0:T(2,128)S(1)}, s32[2,24]{1,0:T(2,128)S(1)}, f32[12,128]{1,0:T(8,128)S(1)}, /*index=5...) while((s32[]{:T(128)}, f32[1024,8,128]{2,1,0:T(8,128)}, ...), condition=%wide.region_2.6_spmd.clone.clone.clone, body=%wide.region_1.5_spmd.clone.clone.clone.sunk | while | flops 9982357504 | bytes 175380896 | solution.py:96
  318.4 9.9 %gather_fusion.1 = f32[24,1024,128]{2,1,0:T(8,128)} fusion(f32[1024,12,128]{2,0,1:T(8,128)} %get-tuple-element.394, s32[1024]{0:T(1024)S(1)} %pad_clamp_fusion.6), kind=kCustom, calls=%fused_computation.2.clone.clone.1 | custom fusion | bytes 25165920 | tf_op jit(solution)/shard_map/while/body/eval_jaxpr/jit(_take)/gather | solution.py:78
  328.3 9.3 %gather_fusion.2 = f32[24,1024,128]{2,1,0:T(8,128)} fusion(f32[1024,8,128]{2,0,1:T(8,128)} %get-tuple-element.393, s32[1024]{0:T(1024)S(1)} %pad_clamp_fusion.7), kind=kCustom, calls=%fused_computation.6.clone.clone.clone.clone.1 | custom fusion | bytes 25165920 | tf_op jit(solution)/shard_map/while/body/eval_jaxpr/jit(_take)/gather | solution.py:77
  337.5 25.6 %fusion.85 = f32[24,128,128]{2,1,0:T(8,128)S(1)} fusion(f32[24,1024,128]{2,1,0:T(8,128)} %gather_fusion.1, f32[24,1024,128]{2,1,0:T(8,128)} %gather_fusion.2, pred[24]{0:T(512)(128)(4,1)S(1)} %get-tuple-element.350, pred[24]{0:T(512)(128)(4,1)S(1)} %get-tuple-element.351), kind=kOutput, calls=%fused_computation.12.clone.1 | convolution fusion | flops 4838129664 | bytes 26738736 | tf_op jit(solution)/shard_map/while/body/eval_jaxpr/mti,mtj->tij/dot_general | solution.py:80
  365.6 9.9 %gather_fusion = f32[24,1024,128]{2,1,0:T(8,128)} fusion(f32[1024,12,128]{2,0,1:T(8,128)} %get-tuple-element.396, s32[1024]{0:T(1024)S(1)} %pad_clamp_fusion.6), kind=kCustom, calls=%fused_computation.5.clone.clone.1 | custom fusion | bytes 25165920 | tf_op jit(solution)/shard_map/while/body/eval_jaxpr/jit(_take)/gather | solution.py:79
  375.5 17.0 %fusion.88 = f32[1024,24,128]{0,2,1:T(8,128)} fusion(f32[24,1024,128]{2,1,0:T(8,128)} %gather_fusion, pred[24]{0:T(512)(128)(4,1)S(1)} %get-tuple-element.350, f32[24,128,128]{2,1,0:T(8,128)S(1)} %fusion.85, f32[24]{0:T(128)S(1)} %fusion.86, f32[24,128]{1,0:T(8,128)S(1)} %get-tuple-element.352, f32[24,128]{1,0:T(8,128)S(1)} %get-tuple-element.356, ...), kind=kOutput, calls=%fused_computation.23.clone.1 | convolution fusion | flops 4840095744 | bytes 26787960 | tf_op jit(solution)/shard_map/while/body/eval_jaxpr/mtj,tij->mti/dot_general | solution.py:91
  392.6 12.6 %copy.44 = f32[1024,24,128]{2,1,0:T(8,128)} copy(f32[1024,24,128]{0,2,1:T(8,128)} %fusion.88) | data formatting | bytes 25165824 | tf_op jit(solution)/shard_map/while/body/eval_jaxpr/mtj,tij->mti/transpose | solution.py:91
  405.2 8.8 %bitcast_add_fusion.3 = f32[1024,8,128]{2,1,0:T(8,128)} fusion(f32[1024,8,128]{2,1,0:T(8,128)} %get-tuple-element.374, f32[1024,24,128]{2,1,0:T(8,128)} %copy.44, pred[]{:T(512)S(6)} %compare.10, s32[24]{0:T(128)S(1)} %get-tuple-element.348), kind=kOutput, calls=%fused_computation.24.clone.1 | convolution fusion | flops 304087232 | bytes 20971616 | tf_op jit(solution)/shard_map/while/body/eval_jaxpr/mti,tp->mpi/dot_general | solution.py:93
  414.0 9.9 %gather_fusion.1 = f32[24,1024,128]{2,1,0:T(8,128)} fusion(f32[1024,12,128]{2,0,1:T(8,128)} %get-tuple-element.394, s32[1024]{0:T(1024)S(1)} %pad_clamp_fusion.6), kind=kCustom, calls=%fused_computation.2.clone.clone.1 | custom fusion | bytes 25165920 | tf_op jit(solution)/shard_map/while/body/eval_jaxpr/jit(_take)/gather | solution.py:78
  423.9 9.3 %gather_fusion.2 = f32[24,1024,128]{2,1,0:T(8,128)} fusion(f32[1024,8,128]{2,0,1:T(8,128)} %get-tuple-element.393, s32[1024]{0:T(1024)S(1)} %pad_clamp_fusion.7), kind=kCustom, calls=%fused_computation.6.clone.clone.clone.clone.1 | custom fusion | bytes 25165920 | tf_op jit(solution)/shard_map/while/body/eval_jaxpr/jit(_take)/gather | solution.py:77
  433.2 25.6 %fusion.85 = f32[24,128,128]{2,1,0:T(8,128)S(1)} fusion(f32[24,1024,128]{2,1,0:T(8,128)} %gather_fusion.1, f32[24,1024,128]{2,1,0:T(8,128)} %gather_fusion.2, pred[24]{0:T(512)(128)(4,1)S(1)} %get-tuple-element.350, pred[24]{0:T(512)(128)(4,1)S(1)} %get-tuple-element.351), kind=kOutput, calls=%fused_computation.12.clone.1 | convolution fusion | flops 4838129664 | bytes 26738736 | tf_op jit(solution)/shard_map/while/body/eval_jaxpr/mti,mtj->tij/dot_general | solution.py:80
  461.3 9.9 %gather_fusion = f32[24,1024,128]{2,1,0:T(8,128)} fusion(f32[1024,12,128]{2,0,1:T(8,128)} %get-tuple-element.396, s32[1024]{0:T(1024)S(1)} %pad_clamp_fusion.6), kind=kCustom, calls=%fused_computation.5.clone.clone.1 | custom fusion | bytes 25165920 | tf_op jit(solution)/shard_map/while/body/eval_jaxpr/jit(_take)/gather | solution.py:79
  471.2 17.0 %fusion.88 = f32[1024,24,128]{0,2,1:T(8,128)} fusion(f32[24,1024,128]{2,1,0:T(8,128)} %gather_fusion, pred[24]{0:T(512)(128)(4,1)S(1)} %get-tuple-element.350, f32[24,128,128]{2,1,0:T(8,128)S(1)} %fusion.85, f32[24]{0:T(128)S(1)} %fusion.86, f32[24,128]{1,0:T(8,128)S(1)} %get-tuple-element.352, f32[24,128]{1,0:T(8,128)S(1)} %get-tuple-element.356, ...), kind=kOutput, calls=%fused_computation.23.clone.1 | convolution fusion | flops 4840095744 | bytes 26787960 | tf_op jit(solution)/shard_map/while/body/eval_jaxpr/mtj,tij->mti/dot_general | solution.py:91
  488.3 12.6 %copy.44 = f32[1024,24,128]{2,1,0:T(8,128)} copy(f32[1024,24,128]{0,2,1:T(8,128)} %fusion.88) | data formatting | bytes 25165824 | tf_op jit(solution)/shard_map/while/body/eval_jaxpr/mtj,tij->mti/transpose | solution.py:91
  500.9 9.4 %bitcast_add_fusion.3 = f32[1024,8,128]{2,1,0:T(8,128)} fusion(f32[1024,8,128]{2,1,0:T(8,128)} %get-tuple-element.374, f32[1024,24,128]{2,1,0:T(8,128)} %copy.44, pred[]{:T(512)S(6)} %compare.10, s32[24]{0:T(128)S(1)} %get-tuple-element.348), kind=kOutput, calls=%fused_computation.24.clone.1 | convolution fusion | flops 304087232 | bytes 20971616 | tf_op jit(solution)/shard_map/while/body/eval_jaxpr/mti,tp->mpi/dot_general | solution.py:93
  510.3 7.0 %bitcast_add_fusion.1 = f32[1024,1024]{1,0:T(8,128)} fusion(f32[128,8,8,128]{3,2,1,0:T(8,128)} %bitcast.73, f32[128,8,1024]{2,0,1:T(8,128)} %all-to-all-done), kind=kLoop, calls=%fused_computation.96 | loop fusion | flops 1048576 | bytes 12582912 | tf_op jit(solution)/shard_map/add | solution.py:105
  (50 shorter events, 12.5 us)
Async XLA Ops:
  6.5 120.0 %all-gather.3.cloned.1.call-start = ((), (), s32[]{:S(2)}) async-start(), calls=%async_computation.1 | async-start | bytes 2359296 | tf_op jit(solution)/shard_map/all_gather | solution.py:39
  8.4 173.6 %all-gather.5.cloned.1.call-start = ((), (), s32[]{:S(2)}) async-start(), calls=%async_computation.2 | async-start | bytes 2359296 | tf_op jit(solution)/shard_map/all_gather | solution.py:40
  15.0 7.4 %copy-start = (f32[2,512]{1,0:T(2,128)S(1)}, f32[2,512]{1,0:T(2,128)}, u32[]{:S(2)}) copy-start(f32[2,512]{1,0:T(2,128)} %param.17) | copy-start | bytes 12292
  15.1 179.2 %all-to-all-start = ((f32[128,8,1024]{2,0,1:T(8,128)}), f32[128,8,1024]{2,0,1:T(8,128)}, u32[]{:S(2)}, u32[]{:S(2)}) async-start(f32[128,8,1024]{2,0,1:T(8,128)} %bitcast.78), calls=%async_computation | async-start | bytes 8388608 | tf_op jit(solution)/shard_map/all_to_all | solution.py:48
  186.0 7.5 %copy-start.1 = (s32[1,1,2,48]{3,2,1,0:T(2,128)S(1)}, s32[1,1,2,48]{3,2,1,0:T(2,128)}, u32[]{:S(2)}) copy-start(s32[1,1,2,48]{3,2,1,0:T(2,128)} %param.18) | copy-start | bytes 1156
  191.7 91.7 %collective-permute-start = (f32[2050,512]{1,0:T(8,128)}, f32[2050,512]{1,0:T(8,128)}, u32[]{:S(2)}, u32[]{:S(2)}) collective-permute-start(f32[2050,512]{1,0:T(8,128)} %copy.29), channel_id=1, source_target_pairs={{0,8},{8,16},{16,24},{24,0},{1,9},{9,17},{17,25},{25,1},{2,10},{10... | collective-permute-start | bytes 12595208 | tf_op jit(solution)/shard_map/ppermute | solution.py:16
  191.7 97.2 %collective-permute-start.1 = (f32[2050,512]{1,0:T(8,128)}, f32[2050,512]{1,0:T(8,128)}, u32[]{:S(2)}, u32[]{:S(2)}) collective-permute-start(f32[2050,512]{1,0:T(8,128)} %copy.29), channel_id=1, source_target_pairs={{8,0},{16,8},{24,16},{0,24},{9,1},{17,9},{25,17},{1,25},{10,2},{18... | collective-permute-start | bytes 12595208 | tf_op jit(solution)/shard_map/ppermute | solution.py:19
Sparse Core Ops, SparseCore 0:
  9.4 117.1 all-gather.2
  128.6 53.3 all-gather.4
where the time goes:
time: 525 us; the launch traced here: 524 us
  waiting for transfers between devices  239 us (46%)
  local copies, waits for them, and re-layouts  133 us (25%)
  matrix products  104 us (20%)
  other arithmetic  25.5 us (5%)
  between operations  14.1 us (3%)
  starting transfers between devices  9.2 us (2%)
    all_gather x1, waiting for transfers between devices, shards(): lax.all_gather(obs_ensemble, 'mem', axis=0, tiled=True)  104 us
    ppermute x1, waiting for transfers between devices, padded(): lax.ppermute(lax.slice_in_dim(block, block.shape[dim] - width, None, axis...  83.1 us
    all_gather x1, waiting for transfers between devices, shards(): lax.all_gather(innovations, 'mem', axis=0, tiled=True)  51.9 us
    dot_general x2, matrix products, tile_batch(): jnp.einsum('mti,mtj->tij', x_blocks, y_blocks, precision=highest)  51.3 us
    dot_general x2, matrix products, tile_batch(): increment = jnp.einsum('mtj,tij->mti', w_blocks, weights, precision=highest)  34.1 us
    transpose x2, local copies, waits for them, and re-layouts, tile_batch(): increment = jnp.einsum('mtj,tij->mti', w_blocks, weights, precision=highest)  25.2 us
    unnamed x11, local copies, waits for them, and re-layouts  23 us
    gather x2, local copies, waits for them, and re-layouts, tile_batch(): y_blocks = jnp.take(anom_grid, obs_ids, axis=1)  19.8 us
  transfers between devices with their start and end apart: 5, of which 3 were waited for; matrix products, arithmetic and copies ran while one was open for 6% of the time, Pallas kernels for 0%

commit v1 on v0

v1 whole, which is shorter than its diff:
```python
import functools

import jax
import jax.numpy as jnp
from jax import lax
from jax.experimental import pallas as pl
from jax.experimental.pallas import tpu as pltpu
from jax.sharding import PartitionSpec as P

taper_reach = 0.6
tile_side = 128
chunks = 2
pieces = 2
f32, bf16 = jnp.float32, jnp.bfloat16
anywhere = pl.BlockSpec(memory_space=pl.ANY)
in_vmem = pl.BlockSpec(memory_space=pltpu.VMEM)
vmem_limit = 56 * 1024 * 1024


def dot(a, b):
    return lax.dot_general(a, b, (((1,), (0,)), ((), ())), preferred_element_type=f32)


def split(x):
    high = x.astype(bf16)
    return high, (x - high.astype(f32)).astype(bf16)


def swap(x, axis, distance):
    size = lax.axis_size(axis)
    return lax.ppermute(x, axis, [(i, i ^ distance) for i in range(size)])


def prep_obs_kernel(order, x_ref, high_ref, low_ref):
    blocks, rows, _ = x_ref.shape
    total = jnp.sum(x_ref[0], axis=0, keepdims=True)
    for i in range(1, blocks):
        total += jnp.sum(x_ref[i], axis=0, keepdims=True)
    mean = total / (blocks * rows)
    for i in range(blocks):
        high, low = split((x_ref[i] - mean).T)
        at = pl.ds(order[i] * rows, rows)
        high_ref[:, at] = high
        low_ref[:, at] = low


def prep_obs(x, order):
    blocks, rows, width = x.shape
    return pl.pallas_call(
        functools.partial(prep_obs_kernel, order),
        out_shape=[jax.ShapeDtypeStruct((width, blocks * rows), bf16)] * 2,
        in_specs=[in_vmem],
        out_specs=[in_vmem] * 2,
        compiler_params=pltpu.CompilerParams(vmem_limit_bytes=vmem_limit),
        cost_estimate=pl.CostEstimate(flops=8 * x.size, bytes_accessed=8 * x.size, transcendentals=0),
    )(x)


def prep_innov_kernel(order, x_ref, high_ref, low_ref):
    blocks, rows, _ = x_ref.shape
    for i in range(blocks):
        high, low = split(x_ref[i])
        at = pl.ds(order[i] * rows, rows)
        high_ref[at, :] = high
        low_ref[at, :] = low


def prep_innov(x, order):
    blocks, rows, width = x.shape
    return pl.pallas_call(
        functools.partial(prep_innov_kernel, order),
        out_shape=[jax.ShapeDtypeStruct((blocks * rows, width), bf16)] * 2,
        in_specs=[in_vmem],
        out_specs=[in_vmem] * 2,
        compiler_params=pltpu.CompilerParams(vmem_limit_bytes=vmem_limit),
        cost_estimate=pl.CostEstimate(flops=4 * x.size, bytes_accessed=8 * x.size, transcendentals=0),
    )(x)


def update_kernel(npoint, nobs, first, start, *refs):
    me_ref = refs[0]
    refs = refs[1:]
    points, refs = refs[:npoint], refs[npoint:]
    obs_high, refs = refs[:nobs], refs[nobs:]
    obs_low, refs = refs[:nobs], refs[nobs:]
    inn_high, refs = refs[:nobs], refs[nobs:]
    inn_low, refs = refs[:nobs], refs[nobs:]
    taper = refs[0]
    refs = refs[1 if first else 2 :]
    out, total, x_high, x_low, yh, yl, wh, wl, tap, sem_x, sem_y, sem_out = refs
    rows = points[0].shape[0]
    width = points[0].shape[1]
    group = yh.shape[1]
    x_copies = [
        pltpu.make_async_copy(points[i], total.at[pl.ds(i * rows, rows)], sem_x.at[i])
        for i in range(npoint)
    ]
    obs_copies = []
    for i in range(nobs):
        obs_copies.append(
            [
                pltpu.make_async_copy(obs_high[i], yh.at[i], sem_y.at[i, 0]),
                pltpu.make_async_copy(obs_low[i], yl.at[i], sem_y.at[i, 1]),
                pltpu.make_async_copy(
                    taper.at[pl.ds(i * group, group), pl.ds(start, width)], tap.at[i], sem_y.at[i, 2]
                ),
                pltpu.make_async_copy(inn_high[i], wh.at[i], sem_y.at[i, 3]),
                pltpu.make_async_copy(inn_low[i], wl.at[i], sem_y.at[i, 4]),
            ]
        )
    for copy in x_copies:
        copy.start()
    for group_copies in obs_copies:
        for copy in group_copies:
            copy.start()
    for i, copy in enumerate(x_copies):
        copy.wait()
        at = pl.ds(i * rows, rows)
        x_high[at, :], x_low[at, :] = split(total[at, :])

    for i in range(nobs):
        for copy in obs_copies[i][:3]:
            copy.wait()
        cov = dot(yh[i], x_high[...]) + dot(yl[i], x_high[...]) + dot(yh[i], x_low[...])
        weight_high, weight_low = split(cov * tap[i])
        for copy in obs_copies[i][3:]:
            copy.wait()
        total[...] += (
            dot(wh[i], weight_high) + dot(wl[i], weight_high) + dot(wh[i], weight_low)
        )
    me = me_ref[0]
    local = sem_out.shape[0]
    members = total.shape[0]
    ml = members // local
    out_copies = [
        pltpu.make_async_copy(
            total.at[pl.ds(r * ml, ml)],
            out.at[pl.ds(pl.multiple_of((me ^ r) * ml, 8), ml), pl.ds(start, width)],
            sem_out.at[r],
        )
        for r in range(local)
    ]
    for copy in out_copies:
        copy.start()
    for copy in out_copies:
        copy.wait()


def update(me, blocks, obs, innov, taper, out, start, groups, per_device):
    npoint, nobs = len(blocks), len(obs)
    rows, width = blocks[0].shape
    members = rows * npoint
    group = obs[0][0].shape[0]
    first = out is None
    operands = [me, *blocks]
    operands += [o[0] for o in obs] + [o[1] for o in obs]
    operands += [w[0] for w in innov] + [w[1] for w in innov]
    operands += [taper] + ([] if first else [out])
    flops = 3 * 4 * members * width * group * nobs
    return pl.pallas_call(
        functools.partial(update_kernel, npoint, nobs, first, start),
        out_shape=jax.ShapeDtypeStruct((members, per_device), f32),
        in_specs=[pl.BlockSpec(memory_space=pltpu.SMEM)] + [anywhere] * (len(operands) - 1),
        out_specs=anywhere,
        scratch_shapes=[
            pltpu.VMEM((members, width), f32),
            pltpu.VMEM((members, width), bf16),
            pltpu.VMEM((members, width), bf16),
            pltpu.VMEM((nobs, group, members), bf16),
            pltpu.VMEM((nobs, group, members), bf16),
            pltpu.VMEM((nobs, members, group), bf16),
            pltpu.VMEM((nobs, members, group), bf16),
            pltpu.VMEM((nobs, group, width), f32),
            pltpu.SemaphoreType.DMA((npoint,)),
            pltpu.SemaphoreType.DMA((nobs, 5)),
            pltpu.SemaphoreType.DMA((groups,)),
        ],
        input_output_aliases={} if first else {len(operands) - 1: 0},
        compiler_params=pltpu.CompilerParams(vmem_limit_bytes=vmem_limit),
        cost_estimate=pl.CostEstimate(
            flops=flops, bytes_accessed=8 * group * nobs * members, transcendentals=0
        ),
    )(*operands)


def shards(state, obs_ensemble, innovations, obs_coords, tile_list, tile_counts):
    ml = state.shape[0]
    groups = lax.axis_size("mem")
    domains = lax.axis_size("dom")
    per_domain = state.shape[1]
    per_device = per_domain // groups
    obs_local = obs_ensemble.shape[1]
    members = ml * groups
    me = lax.axis_index("mem")
    domain = lax.axis_index("dom")
    odd = domain % 2
    side = me % 2
    far = me // 2
    nfar = groups // 2

    bits = []
    b = groups // 2
    while b >= 1:
        bits.append(b)
        b //= 2
    order = [0]
    for b in bits:
        order = order + [r ^ b for r in order]

    def gathered(x):
        x = x[None]
        for b in bits:
            x = jnp.concatenate([x, swap(x, "mem", b)], axis=0)
        return x

    across = [((i + 1) % domains, (i + 2) % domains) for i in range(0, domains, 2)]
    across = across + [(t, s) for s, t in across]
    chip = [(i, i ^ 1) for i in range(domains)]

    width_piece = obs_local // pieces

    def collected(array, prep):
        out = []
        for p in range(pieces):
            own = gathered(array[:, p * width_piece : (p + 1) * width_piece])
            beside = lax.ppermute(own, "dom", chip)
            beyond = lax.ppermute(own, "dom", across)
            out.append([prep(x, order) for x in (own, beside, beyond)])
        return [out[p][s] for s in range(3) for p in range(pieces)]

    obs = collected(obs_ensemble, prep_obs)
    innov = collected(innovations, prep_innov)

    width = per_device // chunks
    grid = state.reshape(ml, nfar, 2, per_device)
    point_blocks = []
    for c in range(chunks):
        part = lax.slice_in_dim(grid, c * width, (c + 1) * width, axis=3)
        keep = lax.dynamic_index_in_dim(part, side, 2, False).transpose(1, 0, 2)
        give = lax.dynamic_index_in_dim(part, 1 - side, 2, False).transpose(1, 0, 2)
        got = swap(give, "mem", 1)
        blocks = []
        for j in range(nfar):
            pair = jnp.concatenate(
                [
                    lax.dynamic_index_in_dim(keep, far ^ j, 0, False),
                    lax.dynamic_index_in_dim(got, far ^ j, 0, False),
                ],
                axis=0,
            )
            blocks.append(pair if j == 0 else swap(pair, "mem", 2 * j))
        point_blocks.append(blocks)

    coord_own = obs_coords
    coord_beside = lax.ppermute(obs_coords, "dom", chip)
    coord_beyond = lax.ppermute(obs_coords, "dom", across)
    coords = jnp.concatenate([coord_own, coord_beside, coord_beyond], axis=1)
    nblocks = per_device // tile_side
    window = obs_local // tile_side
    point_ids, obs_ids = tile_list[0, 0, 0], tile_list[0, 0, 1]
    slots = point_ids.shape[0]
    live = (jnp.arange(slots, dtype=jnp.int32) < tile_counts[0, 0]).astype(f32)
    position = jnp.stack([jnp.int32(1), 2 - 2 * odd, 2 * odd]).astype(jnp.int32)
    block_ids = (position[:, None] * window + jnp.arange(window, dtype=jnp.int32)[None]).reshape(-1)
    by_obs = (obs_ids[None, :] == block_ids[:, None]).astype(f32) * live[None]
    by_point = (point_ids[:, None] == jnp.arange(nblocks, dtype=jnp.int32)[None]).astype(f32)
    mask = jnp.sum(by_obs[:, :, None] * by_point[None], axis=1)
    mask = jnp.repeat(mask, tile_side, axis=1) / (members - 1)
    within = me * per_device + jnp.arange(per_device, dtype=jnp.int32)
    point_x = domain.astype(f32) + ((within % 32).astype(f32) + 0.5) / 32.0
    point_y = ((within // 32).astype(f32) + 0.5) / float(per_domain // 32)
    gap_x = jnp.abs(point_x[None, :] - coords[0][:, None])
    gap_x = jnp.minimum(gap_x, float(domains) - gap_x)
    gap_y = point_y[None, :] - coords[1][:, None]
    taper = jnp.exp(-(gap_x * gap_x + gap_y * gap_y) / (2.0 * taper_reach * taper_reach))
    taper = (taper.reshape(-1, tile_side, per_device) * mask[:, None, :]).reshape(-1, per_device)

    out = None
    for c in range(chunks):
        out = update(
            me.astype(jnp.int32).reshape(1),
            point_blocks[c],
            obs,
            innov,
            taper,
            out,
            c * width,
            groups,
            per_device,
        )
    return out


def solution(mesh):
    return jax.shard_map(
        shards,
        mesh=mesh,
        in_specs=(
            P("mem", "dom"),
            P("mem", "dom"),
            P("mem", "dom"),
            P(None, "dom"),
            P("dom", "mem", None, None),
            P("dom", "mem"),
        ),
        out_specs=P(None, ("dom", "mem")),
        check_vma=False,
    )
```

time: 525 us -> 299 us (0.57)
  waiting for transfers between devices: 239 us -> 127 us
  matrix products: 104 us -> 0 us
  local copies, waits for them, and re-layouts: 133 us -> 38.9 us
  Pallas kernels: 0 us -> 68.5 us
  starting transfers between devices: 9.2 us -> 31.5 us
  between operations: 14.1 us -> 1.28 us
    all_gather x2 -> x0, waiting for transfers between devices: 156 us -> none  [the longest x1 104 us: shards(): lax.all_gather(obs_ensemble, 'mem', axis=0, tiled=True)]
    dot_general x6 -> x0, matrix products: 104 us -> none  [the longest x2 51.3 us: tile_batch(): jnp.einsum('mti,mtj->tij', x_blocks, y_blocks, precision=highest)]
    pallas_call x0 -> x14, Pallas kernels: none -> 68.5 us  [the longest x2 38.6 us: update(): pl.pallas_call(functools.partial(update_kernel, npoint, nobs, first, star...]
    gather x14 -> x0, local copies, waits for them, and re-layouts: 62.7 us -> none  [the longest x2 19.8 us: tile_batch(): y_blocks = jnp.take(anom_grid, obs_ids, axis=1)]
    ppermute x2 -> x30, waiting for transfers between devices: 83.1 us -> 127 us  [the longest x20 113 us: swap(): return lax.ppermute(x, axis, [(i, i ^ distance) for i in range(size)])]
    ppermute x2 -> x30, starting transfers between devices: 1.75 us -> 31.5 us  [the longest x20 27.8 us: swap(): return lax.ppermute(x, axis, [(i, i ^ distance) for i in range(size)])]
    transpose x2 -> x0, local copies, waits for them, and re-layouts: 25.2 us -> none  [tile_batch(): increment = jnp.einsum('mtj,tij->mti', w_blocks, weights, precision=highest)]
    concatenate x2 -> x20, other arithmetic: 12.6 us -> 23.9 us  [the longest x12 14.9 us: gathered(): x = jnp.concatenate([x, swap(x, 'mem', b)], axis=0)]
  transfers between devices with their start and end apart: 5 -> 30, of which waited for: 3 -> 11; matrix products, arithmetic and copies ran while one was open for 6% -> 22% of each run, Pallas kernels for 0% -> 16%
where the time goes in v1:
time: 299 us; the launch traced here: 298 us
  waiting for transfers between devices  127 us (42%)
  Pallas kernels  68.5 us (23%)
  local copies, waits for them, and re-layouts  38.9 us (13%)
  starting transfers between devices  31.5 us (11%)
  other arithmetic  30.1 us (10%)
    ppermute x20, waiting for transfers between devices, swap(): return lax.ppermute(x, axis, [(i, i ^ distance) for i in range(size)])  113 us
    pallas_call x2, Pallas kernels, update(): pl.pallas_call(functools.partial(update_kernel, npoint, nobs, first, star...  38.6 us
    ppermute x20, starting transfers between devices, swap(): return lax.ppermute(x, axis, [(i, i ^ distance) for i in range(size)])  27.8 us
    pallas_call x6, Pallas kernels, prep_obs(): pl.pallas_call(functools.partial(prep_obs_kernel, order), out_shape=[jax....  15.8 us
    concatenate x12, other arithmetic, gathered(): x = jnp.concatenate([x, swap(x, 'mem', b)], axis=0)  14.9 us
    ppermute x4, waiting for transfers between devices, collected(): beyond = lax.ppermute(own, 'dom', across)  14.5 us
    pallas_call x6, Pallas kernels, prep_innov(): pl.pallas_call(functools.partial(prep_innov_kernel, order), out_shape=[ja...  14.1 us
    unnamed x64, local copies, waits for them, and re-layouts  11.8 us
  transfers between devices with their start and end apart: 30, of which 11 were waited for; matrix products, arithmetic and copies ran while one was open for 22% of the time, Pallas kernels for 16%

profile of v1, /device:TPU:0, one launch (start us, length us, event | category | flops | bytes accessed | tf_op | source)
XLA Modules:
  0.0 297.7 jit_solution(3068602121515848044)
XLA Ops:
  2.1 3.6 %collective-permute-start.7 = (f32[1,128,256]{2,1,0:T(8,128)S(1)}, f32[1,128,256]{2,1,0:T(8,128)}, u32[]{:S(2)}, u32[]{:S(2)}) collective-permute-start(f32[1,128,256]{2,1,0:T(8,128)S(1)} %get-tuple-element.75), channel_id=1, source_target_pairs={{0,4},{1,5},{2,6},{3,7},{4,0},{5,1},{6,2},{7,3},{8,12},{9,13},{10,... | collective-permute-start | bytes 393224 | tf_op jit(solution)/shard_map/ppermute | solution.py:31
  6.7 3.0 collective-permute-start.17
  11.3 6.6 %reshape.223 = f32[128,4,2,1024]{3,2,1,0:T(2,128)} reshape(f32[128,8192]{1,0:T(8,128)} %param.6) | data formatting | bytes 8388608 | tf_op jit(solution)/shard_map/reshape | solution.py:235
  17.8 5.5 %fusion.19 = (f32[128,4,2,512]{3,2,1,0:T(2,128)S(1)}, f32[128,4,2,512]{3,2,1,0:T(2,128)}) fusion(f32[128,4,2,1024]{3,2,1,0:T(2,128)} %reshape.223), kind=kLoop, calls=%fused_computation.93 | loop fusion | bytes 8388608 | tf_op jit(solution)/shard_map/slice | solution.py:238
  24.4 3.6 %constant_dynamic-slice_fusion.8 = f32[128,4,1,512]{3,2,1,0:T(1,128)} fusion(f32[128,4,2,512]{3,2,1,0:T(2,128)} %get-tuple-element.56, s32[]{:T(128)S(6)} %select_n.84), kind=kLoop, calls=%fused_computation.69 | loop fusion | bytes 2097156 | tf_op jit(solution)/shard_map/jit(dynamic_index_in_dim)/dynamic_slice | solution.py:240
  29.9 2.5 copy.36
  41.9 2.2 collective-permute-done.5
  46.9 2.7 collective-permute-done.15
  53.3 6.2 %collective-permute-done.8 = f32[2,128,256]{2,1,0:T(8,128)S(1)} collective-permute-done((f32[2,128,256]{2,1,0:T(8,128)S(1)}, f32[2,128,256]{2,1,0:T(8,128)S(1)}, u32[]{:S(2)}, u32[]{:S(2)}) %collective-permute-start.8) | collective-permute-done | bytes 262176 | tf_op jit(solution)/shard_map/ppermute | solution.py:31
  70.5 3.5 %constant_dynamic-slice_fusion = (f32[128,1,1,512]{3,2,1,0:T(1,128)S(1)}, f32[128,1,1,512]{3,2,1,0:T(1,128)S(1)}, f32[128,1,1,512]{3,2,1,0:T(1,128)S(1)}, f32[12...) fusion(f32[128,4,2,512]{3,2,1,0:T(2,128)S(1)} %get-tuple-elemen, ...), kind=kLoop, calls=%fused_computation.61 | loop fusion | bytes 4194324 | tf_op jit(solution)/shard_map/dynamic-slice.15
  75.2 50.5 %collective-permute-done.19 = f32[4,128,256]{2,1,0:T(8,128)} collective-permute-done((f32[4,128,256]{2,1,0:T(8,128)}, f32[4,128,256]{2,1,0:T(8,128)}, u32[]{:S(2)}, u32[]{:S(2)}) %collective-permute-start.19) | collective-permute-done | bytes 524320 | tf_op jit(solution)/shard_map/ppermute | solution.py:31
  125.7 9.4 %collective-permute-done.9 = f32[4,128,256]{2,1,0:T(8,128)} collective-permute-done((f32[4,128,256]{2,1,0:T(8,128)}, f32[4,128,256]{2,1,0:T(8,128)}, u32[]{:S(2)}, u32[]{:S(2)}) %collective-permute-start.9) | collective-permute-done | bytes 524320 | tf_op jit(solution)/shard_map/ppermute | solution.py:31
  142.5 4.6 %fusion.5.refs_29_ = f32[1536,1024]{1,0:T(8,128)} fusion(f32[12,1024]{1,0:T(8,128)S(1)} %bitcast.80, f32[1536]{0:T(1024)S(1)} %get-tuple-element.54, f32[1024]{0:T(1024)S(1)} %get-tuple-element.84, f32[1536]{0:T(1024)S(1)} %get-tuple-element.53, f32[1024]{0:T(1024)S(1)} %get-tuple-element.83), kind=kLoop, calls=%fused_computation.6 | loop fusion | flops 17301504 | bytes 6361088 | tf_op jit(solution)/shard_map/mul | solution.py:276
  147.1 2.3 shard_map.70
  149.4 2.4 shard_map.71
  151.8 2.6 shard_map.64
  156.5 2.6 shard_map.65
  169.3 13.9 %collective-permute-done.23.x_ref = f32[8,128,256]{2,1,0:T(8,128)} collective-permute-done((f32[8,128,256]{2,1,0:T(8,128)S(1)}, f32[8,128,256]{2,1,0:T(8,128)}, u32[]{:S(2)}, u32[]{:S(2)}) %collective-permute-start.23) | collective-permute-done | bytes 1048608 | tf_op jit(solution)/shard_map/ppermute | solution.py:227
  183.2 2.2 collective-permute-start.28
  190.6 2.4 shard_map.74
  192.9 2.3 shard_map.72
  195.3 2.3 shard_map.75
  197.6 2.3 shard_map.73
  199.9 2.7 shard_map.68
  202.6 2.6 shard_map.66
  205.3 3.5 %collective-permute-start.3 = (f32[256,512]{1,0:T(8,128)S(1)}, f32[256,512]{1,0:T(8,128)S(1)}, u32[]{:S(2)}, u32[]{:S(2)}) collective-permute-start(f32[256,512]{1,0:T(8,128)S(1)} %pad_maximum_fusion.7), channel_id=1, source_target_pairs={{0,6},{1,7},{2,4},{3,5},{4,2},{5,3},{6,0},{7,1},{8,14},{9,15},{10,... | collective-permute-start | bytes 1572872 | tf_op jit(solution)/shard_map/ppermute | solution.py:31
  208.8 2.6 shard_map.69
  212.3 2.6 shard_map.67
  215.6 28.6 %collective-permute-done.28.refs_3_ = f32[256,512]{1,0:T(8,128)} collective-permute-done((f32[256,512]{1,0:T(8,128)}, f32[256,512]{1,0:T(8,128)}, u32[]{:S(2)}, u32[]{:S(2)}) %collective-permute-start.28) | collective-permute-done | bytes 524320 | tf_op jit(solution)/shard_map/ppermute | solution.py:31
  244.9 19.2 %shard_map.76.refs_30_ = f32[1024,1024]{1,0:T(8,128)} custom-call(s32[1]{0:T(128)} %bitcast.refs_0_, f32[256,512]{1,0:T(8,128)} %pad_maximum_fusion.12.refs_1_, f32[256,512]{1,0:T(8,128)} %collective-permute-done.27.refs_2_, f32[256,512]{1,0:T(8,128)} %collective-permute-done.28.refs_3_, f32[256,512]{1,0:T(8,128)} %copy-done.21, ...), custom_call_target="tpu_custom_call" | custom-call | flops 9663676416 | bytes 12582912 | tf_op jit(solution)/shard_map/pallas_call | solution.py:160
  264.2 12.3 %collective-permute-done.2.refs_3_ = f32[256,512]{1,0:T(8,128)S(1)} collective-permute-done((f32[256,512]{1,0:T(8,128)S(1)}, f32[256,512]{1,0:T(8,128)S(1)}, u32[]{:S(2)}, u32[]{:S(2)}) %collective-permute-start.2) | collective-permute-done | bytes 524320 | tf_op jit(solution)/shard_map/ppermute | solution.py:31
  278.1 19.4 %shard_map.77 = f32[1024,1024]{1,0:T(8,128)} custom-call(s32[1]{0:T(128)} %bitcast.refs_0_, f32[256,512]{1,0:T(8,128)} %pad_maximum_fusion.4.refs_1_, f32[256,512]{1,0:T(8,128)} %copy-done.24, f32[256,512]{1,0:T(8,128)} %copy-done.23, f32[256,512]{1,0:T(8,128)} %copy-done.22, ...), custom_call_target="tpu_custom_call", output_to_operand_aliasing={{}: (30, {})} | custom-call | flops 9663676416 | bytes 12582912 | tf_op jit(solution)/shard_map/pallas_call | solution.py:160
  (148 shorter events, 63.6 us)
Async XLA Ops:
  0.0 66.3 %collective-permute-start.24 = (f32[2,512]{1,0:T(2,128)}, f32[2,512]{1,0:T(2,128)S(1)}, u32[]{:S(2)}, u32[]{:S(2)}) collective-permute-start(f32[2,512]{1,0:T(2,128)} %param.9), channel_id=1, source_target_pairs={{0,8},{8,0},{16,24},{24,16},{1,9},{9,1},{17,25},{25,17},{2,10},{10... | collective-permute-start | bytes 12296 | tf_op jit(solution)/shard_map/ppermute | solution.py:255
  2.1 38.6 %collective-permute-start.7 = (f32[1,128,256]{2,1,0:T(8,128)S(1)}, f32[1,128,256]{2,1,0:T(8,128)}, u32[]{:S(2)}, u32[]{:S(2)}) collective-permute-start(f32[1,128,256]{2,1,0:T(8,128)S(1)} %get-tuple-element.75), channel_id=1, source_target_pairs={{0,4},{1,5},{2,6},{3,7},{4,0},{5,1},{6,2},{7,3},{8,12},{9,13},{10,... | collective-permute-start | bytes 393224 | tf_op jit(solution)/shard_map/ppermute | solution.py:31
  5.7 28.1 %collective-permute-start.4 = (f32[1,128,256]{2,1,0:T(8,128)}, f32[1,128,256]{2,1,0:T(8,128)}, u32[]{:S(2)}, u32[]{:S(2)}) collective-permute-start(f32[1,128,256]{2,1,0:T(8,128)} %get-tuple-element.76), channel_id=1, source_target_pairs={{0,4},{1,5},{2,6},{3,7},{4,0},{5,1},{6,2},{7,3},{8,12},{9,13},{10,... | collective-permute-start | bytes 393224 | tf_op jit(solution)/shard_map/ppermute | solution.py:31
  6.7 31.1 %collective-permute-start.17 = (f32[1,128,256]{2,1,0:T(8,128)S(1)}, f32[1,128,256]{2,1,0:T(8,128)}, u32[]{:S(2)}, u32[]{:S(2)}) collective-permute-start(f32[1,128,256]{2,1,0:T(8,128)S(1)} %get-tuple-element.73), channel_id=1, source_target_pairs={{0,4},{1,5},{2,6},{3,7},{4,0},{5,1},{6,2},{7,3},{8,12},{9,13},{10,... | collective-permute-start | bytes 393224 | tf_op jit(solution)/shard_map/ppermute | solution.py:31
  9.7 27.0 %collective-permute-start.14 = (f32[1,128,256]{2,1,0:T(8,128)S(1)}, f32[1,128,256]{2,1,0:T(8,128)}, u32[]{:S(2)}, u32[]{:S(2)}) collective-permute-start(f32[1,128,256]{2,1,0:T(8,128)S(1)} %get-tuple-element.74), channel_id=1, source_target_pairs={{0,4},{1,5},{2,6},{3,7},{4,0},{5,1},{6,2},{7,3},{8,12},{9,13},{10,... | collective-permute-start | bytes 393224 | tf_op jit(solution)/shard_map/ppermute | solution.py:31
  34.8 9.3 %collective-permute-start.5 = (f32[2,128,256]{2,1,0:T(8,128)S(1)}, f32[2,128,256]{2,1,0:T(8,128)S(1)}, u32[]{:S(2)}, u32[]{:S(2)}) collective-permute-start(f32[2,128,256]{2,1,0:T(8,128)S(1)} %pad_maximum_fusion.16), channel_id=1, source_target_pairs={{0,2},{1,3},{2,0},{3,1},{4,6},{5,7},{6,4},{7,5},{8,10},{9,11},{10,... | collective-permute-start | bytes 786440 | tf_op jit(solution)/shard_map/ppermute | solution.py:31
  37.6 12.1 %collective-permute-start.15 = (f32[2,128,256]{2,1,0:T(8,128)S(1)}, f32[2,128,256]{2,1,0:T(8,128)S(1)}, u32[]{:S(2)}, u32[]{:S(2)}) collective-permute-start(f32[2,128,256]{2,1,0:T(8,128)S(1)} %pad_maximum_fusion.18), channel_id=1, source_target_pairs={{0,2},{1,3},{2,0},{3,1},{4,6},{5,7},{6,4},{7,5},{8,10},{9,11},{10,... | collective-permute-start | bytes 786440 | tf_op jit(solution)/shard_map/ppermute | solution.py:31
  38.8 22.6 %collective-permute-start.18 = (f32[2,128,256]{2,1,0:T(8,128)S(1)}, f32[2,128,256]{2,1,0:T(8,128)S(1)}, u32[]{:S(2)}, u32[]{:S(2)}) collective-permute-start(f32[2,128,256]{2,1,0:T(8,128)S(1)} %pad_maximum_fusion.19), channel_id=1, source_target_pairs={{0,2},{1,3},{2,0},{3,1},{4,6},{5,7},{6,4},{7,5},{8,10},{9,11},{10,... | collective-permute-start | bytes 786440 | tf_op jit(solution)/shard_map/ppermute | solution.py:31
  41.6 18.0 %collective-permute-start.8 = (f32[2,128,256]{2,1,0:T(8,128)S(1)}, f32[2,128,256]{2,1,0:T(8,128)S(1)}, u32[]{:S(2)}, u32[]{:S(2)}) collective-permute-start(f32[2,128,256]{2,1,0:T(8,128)S(1)} %pad_maximum_fusion.17), channel_id=1, source_target_pairs={{0,2},{1,3},{2,0},{3,1},{4,6},{5,7},{6,4},{7,5},{8,10},{9,11},{10,... | collective-permute-start | bytes 786440 | tf_op jit(solution)/shard_map/ppermute | solution.py:31
  45.0 19.6 %collective-permute-start.6 = (f32[4,128,256]{2,1,0:T(8,128)S(1)}, f32[4,128,256]{2,1,0:T(8,128)S(1)}, u32[]{:S(2)}, u32[]{:S(2)}) collective-permute-start(f32[4,128,256]{2,1,0:T(8,128)S(1)} %pad_maximum_fusion.8), channel_id=1, source_target_pairs={{0,1},{1,0},{2,3},{3,2},{4,5},{5,4},{6,7},{7,6},{8,9},{9,8},{10,11... | collective-permute-start | bytes 1572872 | tf_op jit(solution)/shard_map/ppermute | solution.py:31
  50.7 18.7 %collective-permute-start.16 = (f32[4,128,256]{2,1,0:T(8,128)S(1)}, f32[4,128,256]{2,1,0:T(8,128)S(1)}, u32[]{:S(2)}, u32[]{:S(2)}) collective-permute-start(f32[4,128,256]{2,1,0:T(8,128)S(1)} %pad_maximum_fusion.10), channel_id=1, source_target_pairs={{0,1},{1,0},{2,3},{3,2},{4,5},{5,4},{6,7},{7,6},{8,9},{9,8},{10,11... | collective-permute-start | bytes 1572872 | tf_op jit(solution)/shard_map/ppermute | solution.py:31
  59.6 8.4 %collective-permute-start.25 = (f32[2,512]{1,0:T(2,128)S(1)}, f32[2,512]{1,0:T(2,128)S(1)}, u32[]{:S(2)}, u32[]{:S(2)}) collective-permute-start(f32[2,512]{1,0:T(2,128)S(1)} %copy-done.13), channel_id=1, source_target_pairs={{8,16},{24,0},{16,8},{0,24},{9,17},{25,1},{17,9},{1,25},{10,18},{2... | collective-permute-start | bytes 12296 | tf_op jit(solution)/shard_map/ppermute | solution.py:256
  61.4 74.9 %collective-permute-start.26 = (f32[4,128,512]{2,1,0:T(8,128)}, f32[4,128,512]{2,1,0:T(8,128)}, u32[]{:S(2)}, u32[]{:S(2)}) collective-permute-start(f32[4,128,512]{2,1,0:T(8,128)} %bitcast.61), channel_id=1, source_target_pairs={{0,1},{1,0},{2,3},{3,2},{4,5},{5,4},{6,7},{7,6},{8,9},{9,8},{10,11... | collective-permute-start | bytes 3145736 | tf_op jit(solution)/shard_map/ppermute | solution.py:31
  64.7 73.0 %collective-permute-start = (f32[4,128,512]{2,1,0:T(8,128)}, f32[4,128,512]{2,1,0:T(8,128)}, u32[]{:S(2)}, u32[]{:S(2)}) collective-permute-start(f32[4,128,512]{2,1,0:T(8,128)} %bitcast.62), channel_id=1, source_target_pairs={{0,1},{1,0},{2,3},{3,2},{4,5},{5,4},{6,7},{7,6},{8,9},{9,8},{10,11... | collective-permute-start | bytes 3145736 | tf_op jit(solution)/shard_map/ppermute | solution.py:31
  66.3 76.1 %copy-start = (f32[8,128,256]{2,1,0:T(8,128)}, f32[8,128,256]{2,1,0:T(8,128)S(1)}, u32[]{:S(2)}) copy-start(f32[8,128,256]{2,1,0:T(8,128)S(1)} %pad_maximum_fusion.x_ref) | copy-start | bytes 3145732
  66.3 59.4 %collective-permute-start.19 = (f32[4,128,256]{2,1,0:T(8,128)}, f32[4,128,256]{2,1,0:T(8,128)}, u32[]{:S(2)}, u32[]{:S(2)}) collective-permute-start(f32[4,128,256]{2,1,0:T(8,128)} %pad_maximum_fusion.11), channel_id=1, source_target_pairs={{0,1},{1,0},{2,3},{3,2},{4,5},{5,4},{6,7},{7,6},{8,9},{9,8},{10,11... | collective-permute-start | bytes 1572872 | tf_op jit(solution)/shard_map/ppermute | solution.py:31
  67.9 67.2 %collective-permute-start.9 = (f32[4,128,256]{2,1,0:T(8,128)}, f32[4,128,256]{2,1,0:T(8,128)}, u32[]{:S(2)}, u32[]{:S(2)}) collective-permute-start(f32[4,128,256]{2,1,0:T(8,128)} %pad_maximum_fusion.9), channel_id=1, source_target_pairs={{0,1},{1,0},{2,3},{3,2},{4,5},{5,4},{6,7},{7,6},{8,9},{9,8},{10,11... | collective-permute-start | bytes 1572872 | tf_op jit(solution)/shard_map/ppermute | solution.py:31
  70.3 68.0 %collective-permute-start.12 = (f32[8,128,256]{2,1,0:T(8,128)S(1)}, f32[8,128,256]{2,1,0:T(8,128)}, u32[]{:S(2)}, u32[]{:S(2)}) collective-permute-start(f32[8,128,256]{2,1,0:T(8,128)S(1)} %pad_maximum_fusion.x_ref), channel_id=1, source_target_pairs={{8,16},{24,0},{16,8},{0,24},{9,17},{25,1},{17,9},{1,25},{10,18},{2... | collective-permute-start | bytes 3145736 | tf_op jit(solution)/shard_map/ppermute | solution.py:227
  70.5 72.0 %copy-start.17 = (f32[2,512]{1,0:T(2,128)S(1)}, f32[2,512]{1,0:T(2,128)}, u32[]{:S(2)}) copy-start(f32[2,512]{1,0:T(2,128)} %copy-done.16) | copy-start | bytes 12292
  125.7 33.4 %collective-permute-start.10 = (f32[8,128,256]{2,1,0:T(8,128)S(1)}, f32[8,128,256]{2,1,0:T(8,128)S(1)}, u32[]{:S(2)}, u32[]{:S(2)}) collective-permute-start(f32[8,128,256]{2,1,0:T(8,128)S(1)} %pad_maximum_fusion.x_ref), channel_id=1, source_target_pairs={{0,8},{8,0},{16,24},{24,16},{1,9},{9,1},{17,25},{25,17},{2,10},{10... | collective-permute-start | bytes 3145736 | tf_op jit(solution)/shard_map/ppermute | solution.py:226
  135.1 25.5 %collective-permute-start.22 = (f32[8,128,256]{2,1,0:T(8,128)S(1)}, f32[8,128,256]{2,1,0:T(8,128)S(1)}, u32[]{:S(2)}, u32[]{:S(2)}) collective-permute-start(f32[8,128,256]{2,1,0:T(8,128)S(1)} %pad_maximum_fusion.2.x_ref), channel_id=1, source_target_pairs={{8,16},{24,0},{16,8},{0,24},{9,17},{25,1},{17,9},{1,25},{10,18},{2... | collective-permute-start | bytes 3145736 | tf_op jit(solution)/shard_map/ppermute | solution.py:227
  136.3 31.7 %collective-permute-start.20 = (f32[8,128,256]{2,1,0:T(8,128)S(1)}, f32[8,128,256]{2,1,0:T(8,128)}, u32[]{:S(2)}, u32[]{:S(2)}) collective-permute-start(f32[8,128,256]{2,1,0:T(8,128)S(1)} %pad_maximum_fusion.2.x_ref), channel_id=1, source_target_pairs={{0,8},{8,0},{16,24},{24,16},{1,9},{9,1},{17,25},{25,17},{2,10},{10... | collective-permute-start | bytes 3145736 | tf_op jit(solution)/shard_map/ppermute | solution.py:226
  137.7 45.4 %collective-permute-start.23 = (f32[8,128,256]{2,1,0:T(8,128)S(1)}, f32[8,128,256]{2,1,0:T(8,128)}, u32[]{:S(2)}, u32[]{:S(2)}) collective-permute-start(f32[8,128,256]{2,1,0:T(8,128)S(1)} %pad_maximum_fusion.3.x_ref), channel_id=1, source_target_pairs={{8,16},{24,0},{16,8},{0,24},{9,17},{25,1},{17,9},{1,25},{10,18},{2... | collective-permute-start | bytes 3145736 | tf_op jit(solution)/shard_map/ppermute | solution.py:227
  138.2 47.1 %collective-permute-start.21 = (f32[8,128,256]{2,1,0:T(8,128)S(1)}, f32[8,128,256]{2,1,0:T(8,128)}, u32[]{:S(2)}, u32[]{:S(2)}) collective-permute-start(f32[8,128,256]{2,1,0:T(8,128)S(1)} %pad_maximum_fusion.3.x_ref), channel_id=1, source_target_pairs={{0,8},{8,0},{16,24},{24,16},{1,9},{9,1},{17,25},{25,17},{2,10},{10... | collective-permute-start | bytes 3145736 | tf_op jit(solution)/shard_map/ppermute | solution.py:226
  159.2 46.1 %collective-permute-start.13 = (f32[8,128,256]{2,1,0:T(8,128)}, f32[8,128,256]{2,1,0:T(8,128)S(1)}, u32[]{:S(2)}, u32[]{:S(2)}) collective-permute-start(f32[8,128,256]{2,1,0:T(8,128)} %pad_maximum_fusion.1.x_ref), channel_id=1, source_target_pairs={{8,16},{24,0},{16,8},{0,24},{9,17},{25,1},{17,9},{1,25},{10,18},{2... | collective-permute-start | bytes 3145736 | tf_op jit(solution)/shard_map/ppermute | solution.py:227
  160.6 50.8 %collective-permute-start.11 = (f32[8,128,256]{2,1,0:T(8,128)}, f32[8,128,256]{2,1,0:T(8,128)S(1)}, u32[]{:S(2)}, u32[]{:S(2)}) collective-permute-start(f32[8,128,256]{2,1,0:T(8,128)} %pad_maximum_fusion.1.x_ref), channel_id=1, source_target_pairs={{0,8},{8,0},{16,24},{24,16},{1,9},{9,1},{17,25},{25,17},{2,10},{10... | collective-permute-start | bytes 3145736 | tf_op jit(solution)/shard_map/ppermute | solution.py:226
  168.0 46.9 %collective-permute-start.27 = (f32[256,512]{1,0:T(8,128)}, f32[256,512]{1,0:T(8,128)}, u32[]{:S(2)}, u32[]{:S(2)}) collective-permute-start(f32[256,512]{1,0:T(8,128)} %pad_maximum_fusion.13), channel_id=1, source_target_pairs={{0,2},{1,3},{2,0},{3,1},{4,6},{5,7},{6,4},{7,5},{8,10},{9,11},{10,... | collective-permute-start | bytes 1572872 | tf_op jit(solution)/shard_map/ppermute | solution.py:31
  183.2 61.0 %collective-permute-start.28 = (f32[256,512]{1,0:T(8,128)}, f32[256,512]{1,0:T(8,128)}, u32[]{:S(2)}, u32[]{:S(2)}) collective-permute-start(f32[256,512]{1,0:T(8,128)} %pad_maximum_fusion.14), channel_id=1, source_target_pairs={{0,4},{1,5},{2,6},{3,7},{4,0},{5,1},{6,2},{7,3},{8,12},{9,13},{10,... | collective-permute-start | bytes 1572872 | tf_op jit(solution)/shard_map/ppermute | solution.py:31
  185.4 58.7 %collective-permute-start.29 = (f32[256,512]{1,0:T(8,128)}, f32[256,512]{1,0:T(8,128)S(1)}, u32[]{:S(2)}, u32[]{:S(2)}) collective-permute-start(f32[256,512]{1,0:T(8,128)} %pad_maximum_fusion.15), channel_id=1, source_target_pairs={{0,6},{1,7},{2,4},{3,5},{4,2},{5,3},{6,0},{7,1},{8,14},{9,15},{10,... | collective-permute-start | bytes 1572872 | tf_op jit(solution)/shard_map/ppermute | solution.py:31
  205.3 58.9 %collective-permute-start.3 = (f32[256,512]{1,0:T(8,128)S(1)}, f32[256,512]{1,0:T(8,128)S(1)}, u32[]{:S(2)}, u32[]{:S(2)}) collective-permute-start(f32[256,512]{1,0:T(8,128)S(1)} %pad_maximum_fusion.7), channel_id=1, source_target_pairs={{0,6},{1,7},{2,4},{3,5},{4,2},{5,3},{6,0},{7,1},{8,14},{9,15},{10,... | collective-permute-start | bytes 1572872 | tf_op jit(solution)/shard_map/ppermute | solution.py:31
  211.4 65.1 %collective-permute-start.2 = (f32[256,512]{1,0:T(8,128)S(1)}, f32[256,512]{1,0:T(8,128)S(1)}, u32[]{:S(2)}, u32[]{:S(2)}) collective-permute-start(f32[256,512]{1,0:T(8,128)S(1)} %pad_maximum_fusion.6), channel_id=1, source_target_pairs={{0,4},{1,5},{2,6},{3,7},{4,0},{5,1},{6,2},{7,3},{8,12},{9,13},{10,... | collective-permute-start | bytes 1572872 | tf_op jit(solution)/shard_map/ppermute | solution.py:31
  215.0 61.5 %collective-permute-start.1 = (f32[256,512]{1,0:T(8,128)S(1)}, f32[256,512]{1,0:T(8,128)S(1)}, u32[]{:S(2)}, u32[]{:S(2)}) collective-permute-start(f32[256,512]{1,0:T(8,128)S(1)} %pad_maximum_fusion.5), channel_id=1, source_target_pairs={{0,2},{1,3},{2,0},{3,1},{4,6},{5,7},{6,4},{7,5},{8,10},{9,11},{10,... | collective-permute-start | bytes 1572872 | tf_op jit(solution)/shard_map/ppermute | solution.py:31
  (23 other events, 468.9 us)

commit v2 on v0

v2 whole, which is shorter than its diff:
```python
import functools

import jax
import jax.numpy as jnp
from jax import lax
from jax.experimental import pallas as pl
from jax.experimental.pallas import tpu as pltpu
from jax.sharding import PartitionSpec as P

taper_reach = 0.6
tile_side = 128
f32, bf16 = jnp.float32, jnp.bfloat16
anywhere = pl.BlockSpec(memory_space=pl.ANY)
in_vmem = pl.BlockSpec(memory_space=pltpu.VMEM)
span_edges = (0, 6, 8)
small_cost = pl.CostEstimate(flops=1000, bytes_accessed=1000, transcendentals=0)
vmem_limit = 56 * 1024 * 1024


def dot(a, b):
    return lax.dot_general(a, b, (((1,), (0,)), ((), ())), preferred_element_type=f32)


def split(x):
    high = x.astype(bf16)
    return high, (x - high.astype(f32)).astype(bf16)


def swap(x, axis, distance):
    size = lax.axis_size(axis)
    return lax.ppermute(x, axis, [(i, i ^ distance) for i in range(size)])


def after(x, *deps):
    return lax.optimization_barrier((x, *deps))[0] if deps else x


def join_kernel(a_ref, b_ref, out_ref, sems):
    size = a_ref.shape[0]
    copies = [
        pltpu.make_async_copy(a_ref, out_ref.at[pl.ds(0, size)], sems.at[0]),
        pltpu.make_async_copy(b_ref, out_ref.at[pl.ds(size, size)], sems.at[1]),
    ]
    for copy in copies:
        copy.start()
    for copy in copies:
        copy.wait()


def join(a, b):
    return pl.pallas_call(
        join_kernel,
        out_shape=jax.ShapeDtypeStruct((2 * a.shape[0], *a.shape[1:]), a.dtype),
        in_specs=[anywhere] * 2,
        out_specs=in_vmem,
        scratch_shapes=[pltpu.SemaphoreType.DMA((2,))],
        compiler_params=pltpu.CompilerParams(vmem_limit_bytes=vmem_limit),
        cost_estimate=small_cost,
    )(a, b)


def prep_obs_kernel(order, near_ref, far_ref, high_ref, low_ref):
    blocks, rows, width = near_ref.shape
    refs = [near_ref.at[i] for i in range(blocks)] + [far_ref.at[i] for i in range(blocks)]
    total = jnp.zeros((1, width), f32)
    for ref in refs:
        total += jnp.sum(ref[...], axis=0, keepdims=True)
    mean = total / (2 * blocks * rows)
    for i, ref in enumerate(refs):
        high, low = split((ref[...] - mean).T)
        at = pl.ds(order[i] * rows, rows)
        high_ref[:, at] = high
        low_ref[:, at] = low


def prep_obs(pair, order):
    blocks, rows, width = pair[0].shape
    whole = pl.BlockSpec((blocks, rows, 128), lambda j: (0, 0, j))
    return pl.pallas_call(
        functools.partial(prep_obs_kernel, order),
        grid=(width // 128,),
        out_shape=[jax.ShapeDtypeStruct((width, 2 * blocks * rows), bf16)] * 2,
        in_specs=[whole] * 2,
        out_specs=[pl.BlockSpec((128, 2 * blocks * rows), lambda j: (j, 0))] * 2,
        compiler_params=pltpu.CompilerParams(vmem_limit_bytes=vmem_limit),
        cost_estimate=small_cost,
    )(*pair)


def update_kernel(parts, order, first, start, *refs):
    me_ref, points, refs = refs[0], refs[1], refs[2:]
    me = me_ref[0]
    nobs = len(parts)
    obs_high, refs = refs[:nobs], refs[nobs:]
    obs_low, refs = refs[:nobs], refs[nobs:]
    ninn = len(refs) - (15 if first else 16)
    inn, refs = refs[:ninn], refs[ninn:]
    taper = refs[0]
    refs = refs[1 if first else 2 :]
    out, total, x_high, x_low, yh, yl, w, tap, kh, kl, sem_x, sem_y, sem_w, sem_out = refs
    members, width = total.shape
    local = len(order)
    ml = members // local
    window = tap.shape[0]
    slot_obs = window // 3
    band = min(512, members)
    x_copies = [
        pltpu.make_async_copy(
            points.at[lax.div(me ^ r, 2), r % 2], total.at[pl.ds(r * ml, ml)], sem_x
        )
        for r in range(local)
    ]
    y_copies = []
    for i, (slot, at, size) in enumerate(parts):
        here = pl.ds(at, size)
        y_copies.append(
            [
                pltpu.make_async_copy(obs_high[i], yh.at[here], sem_y.at[slot, 0]),
                pltpu.make_async_copy(obs_low[i], yl.at[here], sem_y.at[slot, 1]),
                pltpu.make_async_copy(
                    taper.at[here, pl.ds(start, width)], tap.at[here], sem_y.at[slot, 2]
                ),
            ]
        )
    w_copies = []
    for i in range(ninn):
        slot, part = i // 2, i % 2
        here = pl.ds(slot * slot_obs, slot_obs)
        for k in range(local // 2):
            at = pl.ds(order[part * (local // 2) + k] * ml, ml)
            w_copies.append(pltpu.make_async_copy(inn[i].at[k], w.at[at, here], sem_w))
    for copy in x_copies + y_copies[0]:
        copy.start()
    pltpu.make_async_copy(total, total, sem_x).wait()

    def halves(i, carry):
        at = pl.ds(pl.multiple_of(i * 128, 128), 128)
        x_high[at, :], x_low[at, :] = split(total[at, :])
        return carry

    lax.fori_loop(0, members // 128, halves, 0)
    for copy in y_copies[1] + y_copies[2] + w_copies:
        copy.start()

    def weights(slot, carry):
        here = pl.ds(pl.multiple_of(slot * slot_obs, 128), slot_obs)
        pltpu.make_async_copy(yh.at[here], yh.at[here], sem_y.at[slot, 0]).wait()
        pltpu.make_async_copy(yl.at[here], yl.at[here], sem_y.at[slot, 1]).wait()
        pltpu.make_async_copy(tap.at[here], tap.at[here], sem_y.at[slot, 2]).wait()
        cov = dot(yh[here, :], x_high[...]) + dot(yl[here, :], x_high[...])
        cov += dot(yh[here, :], x_low[...])
        kh[here, :], kl[here, :] = split(cov * tap[here, :])
        return carry

    lax.fori_loop(0, 3, weights, 0)
    pltpu.make_async_copy(w, w, sem_w).wait()
    blocks = band // ml

    def change(i, carry):
        at = pl.ds(pl.multiple_of(i * band, band), band)
        w_high, w_low = split(w[at, :])
        total[at, :] += dot(w_high, kh[...]) + dot(w_low, kh[...]) + dot(w_high, kl[...])
        for r in range(blocks):
            block = i * blocks + r
            pltpu.make_async_copy(
                total.at[pl.ds(pl.multiple_of(block * ml, ml), ml)],
                out.at[pl.ds(pl.multiple_of((me ^ block) * ml, ml), ml), pl.ds(start, width)],
                sem_out.at[block],
            ).start()
        return carry

    lax.fori_loop(0, members // band, change, 0)
    for block in range(local):
        pltpu.make_async_copy(
            total.at[pl.ds(block * ml, ml)],
            out.at[pl.ds(pl.multiple_of((me ^ block) * ml, ml), ml), pl.ds(start, width)],
            sem_out.at[block],
        ).wait()


def regroup_kernel(begin, side_ref, state_ref, keep_ref, give_ref, sem):
    blocks, ml, width = keep_ref.shape
    per_device = state_ref.shape[1] // (2 * blocks)
    side = side_ref[0]
    copies = []
    for ref, which in ((give_ref, 1 - side), (keep_ref, side)):
        for z in range(blocks):
            at = pl.multiple_of((2 * z + which) * per_device + begin, 128)
            copies.append(pltpu.make_async_copy(state_ref.at[:, pl.ds(at, width)], ref.at[z], sem))
    for copy in copies:
        copy.start()
    pltpu.make_async_copy(keep_ref, keep_ref, sem).wait()
    pltpu.make_async_copy(give_ref, give_ref, sem).wait()


def regroup(side, state, groups, begin, width):
    shape = jax.ShapeDtypeStruct((groups // 2, state.shape[0], width), f32)
    return pl.pallas_call(
        functools.partial(regroup_kernel, begin),
        out_shape=[shape] * 2,
        in_specs=[pl.BlockSpec(memory_space=pltpu.SMEM), anywhere],
        out_specs=[in_vmem] * 2,
        scratch_shapes=[pltpu.SemaphoreType.DMA],
        compiler_params=pltpu.CompilerParams(vmem_limit_bytes=vmem_limit),
        cost_estimate=small_cost,
    )(side, state)


def pair_kernel(begin, a_ref, b_ref, out_ref, sem):
    here = pl.ds(begin, out_ref.shape[3])
    copies = []
    for z in range(a_ref.shape[0]):
        copies.append(pltpu.make_async_copy(a_ref.at[z, :, here], out_ref.at[z, 0], sem))
        copies.append(pltpu.make_async_copy(b_ref.at[z, :, here], out_ref.at[z, 1], sem))
    for copy in copies:
        copy.start()
    pltpu.make_async_copy(out_ref, out_ref, sem).wait()


def pair(a, b, begin, width):
    return pl.pallas_call(
        functools.partial(pair_kernel, begin),
        out_shape=jax.ShapeDtypeStruct((a.shape[0], 2, a.shape[1], width), f32),
        in_specs=[anywhere] * 2,
        out_specs=in_vmem,
        scratch_shapes=[pltpu.SemaphoreType.DMA],
        compiler_params=pltpu.CompilerParams(vmem_limit_bytes=vmem_limit),
        cost_estimate=small_cost,
    )(a, b)


def update(me, points, obs, parts, innov, order, taper, out, start, per_device):
    members, width = 2 * points.shape[0] * points.shape[2], points.shape[3]
    window_obs = taper.shape[0]
    first = out is None
    operands = [me, points, *[o[0] for o in obs], *[o[1] for o in obs], *innov, taper]
    operands += [] if first else [out]
    return pl.pallas_call(
        functools.partial(update_kernel, parts, order, first, start),
        out_shape=jax.ShapeDtypeStruct((members, per_device), f32),
        in_specs=[pl.BlockSpec(memory_space=pltpu.SMEM)] + [anywhere] * (len(operands) - 1),
        out_specs=anywhere,
        scratch_shapes=[
            pltpu.VMEM((members, width), f32),
            pltpu.VMEM((members, width), bf16),
            pltpu.VMEM((members, width), bf16),
            pltpu.VMEM((window_obs, members), bf16),
            pltpu.VMEM((window_obs, members), bf16),
            pltpu.VMEM((members, window_obs), f32),
            pltpu.VMEM((window_obs, width), f32),
            pltpu.VMEM((window_obs, width), bf16),
            pltpu.VMEM((window_obs, width), bf16),
            pltpu.SemaphoreType.DMA,
            pltpu.SemaphoreType.DMA((3, 3)),
            pltpu.SemaphoreType.DMA,
            pltpu.SemaphoreType.DMA((len(order),)),
        ],
        input_output_aliases={} if first else {len(operands) - 1: 0},
        compiler_params=pltpu.CompilerParams(vmem_limit_bytes=vmem_limit),
        cost_estimate=small_cost,
    )(*operands)


def shards(state, obs_ensemble, innovations, obs_coords, tile_list, tile_counts):
    ml = state.shape[0]
    groups = lax.axis_size("mem")
    domains = lax.axis_size("dom")
    per_domain = state.shape[1]
    per_device = per_domain // groups
    obs_local = obs_ensemble.shape[1]
    members = ml * groups
    me = lax.axis_index("mem")
    domain = lax.axis_index("dom")
    odd = domain % 2

    bits = []
    b = groups // 2
    while b >= 1:
        bits.append(b)
        b //= 2
    order = [0]
    for b in bits:
        order = order + [r ^ b for r in order]

    across = [((i + 1) % domains, (i + 2) % domains) for i in range(0, domains, 2)]
    across = across + [(t, s) for s, t in across]
    chip = [(i, i ^ 1) for i in range(domains)]

    def tapered(coord_beside, coord_beyond):
        position = jnp.stack([jnp.int32(1), 2 - 2 * odd, 2 * odd]).astype(jnp.int32)
        coords = jnp.concatenate([obs_coords, coord_beside, coord_beyond], axis=1)
        nblocks = per_device // tile_side
        window = obs_local // tile_side
        point_ids, obs_ids = tile_list[0, 0, 0], tile_list[0, 0, 1]
        slots = point_ids.shape[0]
        live = (jnp.arange(slots, dtype=jnp.int32) < tile_counts[0, 0]).astype(f32)
        block_ids = (position[:, None] * window + jnp.arange(window, dtype=jnp.int32)[None]).reshape(-1)
        by_obs = (obs_ids[None, :] == block_ids[:, None]).astype(f32) * live[None]
        by_point = (point_ids[:, None] == jnp.arange(nblocks, dtype=jnp.int32)[None]).astype(f32)
        mask = jnp.sum(by_obs[:, :, None] * by_point[None], axis=1)
        mask = jnp.repeat(mask, tile_side, axis=1) / (members - 1)
        within = me * per_device + jnp.arange(per_device, dtype=jnp.int32)
        point_x = domain.astype(f32) + ((within % 32).astype(f32) + 0.5) / 32.0
        point_y = ((within // 32).astype(f32) + 0.5) / float(per_domain // 32)
        gap_x = jnp.abs(point_x[None, :] - coords[0][:, None])
        gap_x = jnp.minimum(gap_x, float(domains) - gap_x)
        gap_y = point_y[None, :] - coords[1][:, None]
        taper = jnp.exp(-(gap_x * gap_x + gap_y * gap_y) / (2.0 * taper_reach * taper_reach))
        taper = (taper.reshape(-1, tile_side, per_device) * mask[:, None, :]).reshape(-1, per_device)
        return taper

    edges = [per_device * e // 8 for e in span_edges]
    spans = [(edges[c], edges[c + 1] - edges[c]) for c in range(len(edges) - 1)]
    sides = [[i for i in range(groups) if i % 2 == s] for s in range(2)]
    my_side = (me % 2).astype(jnp.int32).reshape(1)

    keep, give = regroup(my_side, state, groups, 0, per_device)

    def assembled(halves, *deps):
        return lax.all_to_all(
            after(halves, *deps),
            "mem",
            split_axis=0,
            concat_axis=0,
            tiled=True,
            axis_index_groups=sides,
        )

    def far_gathered(x, *deps):
        x, got = x[None], []
        for b in bits[:-1]:
            got.append(swap(after(x, *deps), "mem", b))
            x = join(x, got[-1])
            deps = ()
        return x, got

    def cross(x, *deps):
        return lax.ppermute(after(x, *deps), "dom", across)

    def beside(x, *deps):
        return lax.ppermute(after(x, *deps), "dom", chip)

    def side(x, *deps):
        return swap(after(x, *deps), "mem", 1)

    got = side(give)
    obs_near, obs_got = far_gathered(obs_ensemble)
    inn_near, inn_got = far_gathered(innovations, obs_got[0])
    coord_beside = beside(obs_coords, obs_got[0])
    coord_beyond = cross(obs_coords, obs_got[0])
    taper = tapered(coord_beside, coord_beyond)
    obs_near_beyond = cross(obs_near, coord_beyond)
    obs_far = side(obs_near)
    paired = [pair(keep, got, *span) for span in spans]
    points = [assembled(paired[0], obs_got[-1], inn_got[-1])]
    obs_near_beside = beside(obs_near, obs_near_beyond, obs_far)
    inn_near_beyond = cross(inn_near, obs_near_beside, taper, paired[1])
    inn_far = side(inn_near, obs_near_beside)
    obs_far_beside = beside(obs_far, obs_near_beside)
    ready_own = prep_obs((obs_near, obs_far), order)
    ready_beside = prep_obs((obs_near_beside, obs_far_beside), order)
    obs_far_beyond = cross(obs_far, inn_near_beyond, inn_far, obs_far_beside, ready_own[0])
    inn_far_beyond = side(inn_near_beyond, inn_far)
    inn_near_beside = beside(inn_near, obs_far_beyond, inn_far_beyond, ready_beside[0])
    inn_far_beside = beside(inn_far, inn_near_beside)
    points.append(assembled(paired[1], points[0]))
    ready_beyond = prep_obs((obs_near_beyond, obs_far_beyond), order)
    obs = [ready_own, ready_beside, ready_beyond]
    innov = [inn_near, inn_far, inn_near_beside, inn_far_beside, inn_near_beyond, inn_far_beyond]
    parts = [(slot, slot * obs_local, obs_local) for slot in range(3)]
    out = None
    for c in range(len(spans)):
        out = update(
            me.astype(jnp.int32).reshape(1),
            points[c],
            obs,
            parts,
            innov,
            order,
            taper,
            out,
            spans[c][0],
            per_device,
        )
    return out


def solution(mesh):
    return jax.shard_map(
        shards,
        mesh=mesh,
        in_specs=(
            P("mem", "dom"),
            P("mem", "dom"),
            P("mem", "dom"),
            P(None, "dom"),
            P("dom", "mem", None, None),
            P("dom", "mem"),
        ),
        out_specs=P(None, ("dom", "mem")),
        check_vma=False,
    )
```

time: 525 us -> 187 us (0.36)
  waiting for transfers between devices: 239 us -> 83.9 us
  local copies, waits for them, and re-layouts: 133 us -> 7.59 us
  matrix products: 104 us -> 0 us
  Pallas kernels: 0 us -> 62.6 us
  other arithmetic: 25.5 us -> 4.94 us
  starting transfers between devices: 9.2 us -> 26 us
  between operations: 14.1 us -> 0.87 us
    all_gather x2 -> x0, waiting for transfers between devices: 156 us -> none  [the longest x1 104 us: shards(): lax.all_gather(obs_ensemble, 'mem', axis=0, tiled=True)]
    dot_general x6 -> x0, matrix products: 104 us -> none  [the longest x2 51.3 us: tile_batch(): jnp.einsum('mti,mtj->tij', x_blocks, y_blocks, precision=highest)]
    gather x14 -> x0, local copies, waits for them, and re-layouts: 62.7 us -> none  [the longest x2 19.8 us: tile_batch(): y_blocks = jnp.take(anom_grid, obs_ids, axis=1)]
    pallas_call x0 -> x12, Pallas kernels: none -> 62.6 us  [the longest x2 31.9 us: update(): pl.pallas_call(functools.partial(update_kernel, parts, order, first, star...]
    transpose x2 -> x0, local copies, waits for them, and re-layouts: 25.2 us -> none  [tile_batch(): increment = jnp.einsum('mtj,tij->mti', w_blocks, weights, precision=highest)]
    unnamed x11 -> x32, local copies, waits for them, and re-layouts: 23 us -> 7.4 us
    ppermute x2 -> x17, starting transfers between devices: 1.75 us -> 15.7 us  [the longest x8 12 us: swap(): return lax.ppermute(x, axis, [(i, i ^ distance) for i in range(size)])]
    concatenate x2 -> x0, other arithmetic: 12.6 us -> none  [the longest x1 8.61 us: padded(): block = jnp.concatenate([low, block, high], axis=dim)]
  transfers between devices with their start and end apart: 5 -> 19, of which waited for: 3 -> 12; matrix products, arithmetic and copies ran while one was open for 6% -> 3% of each run, Pallas kernels for 0% -> 25%
where the time goes in v2:
time: 187 us; the launch traced here: 186 us
  waiting for transfers between devices  83.9 us (45%)
  Pallas kernels  62.6 us (33%)
  starting transfers between devices  26 us (14%)
  local copies, waits for them, and re-layouts  7.59 us (4%)
  other arithmetic  4.94 us (3%)
    ppermute x8, waiting for transfers between devices, swap(): return lax.ppermute(x, axis, [(i, i ^ distance) for i in range(size)])  53.5 us
    pallas_call x2, Pallas kernels, update(): pl.pallas_call(functools.partial(update_kernel, parts, order, first, star...  31.9 us
    ppermute x4, waiting for transfers between devices, cross(): return lax.ppermute(after(x, *deps), 'dom', across)  28.5 us
    pallas_call x3, Pallas kernels, prep_obs(): pl.pallas_call(functools.partial(prep_obs_kernel, order), grid=(width //...  12.6 us
    ppermute x8, starting transfers between devices, swap(): return lax.ppermute(x, axis, [(i, i ^ distance) for i in range(size)])  12 us
    all_to_all x2, starting transfers between devices, assembled(): lax.all_to_all(after(halves, *deps), 'mem', split_axis=0, concat_axis=0,...  10.3 us
    pallas_call x4, Pallas kernels, join(): pl.pallas_call(join_kernel, out_shape=jax.ShapeDtypeStruct((2 * a.shape[0...  8.11 us
    unnamed x32, local copies, waits for them, and re-layouts  7.4 us
  transfers between devices with their start and end apart: 19, of which 12 were waited for; matrix products, arithmetic and copies ran while one was open for 3% of the time, Pallas kernels for 25%

profile of v2, /device:TPU:0, one launch (start us, length us, event | category | flops | bytes accessed | tf_op | source)
XLA Modules:
  0.0 186.0 jit_solution(17769866278548297799)
XLA Ops:
  0.0 4.2 %shard_map.64 = (f32[4,128,1024]{2,1,0:T(8,128)}, f32[4,128,1024]{2,1,0:T(8,128)}) custom-call(s32[1]{0:T(128)} %bitcast.1.side_ref, f32[128,8192]{1,0:T(8,128)} %state_ref.1), custom_call_target="tpu_custom_call" | custom-call | flops 1000 | bytes 1000 | tf_op jit(solution)/shard_map/pallas_call | solution.py:198
  4.2 3.0 %collective-permute-start = (f32[4,128,1024]{2,1,0:T(8,128)}, f32[4,128,1024]{2,1,0:T(8,128)S(1)}, u32[]{:S(2)}, u32[]{:S(2)}) collective-permute-start(f32[4,128,1024]{2,1,0:T(8,128)} %get-tuple-element.27), channel_id=1, source_target_pairs={{0,1},{1,0},{2,3},{3,2},{4,5},{5,4},{6,7},{7,6},{8,9},{9,8},{10,11... | collective-permute-start | bytes 6291464 | tf_op jit(solution)/shard_map/ppermute | solution.py:31
  7.2 2.6 %collective-permute-start.1 = (f32[1,128,512]{2,1,0:T(8,128)}, f32[1,128,512]{2,1,0:T(8,128)S(1)}, u32[]{:S(2)}, u32[]{:S(2)}) collective-permute-start(f32[1,128,512]{2,1,0:T(8,128)} %bitcast.19), channel_id=1, source_target_pairs={{0,4},{1,5},{2,6},{3,7},{4,0},{5,1},{6,2},{7,3},{8,12},{9,13},{10,... | collective-permute-start | bytes 786440 | tf_op jit(solution)/shard_map/ppermute | solution.py:31
  9.8 11.9 %collective-permute-done.1.b_ref = f32[1,128,512]{2,1,0:T(8,128)S(1)} collective-permute-done((f32[1,128,512]{2,1,0:T(8,128)}, f32[1,128,512]{2,1,0:T(8,128)S(1)}, u32[]{:S(2)}, u32[]{:S(2)}) %collective-permute-start.1) | collective-permute-done | bytes 262176 | tf_op jit(solution)/shard_map/ppermute | solution.py:31
  22.4 1.9 %shard_map.67.a_ref = f32[2,128,512]{2,1,0:T(8,128)} custom-call(f32[1,128,512]{2,1,0:T(8,128)} %bitcast.20, f32[1,128,512]{2,1,0:T(8,128)} %copy-done.11), custom_call_target="tpu_custom_call" | custom-call | flops 1000 | bytes 1000 | tf_op jit(solution)/shard_map/pallas_call | solution.py:51
  24.3 3.4 %collective-permute-start.2 = (f32[2,128,512]{2,1,0:T(8,128)}, f32[2,128,512]{2,1,0:T(8,128)S(1)}, u32[]{:S(2)}, u32[]{:S(2)}) collective-permute-start(f32[2,128,512]{2,1,0:T(8,128)} %shard_map.67.a_ref), channel_id=1, source_target_pairs={{0,2},{1,3},{2,0},{3,1},{4,6},{5,7},{6,4},{7,5},{8,10},{9,11},{10,... | collective-permute-start | bytes 1572872 | tf_op jit(solution)/shard_map/ppermute | solution.py:31
  27.7 8.0 %collective-permute-done.3.b_ref = f32[1,128,512]{2,1,0:T(8,128)S(1)} collective-permute-done((f32[1,128,512]{2,1,0:T(8,128)}, f32[1,128,512]{2,1,0:T(8,128)S(1)}, u32[]{:S(2)}, u32[]{:S(2)}) %collective-permute-start.3) | collective-permute-done | bytes 262176 | tf_op jit(solution)/shard_map/ppermute | solution.py:31
  36.4 1.8 shard_map.68.a_ref
  38.4 5.8 %collective-permute-done.2.b_ref = f32[2,128,512]{2,1,0:T(8,128)S(1)} collective-permute-done((f32[2,128,512]{2,1,0:T(8,128)}, f32[2,128,512]{2,1,0:T(8,128)S(1)}, u32[]{:S(2)}, u32[]{:S(2)}) %collective-permute-start.2) | collective-permute-done | bytes 524320 | tf_op jit(solution)/shard_map/ppermute | solution.py:31
  45.1 2.2 %shard_map.69.near_ref = f32[4,128,512]{2,1,0:T(8,128)} custom-call(f32[2,128,512]{2,1,0:T(8,128)} %shard_map.67.a_ref, f32[2,128,512]{2,1,0:T(8,128)} %copy-done.9), custom_call_target="tpu_custom_call" | custom-call | flops 1000 | bytes 1000 | tf_op jit(solution)/shard_map/pallas_call | solution.py:51
  47.9 5.9 %collective-permute-done.b_ref = f32[4,128,1024]{2,1,0:T(8,128)S(1)} collective-permute-done((f32[4,128,1024]{2,1,0:T(8,128)}, f32[4,128,1024]{2,1,0:T(8,128)S(1)}, u32[]{:S(2)}, u32[]{:S(2)}) %collective-permute-start) | collective-permute-done | bytes 2097184 | tf_op jit(solution)/shard_map/ppermute | solution.py:31
  53.9 1.4 copy-done.1
  55.3 3.5 %shard_map.66 = f32[4,2,128,768]{3,2,1,0:T(8,128)} custom-call(f32[4,128,1024]{2,1,0:T(8,128)} %get-tuple-element.26.a_ref, f32[4,128,1024]{2,1,0:T(8,128)} %copy-done.1), custom_call_target="tpu_custom_call" | custom-call | flops 1000 | bytes 1000 | tf_op jit(solution)/shard_map/pallas_call | solution.py:221
  59.6 5.4 %all-to-all-start = ((f32[4,2,128,768]{3,2,1,0:T(8,128)}), f32[4,2,128,768]{3,2,1,0:T(8,128)S(1)}, u32[]{:S(2)}, u32[]{:S(2)}) async-start(f32[4,2,128,768]{3,2,1,0:T(8,128)} %shard_map.66), calls=%async_computation | async-start | bytes 6291456 | tf_op jit(solution)/shard_map/all_to_all | solution.py:320
  65.9 7.3 %collective-permute-done.7.near_ref = f32[4,128,512]{2,1,0:T(8,128)} collective-permute-done((f32[4,128,512]{2,1,0:T(8,128)}, f32[4,128,512]{2,1,0:T(8,128)}, u32[]{:S(2)}, u32[]{:S(2)}) %collective-permute-start.7) | collective-permute-done | bytes 1048608 | tf_op jit(solution)/shard_map/ppermute | solution.py:338
  73.1 2.5 %collective-permute-done.5.far_ref = f32[4,128,512]{2,1,0:T(8,128)} collective-permute-done((f32[4,128,512]{2,1,0:T(8,128)}, f32[4,128,512]{2,1,0:T(8,128)}, u32[]{:S(2)}, u32[]{:S(2)}) %collective-permute-start.5) | collective-permute-done | bytes 1048608 | tf_op jit(solution)/shard_map/ppermute | solution.py:31
  76.6 1.7 collective-permute-done.10
  78.4 4.6 %fusion.5.refs_14_ = f32[1536,1024]{1,0:T(8,128)} fusion(f32[12,1024]{1,0:T(8,128)S(1)} %bitcast.17, f32[1536]{0:T(1024)S(1)} %get-tuple-element.48, f32[1024]{0:T(1024)S(1)} %get-tuple-element.52, f32[1536]{0:T(1024)S(1)} %get-tuple-element.47, f32[1024]{0:T(1024)S(1)} %get-tuple-element.51), kind=kLoop, calls=%fused_computation.6 | loop fusion | flops 17301504 | bytes 6361088 | tf_op jit(solution)/shard_map/mul | solution.py:309
  83.0 2.2 %shard_map.72.refs_8_ = f32[4,128,512]{2,1,0:T(8,128)} custom-call(f32[2,128,512]{2,1,0:T(8,128)} %shard_map.68.a_ref, f32[2,128,512]{2,1,0:T(8,128)} %copy-done.8), custom_call_target="tpu_custom_call" | custom-call | flops 1000 | bytes 1000 | tf_op jit(solution)/shard_map/pallas_call | solution.py:51
  85.2 2.3 %shard_map.65 = f32[4,2,128,256]{3,2,1,0:T(8,128)} custom-call(f32[4,128,1024]{2,1,0:T(8,128)} %get-tuple-element.26.a_ref, f32[4,128,1024]{2,1,0:T(8,128)} %copy-done.1), custom_call_target="tpu_custom_call" | custom-call | flops 1000 | bytes 1000 | tf_op jit(solution)/shard_map/pallas_call | solution.py:221
  87.5 1.8 collective-permute-start.12
  90.9 4.2 %shard_map.70 = (bf16[512,1024]{1,0:T(8,128)(2,1)}, bf16[512,1024]{1,0:T(8,128)(2,1)}) custom-call(f32[4,128,512]{2,1,0:T(8,128)} %shard_map.69.near_ref, f32[4,128,512]{2,1,0:T(8,128)} %collective-permute-done.5.far_ref), custom_call_target="tpu_custom_call" | custom-call | flops 1000 | bytes 1000 | tf_op jit(solution)/shard_map/pallas_call | solution.py:79
  95.1 17.9 %collective-permute-done.12.refs_9_ = f32[4,128,512]{2,1,0:T(8,128)S(1)} collective-permute-done((f32[4,128,512]{2,1,0:T(8,128)}, f32[4,128,512]{2,1,0:T(8,128)S(1)}, u32[]{:S(2)}, u32[]{:S(2)}) %collective-permute-start.12) | collective-permute-done | bytes 1048608 | tf_op jit(solution)/shard_map/ppermute | solution.py:31
  113.0 1.9 %collective-permute-done.11.refs_12_ = f32[4,128,512]{2,1,0:T(8,128)S(1)} collective-permute-done((f32[4,128,512]{2,1,0:T(8,128)}, f32[4,128,512]{2,1,0:T(8,128)S(1)}, u32[]{:S(2)}, u32[]{:S(2)}) %collective-permute-start.11) | collective-permute-done | bytes 1048608 | tf_op jit(solution)/shard_map/ppermute | solution.py:338
  115.9 1.2 collective-permute-start.13
  117.7 4.2 %shard_map.71 = (bf16[512,1024]{1,0:T(8,128)(2,1)}, bf16[512,1024]{1,0:T(8,128)(2,1)}) custom-call(f32[4,128,512]{2,1,0:T(8,128)} %collective-permute-done.8.near_ref, f32[4,128,512]{2,1,0:T(8,128)} %copy-done.7), custom_call_target="tpu_custom_call" | custom-call | flops 1000 | bytes 1000 | tf_op jit(solution)/shard_map/pallas_call | solution.py:79
  121.9 19.4 %collective-permute-done.13.far_ref = f32[4,128,512]{2,1,0:T(8,128)S(1)} collective-permute-done((f32[4,128,512]{2,1,0:T(8,128)}, f32[4,128,512]{2,1,0:T(8,128)S(1)}, u32[]{:S(2)}, u32[]{:S(2)}) %collective-permute-start.13) | collective-permute-done | bytes 1048608 | tf_op jit(solution)/shard_map/ppermute | solution.py:338
  141.3 1.4 collective-permute-done.14.refs_13_
  143.6 4.9 %all-to-all-start.1 = ((f32[4,2,128,256]{3,2,1,0:T(8,128)}), f32[4,2,128,256]{3,2,1,0:T(8,128)}, u32[]{:S(2)}, u32[]{:S(2)}) async-start(f32[4,2,128,256]{3,2,1,0:T(8,128)} %shard_map.65), calls=%async_computation.1 | async-start | bytes 2097152 | tf_op jit(solution)/shard_map/all_to_all | solution.py:320
  148.7 4.2 %shard_map.73 = (bf16[512,1024]{1,0:T(8,128)(2,1)}, bf16[512,1024]{1,0:T(8,128)(2,1)}) custom-call(f32[4,128,512]{2,1,0:T(8,128)} %collective-permute-done.7.near_ref, f32[4,128,512]{2,1,0:T(8,128)} %copy-done.6), custom_call_target="tpu_custom_call" | custom-call | flops 1000 | bytes 1000 | tf_op jit(solution)/shard_map/pallas_call | solution.py:79
  153.9 20.9 %shard_map.74.refs_15_ = f32[1024,1024]{1,0:T(8,128)} custom-call(s32[1]{0:T(128)} %bitcast.refs_0_, f32[4,2,128,768]{3,2,1,0:T(8,128)} %copy-done, bf16[512,1024]{1,0:T(8,128)(2,1)} %get-tuple-element.31.refs_2_, bf16[512,1024]{1,0:T(8,128)(2,1)} %get-tuple-element.36.refs_3_, bf16[512,1024]{1,0:T(8,128)(2,1)} %get-tuple-element.40.refs_4_, ...), custom_call_target="tpu_custom_call" | custom-call | flops 1000 | bytes 1000 | tf_op jit(solution)/shard_map/pallas_call | solution.py:238
  175.0 11.0 %shard_map.75 = f32[1024,1024]{1,0:T(8,128)} custom-call(s32[1]{0:T(128)} %bitcast.refs_0_, f32[4,2,128,256]{3,2,1,0:T(8,128)} %all-to-all-done.1.refs_1_, bf16[512,1024]{1,0:T(8,128)(2,1)} %get-tuple-element.31.refs_2_, bf16[512,1024]{1,0:T(8,128)(2,1)} %get-tuple-element.36.refs_3_, ...), custom_call_target="tpu_custom_call", output_to_operand_aliasing={{}: (15, {})} | custom-call | flops 1000 | bytes 1000 | tf_op jit(solution)/shard_map/pallas_call | solution.py:238
  (64 shorter events, 10.4 us)
Async XLA Ops:
  0.0 38.3 %copy-start.12 = (f32[2,512]{1,0:T(2,128)S(1)}, f32[2,512]{1,0:T(2,128)}, u32[]{:S(2)}) copy-start(f32[2,512]{1,0:T(2,128)} %param.9) | copy-start | bytes 12292
  4.2 49.7 %collective-permute-start = (f32[4,128,1024]{2,1,0:T(8,128)}, f32[4,128,1024]{2,1,0:T(8,128)S(1)}, u32[]{:S(2)}, u32[]{:S(2)}) collective-permute-start(f32[4,128,1024]{2,1,0:T(8,128)} %get-tuple-element.27), channel_id=1, source_target_pairs={{0,1},{1,0},{2,3},{3,2},{4,5},{5,4},{6,7},{7,6},{8,9},{9,8},{10,11... | collective-permute-start | bytes 6291464 | tf_op jit(solution)/shard_map/ppermute | solution.py:31
  7.2 14.5 %collective-permute-start.1 = (f32[1,128,512]{2,1,0:T(8,128)}, f32[1,128,512]{2,1,0:T(8,128)S(1)}, u32[]{:S(2)}, u32[]{:S(2)}) collective-permute-start(f32[1,128,512]{2,1,0:T(8,128)} %bitcast.19), channel_id=1, source_target_pairs={{0,4},{1,5},{2,6},{3,7},{4,0},{5,1},{6,2},{7,3},{8,12},{9,13},{10,... | collective-permute-start | bytes 786440 | tf_op jit(solution)/shard_map/ppermute | solution.py:31
  21.7 0.7 copy-start.11
  21.7 14.0 %collective-permute-start.3 = (f32[1,128,512]{2,1,0:T(8,128)}, f32[1,128,512]{2,1,0:T(8,128)S(1)}, u32[]{:S(2)}, u32[]{:S(2)}) collective-permute-start(f32[1,128,512]{2,1,0:T(8,128)} %bitcast.21), channel_id=1, source_target_pairs={{0,4},{1,5},{2,6},{3,7},{4,0},{5,1},{6,2},{7,3},{8,12},{9,13},{10,... | collective-permute-start | bytes 786440 | tf_op jit(solution)/shard_map/ppermute | solution.py:31
  24.3 20.0 %collective-permute-start.2 = (f32[2,128,512]{2,1,0:T(8,128)}, f32[2,128,512]{2,1,0:T(8,128)S(1)}, u32[]{:S(2)}, u32[]{:S(2)}) collective-permute-start(f32[2,128,512]{2,1,0:T(8,128)} %shard_map.67.a_ref), channel_id=1, source_target_pairs={{0,2},{1,3},{2,0},{3,1},{4,6},{5,7},{6,4},{7,5},{8,10},{9,11},{10,... | collective-permute-start | bytes 1572872 | tf_op jit(solution)/shard_map/ppermute | solution.py:31
  38.3 20.5 %collective-permute-start.4 = (f32[2,128,512]{2,1,0:T(8,128)}, f32[2,128,512]{2,1,0:T(8,128)S(1)}, u32[]{:S(2)}, u32[]{:S(2)}) collective-permute-start(f32[2,128,512]{2,1,0:T(8,128)} %shard_map.68.a_ref), channel_id=1, source_target_pairs={{0,2},{1,3},{2,0},{3,1},{4,6},{5,7},{6,4},{7,5},{8,10},{9,11},{10,... | collective-permute-start | bytes 1572872 | tf_op jit(solution)/shard_map/ppermute | solution.py:31
  38.4 9.0 %collective-permute-start.6 = (f32[2,512]{1,0:T(2,128)S(1)}, f32[2,512]{1,0:T(2,128)S(1)}, u32[]{:S(2)}, u32[]{:S(2)}) collective-permute-start(f32[2,512]{1,0:T(2,128)S(1)} %copy-done.12), channel_id=1, source_target_pairs={{8,16},{24,0},{16,8},{0,24},{9,17},{25,1},{17,9},{1,25},{10,18},{2... | collective-permute-start | bytes 12296 | tf_op jit(solution)/shard_map/ppermute | solution.py:338
  44.3 0.8 copy-start.9
  47.3 25.8 %collective-permute-start.7 = (f32[4,128,512]{2,1,0:T(8,128)}, f32[4,128,512]{2,1,0:T(8,128)}, u32[]{:S(2)}, u32[]{:S(2)}) collective-permute-start(f32[4,128,512]{2,1,0:T(8,128)} %shard_map.69.near_ref), channel_id=1, source_target_pairs={{8,16},{24,0},{16,8},{0,24},{9,17},{25,1},{17,9},{1,25},{10,18},{2... | collective-permute-start | bytes 3145736 | tf_op jit(solution)/shard_map/ppermute | solution.py:338
  47.4 28.2 %collective-permute-start.5 = (f32[4,128,512]{2,1,0:T(8,128)}, f32[4,128,512]{2,1,0:T(8,128)}, u32[]{:S(2)}, u32[]{:S(2)}) collective-permute-start(f32[4,128,512]{2,1,0:T(8,128)} %shard_map.69.near_ref), channel_id=1, source_target_pairs={{0,1},{1,0},{2,3},{3,2},{4,5},{5,4},{6,7},{7,6},{8,9},{9,8},{10,11... | collective-permute-start | bytes 3145736 | tf_op jit(solution)/shard_map/ppermute | solution.py:31
  53.9 1.4 copy-start.1
  55.2 10.5 %copy-start.13 = (s32[1,1,2,48]{3,2,1,0:T(2,128)S(1)}, s32[1,1,2,48]{3,2,1,0:T(2,128)}, u32[]{:S(2)}) copy-start(s32[1,1,2,48]{3,2,1,0:T(2,128)} %param.10) | copy-start | bytes 1156
  58.8 0.8 copy-start.8
  59.6 84.0 %all-to-all-start = ((f32[4,2,128,768]{3,2,1,0:T(8,128)}), f32[4,2,128,768]{3,2,1,0:T(8,128)S(1)}, u32[]{:S(2)}, u32[]{:S(2)}) async-start(f32[4,2,128,768]{3,2,1,0:T(8,128)} %shard_map.66), calls=%async_computation | async-start | bytes 6291456 | tf_op jit(solution)/shard_map/all_to_all | solution.py:320
  75.6 11.9 %collective-permute-start.8 = (f32[4,128,512]{2,1,0:T(8,128)}, f32[4,128,512]{2,1,0:T(8,128)}, u32[]{:S(2)}, u32[]{:S(2)}) collective-permute-start(f32[4,128,512]{2,1,0:T(8,128)} %shard_map.69.near_ref), channel_id=1, source_target_pairs={{0,8},{8,0},{16,24},{24,16},{1,9},{9,1},{17,25},{25,17},{2,10},{10... | collective-permute-start | bytes 3145736 | tf_op jit(solution)/shard_map/ppermute | solution.py:341
  75.9 2.4 %collective-permute-start.10 = (f32[2,512]{1,0:T(2,128)S(1)}, f32[2,512]{1,0:T(2,128)S(1)}, u32[]{:S(2)}, u32[]{:S(2)}) collective-permute-start(f32[2,512]{1,0:T(2,128)S(1)} %copy-done.12), channel_id=1, source_target_pairs={{0,8},{8,0},{16,24},{24,16},{1,9},{9,1},{17,25},{25,17},{2,10},{10... | collective-permute-start | bytes 12296 | tf_op jit(solution)/shard_map/ppermute | solution.py:341
  87.5 25.5 %collective-permute-start.12 = (f32[4,128,512]{2,1,0:T(8,128)}, f32[4,128,512]{2,1,0:T(8,128)S(1)}, u32[]{:S(2)}, u32[]{:S(2)}) collective-permute-start(f32[4,128,512]{2,1,0:T(8,128)} %shard_map.72.refs_8_), channel_id=1, source_target_pairs={{0,1},{1,0},{2,3},{3,2},{4,5},{5,4},{6,7},{7,6},{8,9},{9,8},{10,11... | collective-permute-start | bytes 3145736 | tf_op jit(solution)/shard_map/ppermute | solution.py:31
  89.3 25.6 %collective-permute-start.11 = (f32[4,128,512]{2,1,0:T(8,128)}, f32[4,128,512]{2,1,0:T(8,128)S(1)}, u32[]{:S(2)}, u32[]{:S(2)}) collective-permute-start(f32[4,128,512]{2,1,0:T(8,128)} %shard_map.72.refs_8_), channel_id=1, source_target_pairs={{8,16},{24,0},{16,8},{0,24},{9,17},{25,1},{17,9},{1,25},{10,18},{2... | collective-permute-start | bytes 3145736 | tf_op jit(solution)/shard_map/ppermute | solution.py:338
  90.3 24.6 %collective-permute-start.9 = (f32[4,128,512]{2,1,0:T(8,128)}, f32[4,128,512]{2,1,0:T(8,128)S(1)}, u32[]{:S(2)}, u32[]{:S(2)}) collective-permute-start(f32[4,128,512]{2,1,0:T(8,128)} %collective-permute-done.5.far_ref), channel_id=1, source_target_pairs={{0,8},{8,0},{16,24},{24,16},{1,9},{9,1},{17,25},{25,17},{2,10},{10... | collective-permute-start | bytes 3145736 | tf_op jit(solution)/shard_map/ppermute | solution.py:341
  113.0 29.7 %copy-start.2 = (f32[4,128,512]{2,1,0:T(8,128)}, f32[4,128,512]{2,1,0:T(8,128)S(1)}, u32[]{:S(2)}) copy-start(f32[4,128,512]{2,1,0:T(8,128)S(1)} %collective-permute-done.12.refs_9_) | copy-start | bytes 3145732
  114.9 27.8 %copy-start.3 = (f32[4,128,512]{2,1,0:T(8,128)}, f32[4,128,512]{2,1,0:T(8,128)S(1)}, u32[]{:S(2)}) copy-start(f32[4,128,512]{2,1,0:T(8,128)S(1)} %collective-permute-done.11.refs_12_) | copy-start | bytes 3145732
  114.9 1.0 copy-start.7
  115.9 25.4 %collective-permute-start.13 = (f32[4,128,512]{2,1,0:T(8,128)}, f32[4,128,512]{2,1,0:T(8,128)S(1)}, u32[]{:S(2)}, u32[]{:S(2)}) collective-permute-start(f32[4,128,512]{2,1,0:T(8,128)} %collective-permute-done.5.far_ref), channel_id=1, source_target_pairs={{8,16},{24,0},{16,8},{0,24},{9,17},{25,1},{17,9},{1,25},{10,18},{2... | collective-permute-start | bytes 3145736 | tf_op jit(solution)/shard_map/ppermute | solution.py:338
  117.2 25.5 %collective-permute-start.14 = (f32[4,128,512]{2,1,0:T(8,128)S(1)}, f32[4,128,512]{2,1,0:T(8,128)S(1)}, u32[]{:S(2)}, u32[]{:S(2)}) collective-permute-start(f32[4,128,512]{2,1,0:T(8,128)S(1)} %collective-permute-done.11.refs_12_), channel_id=1, source_target_pairs={{0,1},{1,0},{2,3},{3,2},{4,5},{5,4},{6,7},{7,6},{8,9},{9,8},{10,11... | collective-permute-start | bytes 3145736 | tf_op jit(solution)/shard_map/ppermute | solution.py:31
  141.3 1.4 copy-start.6
  142.6 1.0 copy-start.4
  143.6 4.9 %collective-permute-start.15 = (f32[4,128,512]{2,1,0:T(8,128)}, f32[4,128,512]{2,1,0:T(8,128)}, u32[]{:S(2)}, u32[]{:S(2)}) collective-permute-start(f32[4,128,512]{2,1,0:T(8,128)} %shard_map.72.refs_8_), channel_id=1, source_target_pairs={{0,8},{8,0},{16,24},{24,16},{1,9},{9,1},{17,25},{25,17},{2,10},{10... | collective-permute-start | bytes 3145736 | tf_op jit(solution)/shard_map/ppermute | solution.py:341
  143.6 9.3 %copy-start = (f32[4,2,128,768]{3,2,1,0:T(8,128)}, f32[4,2,128,768]{3,2,1,0:T(8,128)S(1)}, u32[]{:S(2)}) copy-start(f32[4,2,128,768]{3,2,1,0:T(8,128)S(1)} %all-to-all-done.refs_1_) | copy-start | bytes 9437188
  143.6 31.4 %all-to-all-start.1 = ((f32[4,2,128,256]{3,2,1,0:T(8,128)}), f32[4,2,128,256]{3,2,1,0:T(8,128)}, u32[]{:S(2)}, u32[]{:S(2)}) async-start(f32[4,2,128,256]{3,2,1,0:T(8,128)} %shard_map.65), calls=%async_computation.1 | async-start | bytes 2097152 | tf_op jit(solution)/shard_map/all_to_all | solution.py:320
  148.5 4.4 %collective-permute-start.16 = (f32[4,128,512]{2,1,0:T(8,128)}, f32[4,128,512]{2,1,0:T(8,128)S(1)}, u32[]{:S(2)}, u32[]{:S(2)}) collective-permute-start(f32[4,128,512]{2,1,0:T(8,128)} %copy-done.2), channel_id=1, source_target_pairs={{0,8},{8,0},{16,24},{24,16},{1,9},{9,1},{17,25},{25,17},{2,10},{10... | collective-permute-start | bytes 3145736 | tf_op jit(solution)/shard_map/ppermute | solution.py:341
  152.9 1.0 copy-start.5
  (1 other events, 0.7 us)

commit v3 on v2

--- a/solution.py
+++ b/solution.py
@@ -35,28 +35,27 @@
     return lax.optimization_barrier((x, *deps))[0] if deps else x
 
 
-def join_kernel(a_ref, b_ref, out_ref, sems):
-    size = a_ref.shape[0]
-    copies = [
-        pltpu.make_async_copy(a_ref, out_ref.at[pl.ds(0, size)], sems.at[0]),
-        pltpu.make_async_copy(b_ref, out_ref.at[pl.ds(size, size)], sems.at[1]),
-    ]
-    for copy in copies:
-        copy.start()
-    for copy in copies:
-        copy.wait()
-
-
-def join(a, b):
+def join_kernel(*refs):
+    out_ref, sem = refs[-2:]
+    at = 0
+    for ref in refs[:-2]:
+        size = ref.shape[0]
+        pltpu.make_async_copy(ref, out_ref.at[pl.ds(at, size)], sem).start()
+        at += size
+    pltpu.make_async_copy(out_ref, out_ref, sem).wait()
+
+
+def join(*blocks):
+    count = sum(block.shape[0] for block in blocks)
     return pl.pallas_call(
         join_kernel,
-        out_shape=jax.ShapeDtypeStruct((2 * a.shape[0], *a.shape[1:]), a.dtype),
-        in_specs=[anywhere] * 2,
+        out_shape=jax.ShapeDtypeStruct((count, *blocks[0].shape[1:]), f32),
+        in_specs=[anywhere] * len(blocks),
         out_specs=in_vmem,
-        scratch_shapes=[pltpu.SemaphoreType.DMA((2,))],
-        compiler_params=pltpu.CompilerParams(vmem_limit_bytes=vmem_limit),
-        cost_estimate=small_cost,
-    )(a, b)
+        scratch_shapes=[pltpu.SemaphoreType.DMA],
+        compiler_params=pltpu.CompilerParams(vmem_limit_bytes=vmem_limit),
+        cost_estimate=small_cost,
+    )(*blocks)
 
 
 def prep_obs_kernel(order, near_ref, far_ref, high_ref, low_ref):
@@ -75,13 +74,14 @@
 
 def prep_obs(pair, order):
     blocks, rows, width = pair[0].shape
-    whole = pl.BlockSpec((blocks, rows, 128), lambda j: (0, 0, j))
+    band = 256 if width % 256 == 0 else 128
+    whole = pl.BlockSpec((blocks, rows, band), lambda j: (0, 0, j))
     return pl.pallas_call(
         functools.partial(prep_obs_kernel, order),
-        grid=(width // 128,),
+        grid=(width // band,),
         out_shape=[jax.ShapeDtypeStruct((width, 2 * blocks * rows), bf16)] * 2,
         in_specs=[whole] * 2,
-        out_specs=[pl.BlockSpec((128, 2 * blocks * rows), lambda j: (j, 0))] * 2,
+        out_specs=[pl.BlockSpec((band, 2 * blocks * rows), lambda j: (j, 0))] * 2,
         compiler_params=pltpu.CompilerParams(vmem_limit_bytes=vmem_limit),
         cost_estimate=small_cost,
     )(*pair)
@@ -104,12 +104,11 @@
     window = tap.shape[0]
     slot_obs = window // 3
     band = min(512, members)
-    x_copies = [
-        pltpu.make_async_copy(
-            points.at[lax.div(me ^ r, 2), r % 2], total.at[pl.ds(r * ml, ml)], sem_x
-        )
-        for r in range(local)
-    ]
+    x_copies = []
+    for r in range(local):
+        paired = len(points.shape) == 4
+        block = points.at[lax.div(me ^ r, 2), r % 2] if paired else points.at[me ^ r]
+        x_copies.append(pltpu.make_async_copy(block, total.at[pl.ds(r * ml, ml)], sem_x))
     y_copies = []
     for i, (slot, at, size) in enumerate(parts):
         here = pl.ds(at, size)
@@ -178,59 +177,84 @@
         ).wait()
 
 
-def regroup_kernel(begin, side_ref, state_ref, keep_ref, give_ref, sem):
-    blocks, ml, width = keep_ref.shape
-    per_device = state_ref.shape[1] // (2 * blocks)
-    side = side_ref[0]
+def side_copies(side, state_ref, begin, out_refs, sem):
+    width = out_refs[0].shape[1]
+    per_device = state_ref.shape[1] // (2 * len(out_refs))
     copies = []
-    for ref, which in ((give_ref, 1 - side), (keep_ref, side)):
-        for z in range(blocks):
-            at = pl.multiple_of((2 * z + which) * per_device + begin, 128)
-            copies.append(pltpu.make_async_copy(state_ref.at[:, pl.ds(at, width)], ref.at[z], sem))
-    for copy in copies:
+    for z, out_ref in enumerate(out_refs):
+        at = pl.multiple_of((2 * z + side) * per_device + begin, 128)
+        copies.append(pltpu.make_async_copy(state_ref.at[:, pl.ds(at, width)], out_ref, sem))
+    return copies
+
+
+def given_kernel(begin, side_ref, state_ref, out_ref, sem):
+    refs = [out_ref.at[z] for z in range(out_ref.shape[0])]
+    for copy in side_copies(1 - side_ref[0], state_ref, begin, refs, sem):
         copy.start()
-    pltpu.make_async_copy(keep_ref, keep_ref, sem).wait()
-    pltpu.make_async_copy(give_ref, give_ref, sem).wait()
-
-
-def regroup(side, state, groups, begin, width):
-    shape = jax.ShapeDtypeStruct((groups // 2, state.shape[0], width), f32)
+    pltpu.make_async_copy(out_ref, out_ref, sem).wait()
+
+
+def given(side, state, groups, begin, width):
+    return pl.pallas_call(
+        functools.partial(given_kernel, begin),
+        out_shape=jax.ShapeDtypeStruct((groups // 2, state.shape[0], width), f32),
+        in_specs=[pl.BlockSpec(memory_space=pltpu.SMEM), anywhere],
+        out_specs=in_vmem,
+        scratch_shapes=[pltpu.SemaphoreType.DMA],
+        compiler_params=pltpu.CompilerParams(vmem_limit_bytes=vmem_limit),
+        cost_estimate=small_cost,
+    )(side, state)
+
+
+def regroup_kernel(begin, state_ref, out_ref, sem):
+    groups, ml, width = out_ref.shape
+    per_device = state_ref.shape[1] // groups
+    for g in range(groups):
+        here = pl.ds(g * per_device + begin, width)
+        pltpu.make_async_copy(state_ref.at[:, here], out_ref.at[g], sem).start()
+    pltpu.make_async_copy(out_ref, out_ref, sem).wait()
+
+
+def regroup(state, groups, begin, width):
     return pl.pallas_call(
         functools.partial(regroup_kernel, begin),
-        out_shape=[shape] * 2,
-        in_specs=[pl.BlockSpec(memory_space=pltpu.SMEM), anywhere],
-        out_specs=[in_vmem] * 2,
+        out_shape=jax.ShapeDtypeStruct((groups, state.shape[0], width), f32),
+        in_specs=[anywhere],
+        out_specs=in_vmem,
         scratch_shapes=[pltpu.SemaphoreType.DMA],
         compiler_params=pltpu.CompilerParams(vmem_limit_bytes=vmem_limit),
         cost_estimate=small_cost,
-    )(side, state)
-
-
-def pair_kernel(begin, a_ref, b_ref, out_ref, sem):
-    here = pl.ds(begin, out_ref.shape[3])
-    copies = []
-    for z in range(a_ref.shape[0]):
-        copies.append(pltpu.make_async_copy(a_ref.at[z, :, here], out_ref.at[z, 0], sem))
-        copies.append(pltpu.make_async_copy(b_ref.at[z, :, here], out_ref.at[z, 1], sem))
+    )(state)
+
+
+def pair_kernel(begin, side_ref, state_ref, got_ref, out_ref, sem):
+    blocks = out_ref.shape[0]
+    copies = side_copies(
+        side_ref[0], state_ref, begin, [out_ref.at[z, 0] for z in range(blocks)], sem
+    )
+    for z in range(blocks):
+        copies.append(pltpu.make_async_copy(got_ref.at[z], out_ref.at[z, 1], sem))
     for copy in copies:
         copy.start()
     pltpu.make_async_copy(out_ref, out_ref, sem).wait()
 
 
-def pair(a, b, begin, width):
+def pair(side, state, got, begin):
+    blocks, ml, width = got.shape
     return pl.pallas_call(
         functools.partial(pair_kernel, begin),
-        out_shape=jax.ShapeDtypeStruct((a.shape[0], 2, a.shape[1], width), f32),
-        in_specs=[anywhere] * 2,
+        out_shape=jax.ShapeDtypeStruct((blocks, 2, ml, width), f32),
+        in_specs=[pl.BlockSpec(memory_space=pltpu.SMEM), anywhere, anywhere],
         out_specs=in_vmem,
         scratch_shapes=[pltpu.SemaphoreType.DMA],
         compiler_params=pltpu.CompilerParams(vmem_limit_bytes=vmem_limit),
         cost_estimate=small_cost,
-    )(a, b)
+    )(side, state, got)
 
 
 def update(me, points, obs, parts, innov, order, taper, out, start, per_device):
-    members, width = 2 * points.shape[0] * points.shape[2], points.shape[3]
+    width = points.shape[-1]
+    members = points.size // width
     window_obs = taper.shape[0]
     first = out is None
     operands = [me, points, *[o[0] for o in obs], *[o[1] for o in obs], *innov, taper]
@@ -314,25 +338,27 @@
     sides = [[i for i in range(groups) if i % 2 == s] for s in range(2)]
     my_side = (me % 2).astype(jnp.int32).reshape(1)
 
-    keep, give = regroup(my_side, state, groups, 0, per_device)
-
-    def assembled(halves, *deps):
+    def exchanged(span, *deps):
+        return side(given(my_side, after(state, *deps), groups, *span))
+
+    def assembled(blocks, within, *deps):
         return lax.all_to_all(
-            after(halves, *deps),
+            after(blocks, *deps),
             "mem",
             split_axis=0,
             concat_axis=0,
             tiled=True,
-            axis_index_groups=sides,
+            axis_index_groups=within,
         )
 
     def far_gathered(x, *deps):
-        x, got = x[None], []
-        for b in bits[:-1]:
-            got.append(swap(after(x, *deps), "mem", b))
-            x = join(x, got[-1])
-            deps = ()
-        return x, got
+        own, others, got = after(x[None], *deps), [], []
+        early = swap(own, "mem", bits[-2])
+        for b in bits[:-2]:
+            got.append(swap(join(own, *others) if others else own, "mem", b))
+            others.append(got[-1])
+        got.append(swap(join(*others) if len(others) > 1 else others[0], "mem", bits[-2]))
+        return join(own, *others, early, got[-1]), got
 
     def cross(x, *deps):
         return lax.ppermute(after(x, *deps), "dom", across)
@@ -343,27 +369,29 @@
     def side(x, *deps):
         return swap(after(x, *deps), "mem", 1)
 
-    got = side(give)
     obs_near, obs_got = far_gathered(obs_ensemble)
+    first = exchanged(spans[0])
     inn_near, inn_got = far_gathered(innovations, obs_got[0])
     coord_beside = beside(obs_coords, obs_got[0])
     coord_beyond = cross(obs_coords, obs_got[0])
     taper = tapered(coord_beside, coord_beyond)
-    obs_near_beyond = cross(obs_near, coord_beyond)
+    obs_near_beyond = cross(obs_near, coord_beyond, coord_beside)
     obs_far = side(obs_near)
-    paired = [pair(keep, got, *span) for span in spans]
-    points = [assembled(paired[0], obs_got[-1], inn_got[-1])]
-    obs_near_beside = beside(obs_near, obs_near_beyond, obs_far)
-    inn_near_beyond = cross(inn_near, obs_near_beside, taper, paired[1])
-    inn_far = side(inn_near, obs_near_beside)
-    obs_far_beside = beside(obs_far, obs_near_beside)
+    paired = pair(my_side, state, first, spans[0][0])
+    points = [assembled(paired, sides, obs_got[-1], inn_got[-1])]
+    obs_near_beside = beside(obs_near, obs_near_beyond, obs_far, taper, inn_near)
+    pause = beside(obs_far, obs_near_beside)
+    inn_near_beyond = cross(inn_near, pause)
+    inn_far = side(inn_near, pause)
+    obs_far_beside = pause
     ready_own = prep_obs((obs_near, obs_far), order)
     ready_beside = prep_obs((obs_near_beside, obs_far_beside), order)
-    obs_far_beyond = cross(obs_far, inn_near_beyond, inn_far, obs_far_beside, ready_own[0])
+    blocks = regroup(after(state, obs_got[-1]), groups, *spans[1])
+    obs_far_beyond = cross(obs_far, inn_near_beyond, inn_far, obs_far_beside, ready_own[0], blocks)
     inn_far_beyond = side(inn_near_beyond, inn_far)
     inn_near_beside = beside(inn_near, obs_far_beyond, inn_far_beyond, ready_beside[0])
     inn_far_beside = beside(inn_far, inn_near_beside)
-    points.append(assembled(paired[1], points[0]))
+    points.append(assembled(blocks, None, points[0]))
     ready_beyond = prep_obs((obs_near_beyond, obs_far_beyond), order)
     obs = [ready_own, ready_beside, ready_beyond]
     innov = [inn_near, inn_far, inn_near_beside, inn_far_beside, inn_near_beyond, inn_far_beyond]

time: 187 us -> 169 us (0.904)
  Pallas kernels: 62.6 us -> 53.6 us
  waiting for transfers between devices: 83.9 us -> 75.4 us
  starting transfers between devices: 26 us -> 28.5 us
  local copies, waits for them, and re-layouts: 7.59 us -> 5.53 us
    ppermute x8 -> x10, waiting for transfers between devices: 53.5 us -> 46.4 us  [swap(): return lax.ppermute(x, axis, [(i, i ^ distance) for i in range(size)])]
    ppermute x4, waiting for transfers between devices: 28.5 us -> 22.3 us  [cross(): return lax.ppermute(after(x, *deps), 'dom', across)]
    ppermute x8 -> x10, starting transfers between devices: 12 us -> 16.1 us  [swap(): return lax.ppermute(x, axis, [(i, i ^ distance) for i in range(size)])]
    ppermute x5, waiting for transfers between devices: 1.73 us -> 5.4 us  [beside(): return lax.ppermute(after(x, *deps), 'dom', chip)]
    pallas_call x3, Pallas kernels: 12.6 us -> 9.08 us  [prep_obs(): pl.pallas_call(functools.partial(prep_obs_kernel, order), grid=(width //...]
    pallas_call x5 -> x4, Pallas kernels: 12.3 us -> 9.2 us  [the longest x2 4.44 us: join(): pl.pallas_call(join_kernel, out_shape=jax.ShapeDtypeStruct((count, *block...]
    unnamed x32 -> x38, local copies, waits for them, and re-layouts: 7.4 us -> 4.58 us
    all_to_all x2, starting transfers between devices: 10.3 us -> 7.95 us  [assembled(): lax.all_to_all(after(blocks, *deps), 'mem', split_axis=0, concat_axis=0,...]
  transfers between devices with their start and end apart: 19 -> 21, of which waited for: 12 -> 12; matrix products, arithmetic and copies ran while one was open for 3% -> 4% of each run, Pallas kernels for 25% -> 25%
where the time goes in v3:
time: 169 us
  waiting for transfers between devices  75.4 us (45%)
  Pallas kernels  53.6 us (32%)
  starting transfers between devices  28.5 us (17%)
  local copies, waits for them, and re-layouts  5.53 us (3%)
  other arithmetic  4.94 us (3%)
    ppermute x10, waiting for transfers between devices, swap(): return lax.ppermute(x, axis, [(i, i ^ distance) for i in range(size)])  46.4 us
    pallas_call x2, Pallas kernels, update(): pl.pallas_call(functools.partial(update_kernel, parts, order, first, star...  31.9 us
    ppermute x4, waiting for transfers between devices, cross(): return lax.ppermute(after(x, *deps), 'dom', across)  22.3 us
    ppermute x10, starting transfers between devices, swap(): return lax.ppermute(x, axis, [(i, i ^ distance) for i in range(size)])  16.1 us
    pallas_call x3, Pallas kernels, prep_obs(): pl.pallas_call(functools.partial(prep_obs_kernel, order), grid=(width //...  9.08 us
    all_to_all x2, starting transfers between devices, assembled(): lax.all_to_all(after(blocks, *deps), 'mem', split_axis=0, concat_axis=0,...  7.95 us
    ppermute x5, waiting for transfers between devices, beside(): return lax.ppermute(after(x, *deps), 'dom', chip)  5.4 us
    mul x1, other arithmetic, tapered(): taper.reshape(-1, tile_side, per_device) * mask[:, None, :]  4.6 us
  transfers between devices with their start and end apart: 21, of which 12 were waited for; matrix products, arithmetic and copies ran while one was open for 4% of the time, Pallas kernels for 25%

profile of v3, /device:TPU:0, one launch (start us, length us, event | category | flops | bytes accessed | tf_op | source)
XLA Modules:
  0.0 168.9 jit_solution(4527072677752278931)
XLA Ops:
  0.0 3.0 %collective-permute-start.5 = (f32[1,128,512]{2,1,0:T(8,128)}, f32[1,128,512]{2,1,0:T(8,128)S(1)}, u32[]{:S(2)}, u32[]{:S(2)}) collective-permute-start(f32[1,128,512]{2,1,0:T(8,128)} %bitcast.19), channel_id=1, source_target_pairs={{0,2},{1,3},{2,0},{3,1},{4,6},{5,7},{6,4},{7,5},{8,10},{9,11},{10,... | collective-permute-start | bytes 786440 | tf_op jit(solution)/shard_map/ppermute | solution.py:31
  3.0 2.6 %collective-permute-start = (f32[1,128,512]{2,1,0:T(8,128)}, f32[1,128,512]{2,1,0:T(8,128)S(1)}, u32[]{:S(2)}, u32[]{:S(2)}) collective-permute-start(f32[1,128,512]{2,1,0:T(8,128)} %bitcast.20), channel_id=1, source_target_pairs={{0,4},{1,5},{2,6},{3,7},{4,0},{5,1},{6,2},{7,3},{8,12},{9,13},{10,... | collective-permute-start | bytes 786440 | tf_op jit(solution)/shard_map/ppermute | solution.py:31
  5.6 2.5 %shard_map.65 = f32[4,128,768]{2,1,0:T(8,128)} custom-call(s32[1]{0:T(128)} %bitcast.2.side_ref, f32[128,8192]{1,0:T(8,128)} %state_ref.4), custom_call_target="tpu_custom_call" | custom-call | flops 1000 | bytes 1000 | tf_op jit(solution)/shard_map/pallas_call | solution.py:198
  8.1 1.6 collective-permute-start.2
  11.3 6.3 %collective-permute-done.refs_1_ = f32[1,128,512]{2,1,0:T(8,128)S(1)} collective-permute-done((f32[1,128,512]{2,1,0:T(8,128)}, f32[1,128,512]{2,1,0:T(8,128)S(1)}, u32[]{:S(2)}, u32[]{:S(2)}) %collective-permute-start) | collective-permute-done | bytes 262176 | tf_op jit(solution)/shard_map/ppermute | solution.py:31
  18.1 1.6 collective-permute-start.7
  19.8 2.7 %collective-permute-start.3 = (f32[1,128,512]{2,1,0:T(8,128)}, f32[1,128,512]{2,1,0:T(8,128)S(1)}, u32[]{:S(2)}, u32[]{:S(2)}) collective-permute-start(f32[1,128,512]{2,1,0:T(8,128)} %bitcast.22), channel_id=1, source_target_pairs={{0,4},{1,5},{2,6},{3,7},{4,0},{5,1},{6,2},{7,3},{8,12},{9,13},{10,... | collective-permute-start | bytes 786440 | tf_op jit(solution)/shard_map/ppermute | solution.py:31
  22.5 2.5 %collective-permute-done.1.refs_3_ = f32[1,128,512]{2,1,0:T(8,128)S(1)} collective-permute-done((f32[1,128,512]{2,1,0:T(8,128)S(1)}, f32[1,128,512]{2,1,0:T(8,128)S(1)}, u32[]{:S(2)}, u32[]{:S(2)}) %collective-permute-start.1) | collective-permute-done | bytes 262176 | tf_op jit(solution)/shard_map/ppermute | solution.py:31
  25.7 2.3 %shard_map.67.near_ref = f32[4,128,512]{2,1,0:T(8,128)} custom-call(f32[1,128,512]{2,1,0:T(8,128)} %bitcast.21, f32[1,128,512]{2,1,0:T(8,128)} %copy-done.12, f32[1,128,512]{2,1,0:T(8,128)} %copy-done.11, f32[1,128,512]{2,1,0:T(8,128)} %copy-done.15), custom_call_target="tpu_custom_call" | custom-call | flops 1000 | bytes 1000 | tf_op jit(solution)/shard_map/pallas_call | solution.py:50
  28.0 1.6 collective-permute-start.6
  29.7 5.2 %collective-permute-done.3.refs_1_ = f32[1,128,512]{2,1,0:T(8,128)S(1)} collective-permute-done((f32[1,128,512]{2,1,0:T(8,128)}, f32[1,128,512]{2,1,0:T(8,128)S(1)}, u32[]{:S(2)}, u32[]{:S(2)}) %collective-permute-start.3) | collective-permute-done | bytes 262176 | tf_op jit(solution)/shard_map/ppermute | solution.py:31
  35.1 2.1 %collective-permute-start.10 = (f32[1,128,512]{2,1,0:T(8,128)S(1)}, f32[1,128,512]{2,1,0:T(8,128)}, u32[]{:S(2)}, u32[]{:S(2)}) collective-permute-start(f32[1,128,512]{2,1,0:T(8,128)S(1)} %bitcast.24), channel_id=1, source_target_pairs={{0,2},{1,3},{2,0},{3,1},{4,6},{5,7},{6,4},{7,5},{8,10},{9,11},{10,... | collective-permute-start | bytes 786440 | tf_op jit(solution)/shard_map/ppermute | solution.py:31
  37.2 8.5 %collective-permute-done.2.got_ref = f32[4,128,768]{2,1,0:T(8,128)S(1)} collective-permute-done((f32[4,128,768]{2,1,0:T(8,128)}, f32[4,128,768]{2,1,0:T(8,128)S(1)}, u32[]{:S(2)}, u32[]{:S(2)}) %collective-permute-start.2) | collective-permute-done | bytes 1572896 | tf_op jit(solution)/shard_map/ppermute | solution.py:31
  46.9 3.5 %shard_map.66 = f32[4,2,128,768]{3,2,1,0:T(8,128)} custom-call(s32[1]{0:T(128)} %bitcast.2.side_ref, f32[128,8192]{1,0:T(8,128)} %state_ref.4, f32[4,128,768]{2,1,0:T(8,128)} %copy-done.6), custom_call_target="tpu_custom_call" | custom-call | flops 1000 | bytes 1000 | tf_op jit(solution)/shard_map/pallas_call | solution.py:244
  51.1 3.7 %all-to-all-start = ((f32[4,2,128,768]{3,2,1,0:T(8,128)}), f32[4,2,128,768]{3,2,1,0:T(8,128)S(1)}, u32[]{:S(2)}, u32[]{:S(2)}) async-start(f32[4,2,128,768]{3,2,1,0:T(8,128)} %shard_map.66), calls=%async_computation | async-start | bytes 6291456 | tf_op jit(solution)/shard_map/all_to_all | solution.py:345
  54.9 4.6 %fusion.5.refs_14_ = f32[1536,1024]{1,0:T(8,128)} fusion(f32[12,1024]{1,0:T(8,128)S(1)} %bitcast.17, f32[1536]{0:T(1024)S(1)} %get-tuple-element.44, f32[1024]{0:T(1024)S(1)} %get-tuple-element.48, f32[1536]{0:T(1024)S(1)} %get-tuple-element.43, f32[1024]{0:T(1024)S(1)} %get-tuple-element.47), kind=kLoop, calls=%fused_computation.6 | loop fusion | flops 17301504 | bytes 6361088 | tf_op jit(solution)/shard_map/mul | solution.py:333
  59.5 2.2 %shard_map.69.refs_8_ = f32[4,128,512]{2,1,0:T(8,128)} custom-call(f32[1,128,512]{2,1,0:T(8,128)} %bitcast.23, f32[1,128,512]{2,1,0:T(8,128)} %copy-done.13, f32[1,128,512]{2,1,0:T(8,128)} %collective-permute-done.10.refs_2_, f32[1,128,512]{2,1,0:T(8,128)} %copy-done.14), custom_call_target="tpu_custom_call" | custom-call | flops 1000 | bytes 1000 | tf_op jit(solution)/shard_map/pallas_call | solution.py:50
  61.7 4.8 %collective-permute-done.6.far_ref = f32[4,128,512]{2,1,0:T(8,128)} collective-permute-done((f32[4,128,512]{2,1,0:T(8,128)}, f32[4,128,512]{2,1,0:T(8,128)}, u32[]{:S(2)}, u32[]{:S(2)}) %collective-permute-start.6) | collective-permute-done | bytes 1048608 | tf_op jit(solution)/shard_map/ppermute | solution.py:31
  66.6 2.7 %collective-permute-done.11.near_ref = f32[4,128,512]{2,1,0:T(8,128)S(1)} collective-permute-done((f32[4,128,512]{2,1,0:T(8,128)S(1)}, f32[4,128,512]{2,1,0:T(8,128)S(1)}, u32[]{:S(2)}, u32[]{:S(2)}) %collective-permute-start.11) | collective-permute-done | bytes 1048608 | tf_op jit(solution)/shard_map/ppermute | solution.py:367
  69.4 2.7 %collective-permute-done.12.far_ref = f32[4,128,512]{2,1,0:T(8,128)S(1)} collective-permute-done((f32[4,128,512]{2,1,0:T(8,128)}, f32[4,128,512]{2,1,0:T(8,128)S(1)}, u32[]{:S(2)}, u32[]{:S(2)}) %collective-permute-start.12) | collective-permute-done | bytes 1048608 | tf_op jit(solution)/shard_map/ppermute | solution.py:367
  72.1 1.5 collective-permute-start.14
  74.6 2.3 %shard_map.64 = f32[8,128,256]{2,1,0:T(8,128)} custom-call(f32[128,8192]{1,0:T(8,128)} %state_ref.4), custom_call_target="tpu_custom_call" | custom-call | flops 1000 | bytes 1000 | tf_op jit(solution)/shard_map/pallas_call | solution.py:219
  76.8 3.0 %shard_map.68 = (bf16[512,1024]{1,0:T(8,128)(2,1)}, bf16[512,1024]{1,0:T(8,128)(2,1)}) custom-call(f32[4,128,512]{2,1,0:T(8,128)} %shard_map.67.near_ref, f32[4,128,512]{2,1,0:T(8,128)} %collective-permute-done.6.far_ref), custom_call_target="tpu_custom_call" | custom-call | flops 1000 | bytes 1000 | tf_op jit(solution)/shard_map/pallas_call | solution.py:79
  79.9 17.6 %collective-permute-done.14.refs_9_ = f32[4,128,512]{2,1,0:T(8,128)S(1)} collective-permute-done((f32[4,128,512]{2,1,0:T(8,128)}, f32[4,128,512]{2,1,0:T(8,128)S(1)}, u32[]{:S(2)}, u32[]{:S(2)}) %collective-permute-start.14) | collective-permute-done | bytes 1048608 | tf_op jit(solution)/shard_map/ppermute | solution.py:31
  97.5 1.7 %collective-permute-done.13.refs_12_ = f32[4,128,512]{2,1,0:T(8,128)S(1)} collective-permute-done((f32[4,128,512]{2,1,0:T(8,128)}, f32[4,128,512]{2,1,0:T(8,128)S(1)}, u32[]{:S(2)}, u32[]{:S(2)}) %collective-permute-start.13) | collective-permute-done | bytes 1048608 | tf_op jit(solution)/shard_map/ppermute | solution.py:364
  101.0 3.0 %shard_map.70 = (bf16[512,1024]{1,0:T(8,128)(2,1)}, bf16[512,1024]{1,0:T(8,128)(2,1)}) custom-call(f32[4,128,512]{2,1,0:T(8,128)} %copy-done.8, f32[4,128,512]{2,1,0:T(8,128)} %copy-done.9), custom_call_target="tpu_custom_call" | custom-call | flops 1000 | bytes 1000 | tf_op jit(solution)/shard_map/pallas_call | solution.py:79
  104.0 20.6 %collective-permute-done.15.far_ref = f32[4,128,512]{2,1,0:T(8,128)S(1)} collective-permute-done((f32[4,128,512]{2,1,0:T(8,128)}, f32[4,128,512]{2,1,0:T(8,128)S(1)}, u32[]{:S(2)}, u32[]{:S(2)}) %collective-permute-start.15) | collective-permute-done | bytes 1048608 | tf_op jit(solution)/shard_map/ppermute | solution.py:364
  124.6 1.4 collective-permute-done.16.refs_13_
  127.0 4.2 %all-to-all-start.1 = ((f32[8,128,256]{2,1,0:T(8,128)}), f32[8,128,256]{2,1,0:T(8,128)}, u32[]{:S(2)}, u32[]{:S(2)}) async-start(f32[8,128,256]{2,1,0:T(8,128)} %shard_map.64), calls=%async_computation.1 | async-start | bytes 2097152 | tf_op jit(solution)/shard_map/all_to_all | solution.py:345
  131.8 3.0 %shard_map.71 = (bf16[512,1024]{1,0:T(8,128)(2,1)}, bf16[512,1024]{1,0:T(8,128)(2,1)}) custom-call(f32[4,128,512]{2,1,0:T(8,128)} %collective-permute-done.9.near_ref, f32[4,128,512]{2,1,0:T(8,128)} %copy-done.7), custom_call_target="tpu_custom_call" | custom-call | flops 1000 | bytes 1000 | tf_op jit(solution)/shard_map/pallas_call | solution.py:79
  135.8 20.9 %shard_map.72.refs_15_ = f32[1024,1024]{1,0:T(8,128)} custom-call(s32[1]{0:T(128)} %bitcast.refs_0_, f32[4,2,128,768]{3,2,1,0:T(8,128)} %copy-done, bf16[512,1024]{1,0:T(8,128)(2,1)} %get-tuple-element.28.refs_2_, bf16[512,1024]{1,0:T(8,128)(2,1)} %get-tuple-element.33.refs_3_, bf16[512,1024]{1,0:T(8,128)(2,1)} %get-tuple-element.36.refs_4_, ...), custom_call_target="tpu_custom_call" | custom-call | flops 1000 | bytes 1000 | tf_op jit(solution)/shard_map/pallas_call | solution.py:262
  157.9 11.0 %shard_map.73 = f32[1024,1024]{1,0:T(8,128)} custom-call(s32[1]{0:T(128)} %bitcast.refs_0_, f32[8,128,256]{2,1,0:T(8,128)} %all-to-all-done.1.refs_1_, bf16[512,1024]{1,0:T(8,128)(2,1)} %get-tuple-element.28.refs_2_, bf16[512,1024]{1,0:T(8,128)(2,1)} %get-tuple-element.33.refs_3_, ...), custom_call_target="tpu_custom_call", output_to_operand_aliasing={{}: (15, {})} | custom-call | flops 1000 | bytes 1000 | tf_op jit(solution)/shard_map/pallas_call | solution.py:262
  (72 shorter events, 11.0 us)
Async XLA Ops:
  0.0 35.1 %copy-start.16 = (f32[2,512]{1,0:T(2,128)S(1)}, f32[2,512]{1,0:T(2,128)}, u32[]{:S(2)}) copy-start(f32[2,512]{1,0:T(2,128)} %param.9) | copy-start | bytes 12292
  0.0 35.1 %copy-start.10 = (f32[128,512]{1,0:T(8,128)S(1)}, f32[128,512]{1,0:T(8,128)}, u32[]{:S(2)}) copy-start(f32[128,512]{1,0:T(8,128)} %param.8) | copy-start | bytes 786436
  0.0 19.8 %collective-permute-start.5 = (f32[1,128,512]{2,1,0:T(8,128)}, f32[1,128,512]{2,1,0:T(8,128)S(1)}, u32[]{:S(2)}, u32[]{:S(2)}) collective-permute-start(f32[1,128,512]{2,1,0:T(8,128)} %bitcast.19), channel_id=1, source_target_pairs={{0,2},{1,3},{2,0},{3,1},{4,6},{5,7},{6,4},{7,5},{8,10},{9,11},{10,... | collective-permute-start | bytes 786440 | tf_op jit(solution)/shard_map/ppermute | solution.py:31
  3.0 14.6 %collective-permute-start = (f32[1,128,512]{2,1,0:T(8,128)}, f32[1,128,512]{2,1,0:T(8,128)S(1)}, u32[]{:S(2)}, u32[]{:S(2)}) collective-permute-start(f32[1,128,512]{2,1,0:T(8,128)} %bitcast.20), channel_id=1, source_target_pairs={{0,4},{1,5},{2,6},{3,7},{4,0},{5,1},{6,2},{7,3},{8,12},{9,13},{10,... | collective-permute-start | bytes 786440 | tf_op jit(solution)/shard_map/ppermute | solution.py:31
  8.1 37.6 %collective-permute-start.2 = (f32[4,128,768]{2,1,0:T(8,128)}, f32[4,128,768]{2,1,0:T(8,128)S(1)}, u32[]{:S(2)}, u32[]{:S(2)}) collective-permute-start(f32[4,128,768]{2,1,0:T(8,128)} %shard_map.65), channel_id=1, source_target_pairs={{0,1},{1,0},{2,3},{3,2},{4,5},{5,4},{6,7},{7,6},{8,9},{9,8},{10,11... | collective-permute-start | bytes 4718600 | tf_op jit(solution)/shard_map/ppermute | solution.py:31
  17.6 7.4 %copy-start.12 = (f32[1,128,512]{2,1,0:T(8,128)}, f32[1,128,512]{2,1,0:T(8,128)S(1)}, u32[]{:S(2)}) copy-start(f32[1,128,512]{2,1,0:T(8,128)S(1)} %collective-permute-done.refs_1_) | copy-start | bytes 786436
  17.6 7.4 %collective-permute-start.1 = (f32[1,128,512]{2,1,0:T(8,128)S(1)}, f32[1,128,512]{2,1,0:T(8,128)S(1)}, u32[]{:S(2)}, u32[]{:S(2)}) collective-permute-start(f32[1,128,512]{2,1,0:T(8,128)S(1)} %collective-permute-done.refs_1_), channel_id=1, source_target_pairs={{0,2},{1,3},{2,0},{3,1},{4,6},{5,7},{6,4},{7,5},{8,10},{9,11},{10,... | collective-permute-start | bytes 786440 | tf_op jit(solution)/shard_map/ppermute | solution.py:31
  18.1 11.5 %collective-permute-start.8 = (f32[2,512]{1,0:T(2,128)}, f32[2,512]{1,0:T(2,128)S(1)}, u32[]{:S(2)}, u32[]{:S(2)}) collective-permute-start(f32[2,512]{1,0:T(2,128)} %param.9), channel_id=1, source_target_pairs={{0,8},{8,0},{16,24},{24,16},{1,9},{9,1},{17,25},{25,17},{2,10},{10... | collective-permute-start | bytes 12296 | tf_op jit(solution)/shard_map/ppermute | solution.py:367
  18.1 11.5 %collective-permute-start.7 = (f32[2,512]{1,0:T(2,128)}, f32[2,512]{1,0:T(2,128)S(1)}, u32[]{:S(2)}, u32[]{:S(2)}) collective-permute-start(f32[2,512]{1,0:T(2,128)} %param.9), channel_id=1, source_target_pairs={{8,16},{24,0},{16,8},{0,24},{9,17},{25,1},{17,9},{1,25},{10,18},{2... | collective-permute-start | bytes 12296 | tf_op jit(solution)/shard_map/ppermute | solution.py:364
  19.8 5.2 %copy-start.11 = (f32[1,128,512]{2,1,0:T(8,128)}, f32[1,128,512]{2,1,0:T(8,128)S(1)}, u32[]{:S(2)}) copy-start(f32[1,128,512]{2,1,0:T(8,128)S(1)} %collective-permute-done.5.refs_2_) | copy-start | bytes 786436
  19.8 15.1 %collective-permute-start.3 = (f32[1,128,512]{2,1,0:T(8,128)}, f32[1,128,512]{2,1,0:T(8,128)S(1)}, u32[]{:S(2)}, u32[]{:S(2)}) collective-permute-start(f32[1,128,512]{2,1,0:T(8,128)} %bitcast.22), channel_id=1, source_target_pairs={{0,4},{1,5},{2,6},{3,7},{4,0},{5,1},{6,2},{7,3},{8,12},{9,13},{10,... | collective-permute-start | bytes 786440 | tf_op jit(solution)/shard_map/ppermute | solution.py:31
  28.0 38.6 %collective-permute-start.6 = (f32[4,128,512]{2,1,0:T(8,128)}, f32[4,128,512]{2,1,0:T(8,128)}, u32[]{:S(2)}, u32[]{:S(2)}) collective-permute-start(f32[4,128,512]{2,1,0:T(8,128)} %shard_map.67.near_ref), channel_id=1, source_target_pairs={{0,1},{1,0},{2,3},{3,2},{4,5},{5,4},{6,7},{7,6},{8,9},{9,8},{10,11... | collective-permute-start | bytes 3145736 | tf_op jit(solution)/shard_map/ppermute | solution.py:31
  29.6 32.1 %collective-permute-start.9 = (f32[4,128,512]{2,1,0:T(8,128)}, f32[4,128,512]{2,1,0:T(8,128)}, u32[]{:S(2)}, u32[]{:S(2)}) collective-permute-start(f32[4,128,512]{2,1,0:T(8,128)} %shard_map.67.near_ref), channel_id=1, source_target_pairs={{8,16},{24,0},{16,8},{0,24},{9,17},{25,1},{17,9},{1,25},{10,18},{2... | collective-permute-start | bytes 3145736 | tf_op jit(solution)/shard_map/ppermute | solution.py:364
  34.9 15.5 %copy-start.13 = (f32[1,128,512]{2,1,0:T(8,128)}, f32[1,128,512]{2,1,0:T(8,128)S(1)}, u32[]{:S(2)}) copy-start(f32[1,128,512]{2,1,0:T(8,128)S(1)} %collective-permute-done.3.refs_1_) | copy-start | bytes 786436
  34.9 15.5 %collective-permute-start.4 = (f32[1,128,512]{2,1,0:T(8,128)S(1)}, f32[1,128,512]{2,1,0:T(8,128)S(1)}, u32[]{:S(2)}, u32[]{:S(2)}) collective-permute-start(f32[1,128,512]{2,1,0:T(8,128)S(1)} %collective-permute-done.3.refs_1_), channel_id=1, source_target_pairs={{0,2},{1,3},{2,0},{3,1},{4,6},{5,7},{6,4},{7,5},{8,10},{9,11},{10,... | collective-permute-start | bytes 786440 | tf_op jit(solution)/shard_map/ppermute | solution.py:31
  35.1 24.4 %collective-permute-start.10 = (f32[1,128,512]{2,1,0:T(8,128)S(1)}, f32[1,128,512]{2,1,0:T(8,128)}, u32[]{:S(2)}, u32[]{:S(2)}) collective-permute-start(f32[1,128,512]{2,1,0:T(8,128)S(1)} %bitcast.24), channel_id=1, source_target_pairs={{0,2},{1,3},{2,0},{3,1},{4,6},{5,7},{6,4},{7,5},{8,10},{9,11},{10,... | collective-permute-start | bytes 786440 | tf_op jit(solution)/shard_map/ppermute | solution.py:31
  51.1 75.8 %all-to-all-start = ((f32[4,2,128,768]{3,2,1,0:T(8,128)}), f32[4,2,128,768]{3,2,1,0:T(8,128)S(1)}, u32[]{:S(2)}, u32[]{:S(2)}) async-start(f32[4,2,128,768]{3,2,1,0:T(8,128)} %shard_map.66), calls=%async_computation | async-start | bytes 6291456 | tf_op jit(solution)/shard_map/all_to_all | solution.py:345
  54.8 11.7 %copy-start.1 = (f32[4,128,512]{2,1,0:T(8,128)S(1)}, f32[4,128,512]{2,1,0:T(8,128)}, u32[]{:S(2)}) copy-start(f32[4,128,512]{2,1,0:T(8,128)} %shard_map.67.near_ref) | copy-start | bytes 3145732
  66.6 2.7 %collective-permute-start.11 = (f32[4,128,512]{2,1,0:T(8,128)S(1)}, f32[4,128,512]{2,1,0:T(8,128)S(1)}, u32[]{:S(2)}, u32[]{:S(2)}) collective-permute-start(f32[4,128,512]{2,1,0:T(8,128)S(1)} %copy-done.1), channel_id=1, source_target_pairs={{0,8},{8,0},{16,24},{24,16},{1,9},{9,1},{17,25},{25,17},{2,10},{10... | collective-permute-start | bytes 3145736 | tf_op jit(solution)/shard_map/ppermute | solution.py:367
  69.2 2.9 %copy-start.8 = (f32[4,128,512]{2,1,0:T(8,128)}, f32[4,128,512]{2,1,0:T(8,128)S(1)}, u32[]{:S(2)}) copy-start(f32[4,128,512]{2,1,0:T(8,128)S(1)} %collective-permute-done.11.near_ref) | copy-start | bytes 3145732
  69.2 2.9 %collective-permute-start.12 = (f32[4,128,512]{2,1,0:T(8,128)}, f32[4,128,512]{2,1,0:T(8,128)S(1)}, u32[]{:S(2)}, u32[]{:S(2)}) collective-permute-start(f32[4,128,512]{2,1,0:T(8,128)} %collective-permute-done.6.far_ref), channel_id=1, source_target_pairs={{0,8},{8,0},{16,24},{24,16},{1,9},{9,1},{17,25},{25,17},{2,10},{10... | collective-permute-start | bytes 3145736 | tf_op jit(solution)/shard_map/ppermute | solution.py:367
  72.1 27.1 %copy-start.9 = (f32[4,128,512]{2,1,0:T(8,128)}, f32[4,128,512]{2,1,0:T(8,128)S(1)}, u32[]{:S(2)}) copy-start(f32[4,128,512]{2,1,0:T(8,128)S(1)} %collective-permute-done.12.far_ref) | copy-start | bytes 3145732
  72.1 25.4 %collective-permute-start.14 = (f32[4,128,512]{2,1,0:T(8,128)}, f32[4,128,512]{2,1,0:T(8,128)S(1)}, u32[]{:S(2)}, u32[]{:S(2)}) collective-permute-start(f32[4,128,512]{2,1,0:T(8,128)} %shard_map.69.refs_8_), channel_id=1, source_target_pairs={{0,1},{1,0},{2,3},{3,2},{4,5},{5,4},{6,7},{7,6},{8,9},{9,8},{10,11... | collective-permute-start | bytes 3145736 | tf_op jit(solution)/shard_map/ppermute | solution.py:31
  73.6 25.6 %collective-permute-start.13 = (f32[4,128,512]{2,1,0:T(8,128)}, f32[4,128,512]{2,1,0:T(8,128)S(1)}, u32[]{:S(2)}, u32[]{:S(2)}) collective-permute-start(f32[4,128,512]{2,1,0:T(8,128)} %shard_map.69.refs_8_), channel_id=1, source_target_pairs={{8,16},{24,0},{16,8},{0,24},{9,17},{25,1},{17,9},{1,25},{10,18},{2... | collective-permute-start | bytes 3145736 | tf_op jit(solution)/shard_map/ppermute | solution.py:364
  97.5 28.5 %copy-start.2 = (f32[4,128,512]{2,1,0:T(8,128)}, f32[4,128,512]{2,1,0:T(8,128)S(1)}, u32[]{:S(2)}) copy-start(f32[4,128,512]{2,1,0:T(8,128)S(1)} %collective-permute-done.14.refs_9_) | copy-start | bytes 3145732
  99.2 26.8 %copy-start.3 = (f32[4,128,512]{2,1,0:T(8,128)}, f32[4,128,512]{2,1,0:T(8,128)S(1)}, u32[]{:S(2)}) copy-start(f32[4,128,512]{2,1,0:T(8,128)S(1)} %collective-permute-done.13.refs_12_) | copy-start | bytes 3145732
  99.2 25.4 %collective-permute-start.15 = (f32[4,128,512]{2,1,0:T(8,128)}, f32[4,128,512]{2,1,0:T(8,128)S(1)}, u32[]{:S(2)}, u32[]{:S(2)}) collective-permute-start(f32[4,128,512]{2,1,0:T(8,128)} %collective-permute-done.6.far_ref), channel_id=1, source_target_pairs={{8,16},{24,0},{16,8},{0,24},{9,17},{25,1},{17,9},{1,25},{10,18},{2... | collective-permute-start | bytes 3145736 | tf_op jit(solution)/shard_map/ppermute | solution.py:364
  100.5 25.5 %collective-permute-start.16 = (f32[4,128,512]{2,1,0:T(8,128)S(1)}, f32[4,128,512]{2,1,0:T(8,128)S(1)}, u32[]{:S(2)}, u32[]{:S(2)}) collective-permute-start(f32[4,128,512]{2,1,0:T(8,128)S(1)} %collective-permute-done.13.refs_12_), channel_id=1, source_target_pairs={{0,1},{1,0},{2,3},{3,2},{4,5},{5,4},{6,7},{7,6},{8,9},{9,8},{10,11... | collective-permute-start | bytes 3145736 | tf_op jit(solution)/shard_map/ppermute | solution.py:31
  126.9 4.3 %collective-permute-start.17 = (f32[4,128,512]{2,1,0:T(8,128)}, f32[4,128,512]{2,1,0:T(8,128)}, u32[]{:S(2)}, u32[]{:S(2)}) collective-permute-start(f32[4,128,512]{2,1,0:T(8,128)} %shard_map.69.refs_8_), channel_id=1, source_target_pairs={{0,8},{8,0},{16,24},{24,16},{1,9},{9,1},{17,25},{25,17},{2,10},{10... | collective-permute-start | bytes 3145736 | tf_op jit(solution)/shard_map/ppermute | solution.py:367
  126.9 7.9 %copy-start = (f32[4,2,128,768]{3,2,1,0:T(8,128)}, f32[4,2,128,768]{3,2,1,0:T(8,128)S(1)}, u32[]{:S(2)}) copy-start(f32[4,2,128,768]{3,2,1,0:T(8,128)S(1)} %all-to-all-done.refs_1_) | copy-start | bytes 9437188
  127.0 31.0 %all-to-all-start.1 = ((f32[8,128,256]{2,1,0:T(8,128)}), f32[8,128,256]{2,1,0:T(8,128)}, u32[]{:S(2)}, u32[]{:S(2)}) async-start(f32[8,128,256]{2,1,0:T(8,128)} %shard_map.64), calls=%async_computation.1 | async-start | bytes 2097152 | tf_op jit(solution)/shard_map/all_to_all | solution.py:345
  131.2 3.6 %collective-permute-start.18 = (f32[4,128,512]{2,1,0:T(8,128)}, f32[4,128,512]{2,1,0:T(8,128)S(1)}, u32[]{:S(2)}, u32[]{:S(2)}) collective-permute-start(f32[4,128,512]{2,1,0:T(8,128)} %copy-done.2), channel_id=1, source_target_pairs={{0,8},{8,0},{16,24},{24,16},{1,9},{9,1},{17,25},{25,17},{2,10},{10... | collective-permute-start | bytes 3145736 | tf_op jit(solution)/shard_map/ppermute | solution.py:367
  (6 other events, 5.9 us)

commit v4 on v3

--- a/solution.py
+++ b/solution.py
@@ -227,29 +227,57 @@
     )(state)
 
 
-def pair_kernel(begin, side_ref, state_ref, got_ref, out_ref, sem):
-    blocks = out_ref.shape[0]
-    copies = side_copies(
-        side_ref[0], state_ref, begin, [out_ref.at[z, 0] for z in range(blocks)], sem
-    )
+def kept_kernel(begin, side_ref, state_ref, out_ref, held, sem_in, sem_out):
+    blocks = held.shape[0]
+    refs = [held.at[z] for z in range(blocks)]
+    for copy in side_copies(side_ref[0], state_ref, begin, refs, sem_in):
+        copy.start()
+    pltpu.make_async_copy(held, held, sem_in).wait()
     for z in range(blocks):
-        copies.append(pltpu.make_async_copy(got_ref.at[z], out_ref.at[z, 1], sem))
-    for copy in copies:
-        copy.start()
-    pltpu.make_async_copy(out_ref, out_ref, sem).wait()
-
-
-def pair(side, state, got, begin):
-    blocks, ml, width = got.shape
-    return pl.pallas_call(
-        functools.partial(pair_kernel, begin),
+        pltpu.make_async_copy(held.at[z], out_ref.at[z, 0], sem_out).start()
+    pltpu.make_async_copy(held, held, sem_out).wait()
+
+
+def kept(side, state, groups, begin, width):
+    blocks, ml = groups // 2, state.shape[0]
+    return pl.pallas_call(
+        functools.partial(kept_kernel, begin),
         out_shape=jax.ShapeDtypeStruct((blocks, 2, ml, width), f32),
-        in_specs=[pl.BlockSpec(memory_space=pltpu.SMEM), anywhere, anywhere],
-        out_specs=in_vmem,
-        scratch_shapes=[pltpu.SemaphoreType.DMA],
-        compiler_params=pltpu.CompilerParams(vmem_limit_bytes=vmem_limit),
-        cost_estimate=small_cost,
-    )(side, state, got)
+        in_specs=[pl.BlockSpec(memory_space=pltpu.SMEM), anywhere],
+        out_specs=anywhere,
+        scratch_shapes=[
+            pltpu.VMEM((blocks, ml, width), f32),
+            pltpu.SemaphoreType.DMA,
+            pltpu.SemaphoreType.DMA,
+        ],
+        compiler_params=pltpu.CompilerParams(vmem_limit_bytes=vmem_limit),
+        cost_estimate=small_cost,
+    )(side, state)
+
+
+def filled_kernel(got_ref, old_ref, out_ref, held, sem_in, sem_out):
+    pltpu.make_async_copy(got_ref, held, sem_in).start()
+    pltpu.make_async_copy(held, held, sem_in).wait()
+    for z in range(held.shape[0]):
+        pltpu.make_async_copy(held.at[z], out_ref.at[z, 1], sem_out).start()
+    pltpu.make_async_copy(held, held, sem_out).wait()
+
+
+def filled(got, old):
+    return pl.pallas_call(
+        filled_kernel,
+        out_shape=jax.ShapeDtypeStruct(old.shape, f32),
+        in_specs=[anywhere, anywhere],
+        out_specs=anywhere,
+        scratch_shapes=[
+            pltpu.VMEM(got.shape, f32),
+            pltpu.SemaphoreType.DMA,
+            pltpu.SemaphoreType.DMA,
+        ],
+        input_output_aliases={1: 0},
+        compiler_params=pltpu.CompilerParams(vmem_limit_bytes=vmem_limit),
+        cost_estimate=small_cost,
+    )(got, old)
 
 
 def update(me, points, obs, parts, innov, order, taper, out, start, per_device):
@@ -338,9 +366,6 @@
     sides = [[i for i in range(groups) if i % 2 == s] for s in range(2)]
     my_side = (me % 2).astype(jnp.int32).reshape(1)
 
-    def exchanged(span, *deps):
-        return side(given(my_side, after(state, *deps), groups, *span))
-
     def assembled(blocks, within, *deps):
         return lax.all_to_all(
             after(blocks, *deps),
@@ -351,9 +376,9 @@
             axis_index_groups=within,
         )
 
-    def far_gathered(x, *deps):
+    def far_gathered(x, ahead, *deps):
         own, others, got = after(x[None], *deps), [], []
-        early = swap(own, "mem", bits[-2])
+        early = swap(own if ahead is None else after(own, ahead), "mem", bits[-2])
         for b in bits[:-2]:
             got.append(swap(join(own, *others) if others else own, "mem", b))
             others.append(got[-1])
@@ -369,15 +394,16 @@
     def side(x, *deps):
         return swap(after(x, *deps), "mem", 1)
 
-    obs_near, obs_got = far_gathered(obs_ensemble)
-    first = exchanged(spans[0])
-    inn_near, inn_got = far_gathered(innovations, obs_got[0])
+    give = given(my_side, state, groups, *spans[0])
+    first = side(give)
+    obs_near, obs_got = far_gathered(obs_ensemble, give)
+    inn_near, inn_got = far_gathered(innovations, None, obs_got[0])
     coord_beside = beside(obs_coords, obs_got[0])
     coord_beyond = cross(obs_coords, obs_got[0])
     taper = tapered(coord_beside, coord_beyond)
     obs_near_beyond = cross(obs_near, coord_beyond, coord_beside)
     obs_far = side(obs_near)
-    paired = pair(my_side, state, first, spans[0][0])
+    paired = filled(first, kept(my_side, state, groups, *spans[0]))
     points = [assembled(paired, sides, obs_got[-1], inn_got[-1])]
     obs_near_beside = beside(obs_near, obs_near_beyond, obs_far, taper, inn_near)
     pause = beside(obs_far, obs_near_beside)

time: 169 us -> 168 us (level)
  starting transfers between devices: 28.5 us -> 26.1 us
  Pallas kernels: 53.6 us -> 55.3 us
    ppermute x10, starting transfers between devices: 16.1 us -> 13.4 us  [swap(): return lax.ppermute(x, axis, [(i, i ^ distance) for i in range(size)])]
    pallas_call x1 -> x2, Pallas kernels: 3.5 us -> 5.15 us  [the longest x1 2.6 us: kept(): pl.pallas_call(functools.partial(kept_kernel, begin), out_shape=jax.Shape...]
  transfers between devices with their start and end apart: 21 -> 21, of which waited for: 12 -> 13; matrix products, arithmetic and copies ran while one was open for 4% -> 4% of each run, Pallas kernels for 25% -> 26%
where the time goes in v4:
time: 168 us
  waiting for transfers between devices  74.8 us (45%)
  Pallas kernels  55.3 us (33%)
  starting transfers between devices  26.1 us (16%)
  local copies, waits for them, and re-layouts  5.55 us (3%)
  other arithmetic  4.94 us (3%)
    ppermute x10, waiting for transfers between devices, swap(): return lax.ppermute(x, axis, [(i, i ^ distance) for i in range(size)])  45.9 us
    pallas_call x2, Pallas kernels, update(): pl.pallas_call(functools.partial(update_kernel, parts, order, first, star...  31.8 us
    ppermute x4, waiting for transfers between devices, cross(): return lax.ppermute(after(x, *deps), 'dom', across)  22.3 us
    ppermute x10, starting transfers between devices, swap(): return lax.ppermute(x, axis, [(i, i ^ distance) for i in range(size)])  13.4 us
    pallas_call x3, Pallas kernels, prep_obs(): pl.pallas_call(functools.partial(prep_obs_kernel, order), grid=(width //...  9.08 us
    all_to_all x2, starting transfers between devices, assembled(): lax.all_to_all(after(blocks, *deps), 'mem', split_axis=0, concat_axis=0,...  7.95 us
    ppermute x5, waiting for transfers between devices, beside(): return lax.ppermute(after(x, *deps), 'dom', chip)  5.4 us
    mul x1, other arithmetic, tapered(): taper.reshape(-1, tile_side, per_device) * mask[:, None, :]  4.6 us
  transfers between devices with their start and end apart: 21, of which 13 were waited for; matrix products, arithmetic and copies ran while one was open for 4% of the time, Pallas kernels for 26%

profile of v4, /device:TPU:0, one launch (start us, length us, event | category | flops | bytes accessed | tf_op | source)
XLA Modules:
  0.0 167.6 jit_solution(17900847851281404841)
XLA Ops:
  0.0 4.0 %collective-permute-start = (f32[1,128,512]{2,1,0:T(8,128)}, f32[1,128,512]{2,1,0:T(8,128)S(1)}, u32[]{:S(2)}, u32[]{:S(2)}) collective-permute-start(f32[1,128,512]{2,1,0:T(8,128)} %bitcast.19), channel_id=1, source_target_pairs={{0,4},{1,5},{2,6},{3,7},{4,0},{5,1},{6,2},{7,3},{8,12},{9,13},{10,... | collective-permute-start | bytes 786440 | tf_op jit(solution)/shard_map/ppermute | solution.py:31
  4.0 2.5 %shard_map.65 = f32[4,128,768]{2,1,0:T(8,128)} custom-call(s32[1]{0:T(128)} %bitcast.2.side_ref, f32[128,8192]{1,0:T(8,128)} %state_ref.4), custom_call_target="tpu_custom_call" | custom-call | flops 1000 | bytes 1000 | tf_op jit(solution)/shard_map/pallas_call | solution.py:198
  6.6 1.6 collective-permute-start.2
  8.2 1.6 collective-permute-start.5
  11.3 4.9 %collective-permute-done.refs_1_ = f32[1,128,512]{2,1,0:T(8,128)S(1)} collective-permute-done((f32[1,128,512]{2,1,0:T(8,128)}, f32[1,128,512]{2,1,0:T(8,128)S(1)}, u32[]{:S(2)}, u32[]{:S(2)}) %collective-permute-start) | collective-permute-done | bytes 262176 | tf_op jit(solution)/shard_map/ppermute | solution.py:31
  17.1 1.6 collective-permute-start.7
  18.8 2.6 %collective-permute-done.5.refs_2_ = f32[1,128,512]{2,1,0:T(8,128)S(1)} collective-permute-done((f32[1,128,512]{2,1,0:T(8,128)}, f32[1,128,512]{2,1,0:T(8,128)S(1)}, u32[]{:S(2)}, u32[]{:S(2)}) %collective-permute-start.5) | collective-permute-done | bytes 262176 | tf_op jit(solution)/shard_map/ppermute | solution.py:31
  22.2 6.7 %collective-permute-done.1.refs_3_ = f32[1,128,512]{2,1,0:T(8,128)S(1)} collective-permute-done((f32[1,128,512]{2,1,0:T(8,128)S(1)}, f32[1,128,512]{2,1,0:T(8,128)S(1)}, u32[]{:S(2)}, u32[]{:S(2)}) %collective-permute-start.1) | collective-permute-done | bytes 262176 | tf_op jit(solution)/shard_map/ppermute | solution.py:31
  29.6 2.3 %shard_map.68.near_ref = f32[4,128,512]{2,1,0:T(8,128)} custom-call(f32[1,128,512]{2,1,0:T(8,128)} %bitcast.21, f32[1,128,512]{2,1,0:T(8,128)} %copy-done.11, f32[1,128,512]{2,1,0:T(8,128)} %copy-done.13, f32[1,128,512]{2,1,0:T(8,128)} %copy-done.15), custom_call_target="tpu_custom_call" | custom-call | flops 1000 | bytes 1000 | tf_op jit(solution)/shard_map/pallas_call | solution.py:50
  32.9 1.7 %collective-permute-done.3.refs_1_ = f32[1,128,512]{2,1,0:T(8,128)S(1)} collective-permute-done((f32[1,128,512]{2,1,0:T(8,128)}, f32[1,128,512]{2,1,0:T(8,128)S(1)}, u32[]{:S(2)}, u32[]{:S(2)}) %collective-permute-start.3) | collective-permute-done | bytes 262176 | tf_op jit(solution)/shard_map/ppermute | solution.py:31
  34.6 2.6 %shard_map.66.old_ref = f32[4,2,128,768]{3,2,1,0:T(8,128)} custom-call(s32[1]{0:T(128)} %bitcast.2.side_ref, f32[128,8192]{1,0:T(8,128)} %state_ref.4), custom_call_target="tpu_custom_call" | custom-call | flops 1000 | bytes 1000 | tf_op jit(solution)/shard_map/pallas_call | solution.py:243
  37.4 2.0 %collective-permute-start.10 = (f32[1,128,512]{2,1,0:T(8,128)S(1)}, f32[1,128,512]{2,1,0:T(8,128)}, u32[]{:S(2)}, u32[]{:S(2)}) collective-permute-start(f32[1,128,512]{2,1,0:T(8,128)S(1)} %bitcast.24), channel_id=1, source_target_pairs={{0,2},{1,3},{2,0},{3,1},{4,6},{5,7},{6,4},{7,5},{8,10},{9,11},{10,... | collective-permute-start | bytes 786440 | tf_op jit(solution)/shard_map/ppermute | solution.py:31
  39.4 4.8 %collective-permute-done.2.got_ref = f32[4,128,768]{2,1,0:T(8,128)S(1)} collective-permute-done((f32[4,128,768]{2,1,0:T(8,128)}, f32[4,128,768]{2,1,0:T(8,128)S(1)}, u32[]{:S(2)}, u32[]{:S(2)}) %collective-permute-start.2) | collective-permute-done | bytes 1572896 | tf_op jit(solution)/shard_map/ppermute | solution.py:31
  45.4 2.6 %shard_map.67 = f32[4,2,128,768]{3,2,1,0:T(8,128)} custom-call(f32[4,128,768]{2,1,0:T(8,128)} %copy-done.6, f32[4,2,128,768]{3,2,1,0:T(8,128)} %shard_map.66.old_ref), custom_call_target="tpu_custom_call", output_to_operand_aliasing={{}: (1, {})} | custom-call | flops 1000 | bytes 1000 | tf_op jit(solution)/shard_map/pallas_call | solution.py:267
  48.7 3.7 %all-to-all-start = ((f32[4,2,128,768]{3,2,1,0:T(8,128)}), f32[4,2,128,768]{3,2,1,0:T(8,128)S(1)}, u32[]{:S(2)}, u32[]{:S(2)}) async-start(f32[4,2,128,768]{3,2,1,0:T(8,128)} %shard_map.67), calls=%async_computation | async-start | bytes 6291456 | tf_op jit(solution)/shard_map/all_to_all | solution.py:370
  52.5 4.6 %fusion.5.refs_14_ = f32[1536,1024]{1,0:T(8,128)} fusion(f32[12,1024]{1,0:T(8,128)S(1)} %bitcast.17, f32[1536]{0:T(1024)S(1)} %get-tuple-element.46, f32[1024]{0:T(1024)S(1)} %get-tuple-element.50, f32[1536]{0:T(1024)S(1)} %get-tuple-element.45, f32[1024]{0:T(1024)S(1)} %get-tuple-element.49), kind=kLoop, calls=%fused_computation.6 | loop fusion | flops 17301504 | bytes 6361088 | tf_op jit(solution)/shard_map/mul | solution.py:361
  57.1 2.2 %shard_map.70.refs_8_ = f32[4,128,512]{2,1,0:T(8,128)} custom-call(f32[1,128,512]{2,1,0:T(8,128)} %bitcast.23, f32[1,128,512]{2,1,0:T(8,128)} %copy-done.12, f32[1,128,512]{2,1,0:T(8,128)} %collective-permute-done.10.refs_2_, f32[1,128,512]{2,1,0:T(8,128)} %copy-done.14), custom_call_target="tpu_custom_call" | custom-call | flops 1000 | bytes 1000 | tf_op jit(solution)/shard_map/pallas_call | solution.py:50
  59.2 6.1 %collective-permute-done.6.far_ref = f32[4,128,512]{2,1,0:T(8,128)} collective-permute-done((f32[4,128,512]{2,1,0:T(8,128)}, f32[4,128,512]{2,1,0:T(8,128)}, u32[]{:S(2)}, u32[]{:S(2)}) %collective-permute-start.6) | collective-permute-done | bytes 1048608 | tf_op jit(solution)/shard_map/ppermute | solution.py:31
  65.3 2.7 %collective-permute-done.11.near_ref = f32[4,128,512]{2,1,0:T(8,128)S(1)} collective-permute-done((f32[4,128,512]{2,1,0:T(8,128)S(1)}, f32[4,128,512]{2,1,0:T(8,128)S(1)}, u32[]{:S(2)}, u32[]{:S(2)}) %collective-permute-start.11) | collective-permute-done | bytes 1048608 | tf_op jit(solution)/shard_map/ppermute | solution.py:392
  68.1 2.7 %collective-permute-done.12.far_ref = f32[4,128,512]{2,1,0:T(8,128)S(1)} collective-permute-done((f32[4,128,512]{2,1,0:T(8,128)}, f32[4,128,512]{2,1,0:T(8,128)S(1)}, u32[]{:S(2)}, u32[]{:S(2)}) %collective-permute-start.12) | collective-permute-done | bytes 1048608 | tf_op jit(solution)/shard_map/ppermute | solution.py:392
  70.9 1.5 collective-permute-start.14
  73.3 2.3 %shard_map.64 = f32[8,128,256]{2,1,0:T(8,128)} custom-call(f32[128,8192]{1,0:T(8,128)} %state_ref.4), custom_call_target="tpu_custom_call" | custom-call | flops 1000 | bytes 1000 | tf_op jit(solution)/shard_map/pallas_call | solution.py:219
  75.6 3.0 %shard_map.69 = (bf16[512,1024]{1,0:T(8,128)(2,1)}, bf16[512,1024]{1,0:T(8,128)(2,1)}) custom-call(f32[4,128,512]{2,1,0:T(8,128)} %shard_map.68.near_ref, f32[4,128,512]{2,1,0:T(8,128)} %collective-permute-done.6.far_ref), custom_call_target="tpu_custom_call" | custom-call | flops 1000 | bytes 1000 | tf_op jit(solution)/shard_map/pallas_call | solution.py:79
  78.6 17.6 %collective-permute-done.14.refs_9_ = f32[4,128,512]{2,1,0:T(8,128)S(1)} collective-permute-done((f32[4,128,512]{2,1,0:T(8,128)}, f32[4,128,512]{2,1,0:T(8,128)S(1)}, u32[]{:S(2)}, u32[]{:S(2)}) %collective-permute-start.14) | collective-permute-done | bytes 1048608 | tf_op jit(solution)/shard_map/ppermute | solution.py:31
  96.3 1.7 %collective-permute-done.13.refs_12_ = f32[4,128,512]{2,1,0:T(8,128)S(1)} collective-permute-done((f32[4,128,512]{2,1,0:T(8,128)}, f32[4,128,512]{2,1,0:T(8,128)S(1)}, u32[]{:S(2)}, u32[]{:S(2)}) %collective-permute-start.13) | collective-permute-done | bytes 1048608 | tf_op jit(solution)/shard_map/ppermute | solution.py:389
  99.7 3.0 %shard_map.71 = (bf16[512,1024]{1,0:T(8,128)(2,1)}, bf16[512,1024]{1,0:T(8,128)(2,1)}) custom-call(f32[4,128,512]{2,1,0:T(8,128)} %copy-done.8, f32[4,128,512]{2,1,0:T(8,128)} %copy-done.9), custom_call_target="tpu_custom_call" | custom-call | flops 1000 | bytes 1000 | tf_op jit(solution)/shard_map/pallas_call | solution.py:79
  102.7 20.6 %collective-permute-done.15.far_ref = f32[4,128,512]{2,1,0:T(8,128)S(1)} collective-permute-done((f32[4,128,512]{2,1,0:T(8,128)}, f32[4,128,512]{2,1,0:T(8,128)S(1)}, u32[]{:S(2)}, u32[]{:S(2)}) %collective-permute-start.15) | collective-permute-done | bytes 1048608 | tf_op jit(solution)/shard_map/ppermute | solution.py:389
  123.4 1.4 collective-permute-done.16.refs_13_
  125.7 4.2 %all-to-all-start.1 = ((f32[8,128,256]{2,1,0:T(8,128)}), f32[8,128,256]{2,1,0:T(8,128)}, u32[]{:S(2)}, u32[]{:S(2)}) async-start(f32[8,128,256]{2,1,0:T(8,128)} %shard_map.64), calls=%async_computation.1 | async-start | bytes 2097152 | tf_op jit(solution)/shard_map/all_to_all | solution.py:370
  130.5 3.0 %shard_map.72 = (bf16[512,1024]{1,0:T(8,128)(2,1)}, bf16[512,1024]{1,0:T(8,128)(2,1)}) custom-call(f32[4,128,512]{2,1,0:T(8,128)} %collective-permute-done.9.near_ref, f32[4,128,512]{2,1,0:T(8,128)} %copy-done.7), custom_call_target="tpu_custom_call" | custom-call | flops 1000 | bytes 1000 | tf_op jit(solution)/shard_map/pallas_call | solution.py:79
  134.6 20.9 %shard_map.73.refs_15_ = f32[1024,1024]{1,0:T(8,128)} custom-call(s32[1]{0:T(128)} %bitcast.refs_0_, f32[4,2,128,768]{3,2,1,0:T(8,128)} %copy-done, bf16[512,1024]{1,0:T(8,128)(2,1)} %get-tuple-element.30.refs_2_, bf16[512,1024]{1,0:T(8,128)(2,1)} %get-tuple-element.35.refs_3_, bf16[512,1024]{1,0:T(8,128)(2,1)} %get-tuple-element.38.refs_4_, ...), custom_call_target="tpu_custom_call" | custom-call | flops 1000 | bytes 1000 | tf_op jit(solution)/shard_map/pallas_call | solution.py:290
  156.7 11.0 %shard_map.74 = f32[1024,1024]{1,0:T(8,128)} custom-call(s32[1]{0:T(128)} %bitcast.refs_0_, f32[8,128,256]{2,1,0:T(8,128)} %all-to-all-done.1.refs_1_, bf16[512,1024]{1,0:T(8,128)(2,1)} %get-tuple-element.30.refs_2_, bf16[512,1024]{1,0:T(8,128)(2,1)} %get-tuple-element.35.refs_3_, ...), custom_call_target="tpu_custom_call", output_to_operand_aliasing={{}: (15, {})} | custom-call | flops 1000 | bytes 1000 | tf_op jit(solution)/shard_map/pallas_call | solution.py:290
  (73 shorter events, 13.0 us)
Async XLA Ops:
  0.0 16.3 %collective-permute-start = (f32[1,128,512]{2,1,0:T(8,128)}, f32[1,128,512]{2,1,0:T(8,128)S(1)}, u32[]{:S(2)}, u32[]{:S(2)}) collective-permute-start(f32[1,128,512]{2,1,0:T(8,128)} %bitcast.19), channel_id=1, source_target_pairs={{0,4},{1,5},{2,6},{3,7},{4,0},{5,1},{6,2},{7,3},{8,12},{9,13},{10,... | collective-permute-start | bytes 786440 | tf_op jit(solution)/shard_map/ppermute | solution.py:31
  6.6 30.8 %copy-start.16 = (f32[2,512]{1,0:T(2,128)S(1)}, f32[2,512]{1,0:T(2,128)}, u32[]{:S(2)}) copy-start(f32[2,512]{1,0:T(2,128)} %param.9) | copy-start | bytes 12292
  6.6 30.8 %copy-start.10 = (f32[128,512]{1,0:T(8,128)S(1)}, f32[128,512]{1,0:T(8,128)}, u32[]{:S(2)}) copy-start(f32[128,512]{1,0:T(8,128)} %param.8) | copy-start | bytes 786436
  6.6 37.6 %collective-permute-start.2 = (f32[4,128,768]{2,1,0:T(8,128)}, f32[4,128,768]{2,1,0:T(8,128)S(1)}, u32[]{:S(2)}, u32[]{:S(2)}) collective-permute-start(f32[4,128,768]{2,1,0:T(8,128)} %shard_map.65), channel_id=1, source_target_pairs={{0,1},{1,0},{2,3},{3,2},{4,5},{5,4},{6,7},{7,6},{8,9},{9,8},{10,11... | collective-permute-start | bytes 4718600 | tf_op jit(solution)/shard_map/ppermute | solution.py:31
  8.2 13.3 %collective-permute-start.5 = (f32[1,128,512]{2,1,0:T(8,128)}, f32[1,128,512]{2,1,0:T(8,128)S(1)}, u32[]{:S(2)}, u32[]{:S(2)}) collective-permute-start(f32[1,128,512]{2,1,0:T(8,128)} %bitcast.20), channel_id=1, source_target_pairs={{0,2},{1,3},{2,0},{3,1},{4,6},{5,7},{6,4},{7,5},{8,10},{9,11},{10,... | collective-permute-start | bytes 786440 | tf_op jit(solution)/shard_map/ppermute | solution.py:31
  16.3 12.6 %copy-start.11 = (f32[1,128,512]{2,1,0:T(8,128)}, f32[1,128,512]{2,1,0:T(8,128)S(1)}, u32[]{:S(2)}) copy-start(f32[1,128,512]{2,1,0:T(8,128)S(1)} %collective-permute-done.refs_1_) | copy-start | bytes 786436
  16.3 12.6 %collective-permute-start.1 = (f32[1,128,512]{2,1,0:T(8,128)S(1)}, f32[1,128,512]{2,1,0:T(8,128)S(1)}, u32[]{:S(2)}, u32[]{:S(2)}) collective-permute-start(f32[1,128,512]{2,1,0:T(8,128)S(1)} %collective-permute-done.refs_1_), channel_id=1, source_target_pairs={{0,2},{1,3},{2,0},{3,1},{4,6},{5,7},{6,4},{7,5},{8,10},{9,11},{10,... | collective-permute-start | bytes 786440 | tf_op jit(solution)/shard_map/ppermute | solution.py:31
  17.1 15.4 %collective-permute-start.8 = (f32[2,512]{1,0:T(2,128)}, f32[2,512]{1,0:T(2,128)S(1)}, u32[]{:S(2)}, u32[]{:S(2)}) collective-permute-start(f32[2,512]{1,0:T(2,128)} %param.9), channel_id=1, source_target_pairs={{0,8},{8,0},{16,24},{24,16},{1,9},{9,1},{17,25},{25,17},{2,10},{10... | collective-permute-start | bytes 12296 | tf_op jit(solution)/shard_map/ppermute | solution.py:392
  17.1 15.4 %collective-permute-start.7 = (f32[2,512]{1,0:T(2,128)}, f32[2,512]{1,0:T(2,128)S(1)}, u32[]{:S(2)}, u32[]{:S(2)}) collective-permute-start(f32[2,512]{1,0:T(2,128)} %param.9), channel_id=1, source_target_pairs={{8,16},{24,0},{16,8},{0,24},{9,17},{25,1},{17,9},{1,25},{10,18},{2... | collective-permute-start | bytes 12296 | tf_op jit(solution)/shard_map/ppermute | solution.py:389
  21.5 7.5 %copy-start.13 = (f32[1,128,512]{2,1,0:T(8,128)}, f32[1,128,512]{2,1,0:T(8,128)S(1)}, u32[]{:S(2)}) copy-start(f32[1,128,512]{2,1,0:T(8,128)S(1)} %collective-permute-done.5.refs_2_) | copy-start | bytes 786436
  21.5 13.2 %collective-permute-start.3 = (f32[1,128,512]{2,1,0:T(8,128)}, f32[1,128,512]{2,1,0:T(8,128)S(1)}, u32[]{:S(2)}, u32[]{:S(2)}) collective-permute-start(f32[1,128,512]{2,1,0:T(8,128)} %bitcast.22), channel_id=1, source_target_pairs={{0,4},{1,5},{2,6},{3,7},{4,0},{5,1},{6,2},{7,3},{8,12},{9,13},{10,... | collective-permute-start | bytes 786440 | tf_op jit(solution)/shard_map/ppermute | solution.py:31
  31.9 33.4 %collective-permute-start.6 = (f32[4,128,512]{2,1,0:T(8,128)}, f32[4,128,512]{2,1,0:T(8,128)}, u32[]{:S(2)}, u32[]{:S(2)}) collective-permute-start(f32[4,128,512]{2,1,0:T(8,128)} %shard_map.68.near_ref), channel_id=1, source_target_pairs={{0,1},{1,0},{2,3},{3,2},{4,5},{5,4},{6,7},{7,6},{8,9},{9,8},{10,11... | collective-permute-start | bytes 3145736 | tf_op jit(solution)/shard_map/ppermute | solution.py:31
  32.5 26.7 %collective-permute-start.9 = (f32[4,128,512]{2,1,0:T(8,128)}, f32[4,128,512]{2,1,0:T(8,128)}, u32[]{:S(2)}, u32[]{:S(2)}) collective-permute-start(f32[4,128,512]{2,1,0:T(8,128)} %shard_map.68.near_ref), channel_id=1, source_target_pairs={{8,16},{24,0},{16,8},{0,24},{9,17},{25,1},{17,9},{1,25},{10,18},{2... | collective-permute-start | bytes 3145736 | tf_op jit(solution)/shard_map/ppermute | solution.py:389
  34.6 13.3 %copy-start.12 = (f32[1,128,512]{2,1,0:T(8,128)}, f32[1,128,512]{2,1,0:T(8,128)S(1)}, u32[]{:S(2)}) copy-start(f32[1,128,512]{2,1,0:T(8,128)S(1)} %collective-permute-done.3.refs_1_) | copy-start | bytes 786436
  34.6 13.3 %collective-permute-start.4 = (f32[1,128,512]{2,1,0:T(8,128)S(1)}, f32[1,128,512]{2,1,0:T(8,128)S(1)}, u32[]{:S(2)}, u32[]{:S(2)}) collective-permute-start(f32[1,128,512]{2,1,0:T(8,128)S(1)} %collective-permute-done.3.refs_1_), channel_id=1, source_target_pairs={{0,2},{1,3},{2,0},{3,1},{4,6},{5,7},{6,4},{7,5},{8,10},{9,11},{10,... | collective-permute-start | bytes 786440 | tf_op jit(solution)/shard_map/ppermute | solution.py:31
  37.4 19.6 %collective-permute-start.10 = (f32[1,128,512]{2,1,0:T(8,128)S(1)}, f32[1,128,512]{2,1,0:T(8,128)}, u32[]{:S(2)}, u32[]{:S(2)}) collective-permute-start(f32[1,128,512]{2,1,0:T(8,128)S(1)} %bitcast.24), channel_id=1, source_target_pairs={{0,2},{1,3},{2,0},{3,1},{4,6},{5,7},{6,4},{7,5},{8,10},{9,11},{10,... | collective-permute-start | bytes 786440 | tf_op jit(solution)/shard_map/ppermute | solution.py:31
  48.7 77.0 %all-to-all-start = ((f32[4,2,128,768]{3,2,1,0:T(8,128)}), f32[4,2,128,768]{3,2,1,0:T(8,128)S(1)}, u32[]{:S(2)}, u32[]{:S(2)}) async-start(f32[4,2,128,768]{3,2,1,0:T(8,128)} %shard_map.67), calls=%async_computation | async-start | bytes 6291456 | tf_op jit(solution)/shard_map/all_to_all | solution.py:370
  52.4 12.9 %copy-start.1 = (f32[4,128,512]{2,1,0:T(8,128)S(1)}, f32[4,128,512]{2,1,0:T(8,128)}, u32[]{:S(2)}) copy-start(f32[4,128,512]{2,1,0:T(8,128)} %shard_map.68.near_ref) | copy-start | bytes 3145732
  65.3 2.7 %collective-permute-start.11 = (f32[4,128,512]{2,1,0:T(8,128)S(1)}, f32[4,128,512]{2,1,0:T(8,128)S(1)}, u32[]{:S(2)}, u32[]{:S(2)}) collective-permute-start(f32[4,128,512]{2,1,0:T(8,128)S(1)} %copy-done.1), channel_id=1, source_target_pairs={{0,8},{8,0},{16,24},{24,16},{1,9},{9,1},{17,25},{25,17},{2,10},{10... | collective-permute-start | bytes 3145736 | tf_op jit(solution)/shard_map/ppermute | solution.py:392
  68.0 2.9 %copy-start.8 = (f32[4,128,512]{2,1,0:T(8,128)}, f32[4,128,512]{2,1,0:T(8,128)S(1)}, u32[]{:S(2)}) copy-start(f32[4,128,512]{2,1,0:T(8,128)S(1)} %collective-permute-done.11.near_ref) | copy-start | bytes 3145732
  68.0 2.9 %collective-permute-start.12 = (f32[4,128,512]{2,1,0:T(8,128)}, f32[4,128,512]{2,1,0:T(8,128)S(1)}, u32[]{:S(2)}, u32[]{:S(2)}) collective-permute-start(f32[4,128,512]{2,1,0:T(8,128)} %collective-permute-done.6.far_ref), channel_id=1, source_target_pairs={{0,8},{8,0},{16,24},{24,16},{1,9},{9,1},{17,25},{25,17},{2,10},{10... | collective-permute-start | bytes 3145736 | tf_op jit(solution)/shard_map/ppermute | solution.py:392
  70.9 27.1 %copy-start.9 = (f32[4,128,512]{2,1,0:T(8,128)}, f32[4,128,512]{2,1,0:T(8,128)S(1)}, u32[]{:S(2)}) copy-start(f32[4,128,512]{2,1,0:T(8,128)S(1)} %collective-permute-done.12.far_ref) | copy-start | bytes 3145732
  70.9 25.4 %collective-permute-start.14 = (f32[4,128,512]{2,1,0:T(8,128)}, f32[4,128,512]{2,1,0:T(8,128)S(1)}, u32[]{:S(2)}, u32[]{:S(2)}) collective-permute-start(f32[4,128,512]{2,1,0:T(8,128)} %shard_map.70.refs_8_), channel_id=1, source_target_pairs={{0,1},{1,0},{2,3},{3,2},{4,5},{5,4},{6,7},{7,6},{8,9},{9,8},{10,11... | collective-permute-start | bytes 3145736 | tf_op jit(solution)/shard_map/ppermute | solution.py:31
  72.4 25.6 %collective-permute-start.13 = (f32[4,128,512]{2,1,0:T(8,128)}, f32[4,128,512]{2,1,0:T(8,128)S(1)}, u32[]{:S(2)}, u32[]{:S(2)}) collective-permute-start(f32[4,128,512]{2,1,0:T(8,128)} %shard_map.70.refs_8_), channel_id=1, source_target_pairs={{8,16},{24,0},{16,8},{0,24},{9,17},{25,1},{17,9},{1,25},{10,18},{2... | collective-permute-start | bytes 3145736 | tf_op jit(solution)/shard_map/ppermute | solution.py:389
  96.3 28.5 %copy-start.2 = (f32[4,128,512]{2,1,0:T(8,128)}, f32[4,128,512]{2,1,0:T(8,128)S(1)}, u32[]{:S(2)}) copy-start(f32[4,128,512]{2,1,0:T(8,128)S(1)} %collective-permute-done.14.refs_9_) | copy-start | bytes 3145732
  98.0 26.8 %copy-start.3 = (f32[4,128,512]{2,1,0:T(8,128)}, f32[4,128,512]{2,1,0:T(8,128)S(1)}, u32[]{:S(2)}) copy-start(f32[4,128,512]{2,1,0:T(8,128)S(1)} %collective-permute-done.13.refs_12_) | copy-start | bytes 3145732
  98.0 25.4 %collective-permute-start.15 = (f32[4,128,512]{2,1,0:T(8,128)}, f32[4,128,512]{2,1,0:T(8,128)S(1)}, u32[]{:S(2)}, u32[]{:S(2)}) collective-permute-start(f32[4,128,512]{2,1,0:T(8,128)} %collective-permute-done.6.far_ref), channel_id=1, source_target_pairs={{8,16},{24,0},{16,8},{0,24},{9,17},{25,1},{17,9},{1,25},{10,18},{2... | collective-permute-start | bytes 3145736 | tf_op jit(solution)/shard_map/ppermute | solution.py:389
  99.2 25.5 %collective-permute-start.16 = (f32[4,128,512]{2,1,0:T(8,128)S(1)}, f32[4,128,512]{2,1,0:T(8,128)S(1)}, u32[]{:S(2)}, u32[]{:S(2)}) collective-permute-start(f32[4,128,512]{2,1,0:T(8,128)S(1)} %collective-permute-done.13.refs_12_), channel_id=1, source_target_pairs={{0,1},{1,0},{2,3},{3,2},{4,5},{5,4},{6,7},{7,6},{8,9},{9,8},{10,11... | collective-permute-start | bytes 3145736 | tf_op jit(solution)/shard_map/ppermute | solution.py:31
  125.7 4.3 %collective-permute-start.17 = (f32[4,128,512]{2,1,0:T(8,128)}, f32[4,128,512]{2,1,0:T(8,128)}, u32[]{:S(2)}, u32[]{:S(2)}) collective-permute-start(f32[4,128,512]{2,1,0:T(8,128)} %shard_map.70.refs_8_), channel_id=1, source_target_pairs={{0,8},{8,0},{16,24},{24,16},{1,9},{9,1},{17,25},{25,17},{2,10},{10... | collective-permute-start | bytes 3145736 | tf_op jit(solution)/shard_map/ppermute | solution.py:392
  125.7 7.9 %copy-start = (f32[4,2,128,768]{3,2,1,0:T(8,128)}, f32[4,2,128,768]{3,2,1,0:T(8,128)S(1)}, u32[]{:S(2)}) copy-start(f32[4,2,128,768]{3,2,1,0:T(8,128)S(1)} %all-to-all-done.refs_1_) | copy-start | bytes 9437188
  125.7 31.0 %all-to-all-start.1 = ((f32[8,128,256]{2,1,0:T(8,128)}), f32[8,128,256]{2,1,0:T(8,128)}, u32[]{:S(2)}, u32[]{:S(2)}) async-start(f32[8,128,256]{2,1,0:T(8,128)} %shard_map.64), calls=%async_computation.1 | async-start | bytes 2097152 | tf_op jit(solution)/shard_map/all_to_all | solution.py:370
  130.0 3.6 %collective-permute-start.18 = (f32[4,128,512]{2,1,0:T(8,128)}, f32[4,128,512]{2,1,0:T(8,128)S(1)}, u32[]{:S(2)}, u32[]{:S(2)}) collective-permute-start(f32[4,128,512]{2,1,0:T(8,128)} %copy-done.2), channel_id=1, source_target_pairs={{0,8},{8,0},{16,24},{24,16},{1,9},{9,1},{17,25},{25,17},{2,10},{10... | collective-permute-start | bytes 3145736 | tf_op jit(solution)/shard_map/ppermute | solution.py:392
  (6 other events, 5.9 us)

commit v5 on v4

--- a/solution.py
+++ b/solution.py
@@ -108,7 +108,7 @@
     for r in range(local):
         paired = len(points.shape) == 4
         block = points.at[lax.div(me ^ r, 2), r % 2] if paired else points.at[me ^ r]
-        x_copies.append(pltpu.make_async_copy(block, total.at[pl.ds(r * ml, ml)], sem_x))
+        x_copies.append(pltpu.make_async_copy(block, total.at[pl.ds(r * ml, ml)], sem_x.at[r]))
     y_copies = []
     for i, (slot, at, size) in enumerate(parts):
         here = pl.ds(at, size)
@@ -130,14 +130,10 @@
             w_copies.append(pltpu.make_async_copy(inn[i].at[k], w.at[at, here], sem_w))
     for copy in x_copies + y_copies[0]:
         copy.start()
-    pltpu.make_async_copy(total, total, sem_x).wait()
-
-    def halves(i, carry):
-        at = pl.ds(pl.multiple_of(i * 128, 128), 128)
+    for r, copy in enumerate(x_copies):
+        copy.wait()
+        at = pl.ds(r * ml, ml)
         x_high[at, :], x_low[at, :] = split(total[at, :])
-        return carry
-
-    lax.fori_loop(0, members // 128, halves, 0)
     for copy in y_copies[1] + y_copies[2] + w_copies:
         copy.start()
 
@@ -302,7 +298,7 @@
             pltpu.VMEM((window_obs, width), f32),
             pltpu.VMEM((window_obs, width), bf16),
             pltpu.VMEM((window_obs, width), bf16),
-            pltpu.SemaphoreType.DMA,
+            pltpu.SemaphoreType.DMA((len(order),)),
             pltpu.SemaphoreType.DMA((3, 3)),
             pltpu.SemaphoreType.DMA,
             pltpu.SemaphoreType.DMA((len(order),)),

time: 168 us -> 168 us (level)
  no operation moved by 1% of the time
where the time goes in v5:
time: 168 us
  waiting for transfers between devices  75 us (45%)
  Pallas kernels  54.9 us (33%)
  starting transfers between devices  26.3 us (16%)
  local copies, waits for them, and re-layouts  5.55 us (3%)
  other arithmetic  4.94 us (3%)
    ppermute x10, waiting for transfers between devices, swap(): return lax.ppermute(x, axis, [(i, i ^ distance) for i in range(size)])  45.9 us
    pallas_call x2, Pallas kernels, update(): pl.pallas_call(functools.partial(update_kernel, parts, order, first, star...  31.4 us
    ppermute x4, waiting for transfers between devices, cross(): return lax.ppermute(after(x, *deps), 'dom', across)  22.3 us
    ppermute x10, starting transfers between devices, swap(): return lax.ppermute(x, axis, [(i, i ^ distance) for i in range(size)])  13.4 us
    pallas_call x3, Pallas kernels, prep_obs(): pl.pallas_call(functools.partial(prep_obs_kernel, order), grid=(width //...  9.08 us
    all_to_all x2, starting transfers between devices, assembled(): lax.all_to_all(after(blocks, *deps), 'mem', split_axis=0, concat_axis=0,...  8.13 us
    ppermute x5, waiting for transfers between devices, beside(): return lax.ppermute(after(x, *deps), 'dom', chip)  5.4 us
    mul x1, other arithmetic, tapered(): taper.reshape(-1, tile_side, per_device) * mask[:, None, :]  4.6 us
  transfers between devices with their start and end apart: 21, of which 13 were waited for; matrix products, arithmetic and copies ran while one was open for 4% of the time, Pallas kernels for 26%

profile of v5, /device:TPU:0, one launch (start us, length us, event | category | flops | bytes accessed | tf_op | source)
XLA Modules:
  0.0 167.8 jit_solution(3798663827665019167)
XLA Ops:
  0.0 4.0 %collective-permute-start = (f32[1,128,512]{2,1,0:T(8,128)}, f32[1,128,512]{2,1,0:T(8,128)S(1)}, u32[]{:S(2)}, u32[]{:S(2)}) collective-permute-start(f32[1,128,512]{2,1,0:T(8,128)} %bitcast.19), channel_id=1, source_target_pairs={{0,4},{1,5},{2,6},{3,7},{4,0},{5,1},{6,2},{7,3},{8,12},{9,13},{10,... | collective-permute-start | bytes 786440 | tf_op jit(solution)/shard_map/ppermute | solution.py:31
  4.0 2.5 %shard_map.65 = f32[4,128,768]{2,1,0:T(8,128)} custom-call(s32[1]{0:T(128)} %bitcast.2.side_ref, f32[128,8192]{1,0:T(8,128)} %state_ref.4), custom_call_target="tpu_custom_call" | custom-call | flops 1000 | bytes 1000 | tf_op jit(solution)/shard_map/pallas_call | solution.py:194
  6.6 1.6 collective-permute-start.2
  8.2 1.6 collective-permute-start.5
  11.3 4.9 %collective-permute-done.refs_1_ = f32[1,128,512]{2,1,0:T(8,128)S(1)} collective-permute-done((f32[1,128,512]{2,1,0:T(8,128)}, f32[1,128,512]{2,1,0:T(8,128)S(1)}, u32[]{:S(2)}, u32[]{:S(2)}) %collective-permute-start) | collective-permute-done | bytes 262176 | tf_op jit(solution)/shard_map/ppermute | solution.py:31
  17.1 1.6 collective-permute-start.7
  18.8 2.6 %collective-permute-done.5.refs_2_ = f32[1,128,512]{2,1,0:T(8,128)S(1)} collective-permute-done((f32[1,128,512]{2,1,0:T(8,128)}, f32[1,128,512]{2,1,0:T(8,128)S(1)}, u32[]{:S(2)}, u32[]{:S(2)}) %collective-permute-start.5) | collective-permute-done | bytes 262176 | tf_op jit(solution)/shard_map/ppermute | solution.py:31
  22.2 6.7 %collective-permute-done.1.refs_3_ = f32[1,128,512]{2,1,0:T(8,128)S(1)} collective-permute-done((f32[1,128,512]{2,1,0:T(8,128)S(1)}, f32[1,128,512]{2,1,0:T(8,128)S(1)}, u32[]{:S(2)}, u32[]{:S(2)}) %collective-permute-start.1) | collective-permute-done | bytes 262176 | tf_op jit(solution)/shard_map/ppermute | solution.py:31
  29.6 2.3 %shard_map.68.near_ref = f32[4,128,512]{2,1,0:T(8,128)} custom-call(f32[1,128,512]{2,1,0:T(8,128)} %bitcast.21, f32[1,128,512]{2,1,0:T(8,128)} %copy-done.11, f32[1,128,512]{2,1,0:T(8,128)} %copy-done.13, f32[1,128,512]{2,1,0:T(8,128)} %copy-done.15), custom_call_target="tpu_custom_call" | custom-call | flops 1000 | bytes 1000 | tf_op jit(solution)/shard_map/pallas_call | solution.py:50
  32.9 1.7 %collective-permute-done.3.refs_1_ = f32[1,128,512]{2,1,0:T(8,128)S(1)} collective-permute-done((f32[1,128,512]{2,1,0:T(8,128)}, f32[1,128,512]{2,1,0:T(8,128)S(1)}, u32[]{:S(2)}, u32[]{:S(2)}) %collective-permute-start.3) | collective-permute-done | bytes 262176 | tf_op jit(solution)/shard_map/ppermute | solution.py:31
  34.6 2.6 %shard_map.66.old_ref = f32[4,2,128,768]{3,2,1,0:T(8,128)} custom-call(s32[1]{0:T(128)} %bitcast.2.side_ref, f32[128,8192]{1,0:T(8,128)} %state_ref.4), custom_call_target="tpu_custom_call" | custom-call | flops 1000 | bytes 1000 | tf_op jit(solution)/shard_map/pallas_call | solution.py:239
  37.4 2.0 %collective-permute-start.10 = (f32[1,128,512]{2,1,0:T(8,128)S(1)}, f32[1,128,512]{2,1,0:T(8,128)}, u32[]{:S(2)}, u32[]{:S(2)}) collective-permute-start(f32[1,128,512]{2,1,0:T(8,128)S(1)} %bitcast.24), channel_id=1, source_target_pairs={{0,2},{1,3},{2,0},{3,1},{4,6},{5,7},{6,4},{7,5},{8,10},{9,11},{10,... | collective-permute-start | bytes 786440 | tf_op jit(solution)/shard_map/ppermute | solution.py:31
  39.4 4.8 %collective-permute-done.2.got_ref = f32[4,128,768]{2,1,0:T(8,128)S(1)} collective-permute-done((f32[4,128,768]{2,1,0:T(8,128)}, f32[4,128,768]{2,1,0:T(8,128)S(1)}, u32[]{:S(2)}, u32[]{:S(2)}) %collective-permute-start.2) | collective-permute-done | bytes 1572896 | tf_op jit(solution)/shard_map/ppermute | solution.py:31
  45.4 2.6 %shard_map.67 = f32[4,2,128,768]{3,2,1,0:T(8,128)} custom-call(f32[4,128,768]{2,1,0:T(8,128)} %copy-done.6, f32[4,2,128,768]{3,2,1,0:T(8,128)} %shard_map.66.old_ref), custom_call_target="tpu_custom_call", output_to_operand_aliasing={{}: (1, {})} | custom-call | flops 1000 | bytes 1000 | tf_op jit(solution)/shard_map/pallas_call | solution.py:263
  48.7 3.7 %all-to-all-start = ((f32[4,2,128,768]{3,2,1,0:T(8,128)}), f32[4,2,128,768]{3,2,1,0:T(8,128)S(1)}, u32[]{:S(2)}, u32[]{:S(2)}) async-start(f32[4,2,128,768]{3,2,1,0:T(8,128)} %shard_map.67), calls=%async_computation | async-start | bytes 6291456 | tf_op jit(solution)/shard_map/all_to_all | solution.py:366
  52.5 4.6 %fusion.5.refs_14_ = f32[1536,1024]{1,0:T(8,128)} fusion(f32[12,1024]{1,0:T(8,128)S(1)} %bitcast.17, f32[1536]{0:T(1024)S(1)} %get-tuple-element.46, f32[1024]{0:T(1024)S(1)} %get-tuple-element.50, f32[1536]{0:T(1024)S(1)} %get-tuple-element.45, f32[1024]{0:T(1024)S(1)} %get-tuple-element.49), kind=kLoop, calls=%fused_computation.6 | loop fusion | flops 17301504 | bytes 6361088 | tf_op jit(solution)/shard_map/mul | solution.py:357
  57.1 2.2 %shard_map.70.refs_8_ = f32[4,128,512]{2,1,0:T(8,128)} custom-call(f32[1,128,512]{2,1,0:T(8,128)} %bitcast.23, f32[1,128,512]{2,1,0:T(8,128)} %copy-done.12, f32[1,128,512]{2,1,0:T(8,128)} %collective-permute-done.10.refs_2_, f32[1,128,512]{2,1,0:T(8,128)} %copy-done.14), custom_call_target="tpu_custom_call" | custom-call | flops 1000 | bytes 1000 | tf_op jit(solution)/shard_map/pallas_call | solution.py:50
  59.2 6.1 %collective-permute-done.6.far_ref = f32[4,128,512]{2,1,0:T(8,128)} collective-permute-done((f32[4,128,512]{2,1,0:T(8,128)}, f32[4,128,512]{2,1,0:T(8,128)}, u32[]{:S(2)}, u32[]{:S(2)}) %collective-permute-start.6) | collective-permute-done | bytes 1048608 | tf_op jit(solution)/shard_map/ppermute | solution.py:31
  65.3 2.7 %collective-permute-done.11.near_ref = f32[4,128,512]{2,1,0:T(8,128)S(1)} collective-permute-done((f32[4,128,512]{2,1,0:T(8,128)S(1)}, f32[4,128,512]{2,1,0:T(8,128)S(1)}, u32[]{:S(2)}, u32[]{:S(2)}) %collective-permute-start.11) | collective-permute-done | bytes 1048608 | tf_op jit(solution)/shard_map/ppermute | solution.py:388
  68.1 2.7 %collective-permute-done.12.far_ref = f32[4,128,512]{2,1,0:T(8,128)S(1)} collective-permute-done((f32[4,128,512]{2,1,0:T(8,128)}, f32[4,128,512]{2,1,0:T(8,128)S(1)}, u32[]{:S(2)}, u32[]{:S(2)}) %collective-permute-start.12) | collective-permute-done | bytes 1048608 | tf_op jit(solution)/shard_map/ppermute | solution.py:388
  70.9 1.5 collective-permute-start.14
  73.3 2.3 %shard_map.64 = f32[8,128,256]{2,1,0:T(8,128)} custom-call(f32[128,8192]{1,0:T(8,128)} %state_ref.4), custom_call_target="tpu_custom_call" | custom-call | flops 1000 | bytes 1000 | tf_op jit(solution)/shard_map/pallas_call | solution.py:215
  75.6 3.0 %shard_map.69 = (bf16[512,1024]{1,0:T(8,128)(2,1)}, bf16[512,1024]{1,0:T(8,128)(2,1)}) custom-call(f32[4,128,512]{2,1,0:T(8,128)} %shard_map.68.near_ref, f32[4,128,512]{2,1,0:T(8,128)} %collective-permute-done.6.far_ref), custom_call_target="tpu_custom_call" | custom-call | flops 1000 | bytes 1000 | tf_op jit(solution)/shard_map/pallas_call | solution.py:79
  78.6 17.6 %collective-permute-done.14.refs_9_ = f32[4,128,512]{2,1,0:T(8,128)S(1)} collective-permute-done((f32[4,128,512]{2,1,0:T(8,128)}, f32[4,128,512]{2,1,0:T(8,128)S(1)}, u32[]{:S(2)}, u32[]{:S(2)}) %collective-permute-start.14) | collective-permute-done | bytes 1048608 | tf_op jit(solution)/shard_map/ppermute | solution.py:31
  96.3 1.7 %collective-permute-done.13.refs_12_ = f32[4,128,512]{2,1,0:T(8,128)S(1)} collective-permute-done((f32[4,128,512]{2,1,0:T(8,128)}, f32[4,128,512]{2,1,0:T(8,128)S(1)}, u32[]{:S(2)}, u32[]{:S(2)}) %collective-permute-start.13) | collective-permute-done | bytes 1048608 | tf_op jit(solution)/shard_map/ppermute | solution.py:385
  99.7 3.0 %shard_map.71 = (bf16[512,1024]{1,0:T(8,128)(2,1)}, bf16[512,1024]{1,0:T(8,128)(2,1)}) custom-call(f32[4,128,512]{2,1,0:T(8,128)} %copy-done.8, f32[4,128,512]{2,1,0:T(8,128)} %copy-done.9), custom_call_target="tpu_custom_call" | custom-call | flops 1000 | bytes 1000 | tf_op jit(solution)/shard_map/pallas_call | solution.py:79
  102.7 20.6 %collective-permute-done.15.far_ref = f32[4,128,512]{2,1,0:T(8,128)S(1)} collective-permute-done((f32[4,128,512]{2,1,0:T(8,128)}, f32[4,128,512]{2,1,0:T(8,128)S(1)}, u32[]{:S(2)}, u32[]{:S(2)}) %collective-permute-start.15) | collective-permute-done | bytes 1048608 | tf_op jit(solution)/shard_map/ppermute | solution.py:385
  125.7 4.4 %all-to-all-start.1 = ((f32[8,128,256]{2,1,0:T(8,128)}), f32[8,128,256]{2,1,0:T(8,128)}, u32[]{:S(2)}, u32[]{:S(2)}) async-start(f32[8,128,256]{2,1,0:T(8,128)} %shard_map.64), calls=%async_computation.1 | async-start | bytes 2097152 | tf_op jit(solution)/shard_map/all_to_all | solution.py:366
  130.7 3.0 %shard_map.72 = (bf16[512,1024]{1,0:T(8,128)(2,1)}, bf16[512,1024]{1,0:T(8,128)(2,1)}) custom-call(f32[4,128,512]{2,1,0:T(8,128)} %collective-permute-done.9.near_ref, f32[4,128,512]{2,1,0:T(8,128)} %copy-done.7), custom_call_target="tpu_custom_call" | custom-call | flops 1000 | bytes 1000 | tf_op jit(solution)/shard_map/pallas_call | solution.py:79
  134.7 20.5 %shard_map.73.refs_15_ = f32[1024,1024]{1,0:T(8,128)} custom-call(s32[1]{0:T(128)} %bitcast.refs_0_, f32[4,2,128,768]{3,2,1,0:T(8,128)} %copy-done, bf16[512,1024]{1,0:T(8,128)(2,1)} %get-tuple-element.30.refs_2_, bf16[512,1024]{1,0:T(8,128)(2,1)} %get-tuple-element.35.refs_3_, bf16[512,1024]{1,0:T(8,128)(2,1)} %get-tuple-element.38.refs_4_, ...), custom_call_target="tpu_custom_call" | custom-call | flops 1000 | bytes 1000 | tf_op jit(solution)/shard_map/pallas_call | solution.py:286
  155.3 1.4 all-to-all-done.1.refs_1_
  156.7 10.9 %shard_map.74 = f32[1024,1024]{1,0:T(8,128)} custom-call(s32[1]{0:T(128)} %bitcast.refs_0_, f32[8,128,256]{2,1,0:T(8,128)} %all-to-all-done.1.refs_1_, bf16[512,1024]{1,0:T(8,128)(2,1)} %get-tuple-element.30.refs_2_, bf16[512,1024]{1,0:T(8,128)(2,1)} %get-tuple-element.35.refs_3_, ...), custom_call_target="tpu_custom_call", output_to_operand_aliasing={{}: (15, {})} | custom-call | flops 1000 | bytes 1000 | tf_op jit(solution)/shard_map/pallas_call | solution.py:286
  (73 shorter events, 13.1 us)
Async XLA Ops:
  0.0 16.3 %collective-permute-start = (f32[1,128,512]{2,1,0:T(8,128)}, f32[1,128,512]{2,1,0:T(8,128)S(1)}, u32[]{:S(2)}, u32[]{:S(2)}) collective-permute-start(f32[1,128,512]{2,1,0:T(8,128)} %bitcast.19), channel_id=1, source_target_pairs={{0,4},{1,5},{2,6},{3,7},{4,0},{5,1},{6,2},{7,3},{8,12},{9,13},{10,... | collective-permute-start | bytes 786440 | tf_op jit(solution)/shard_map/ppermute | solution.py:31
  6.6 30.8 %copy-start.16 = (f32[2,512]{1,0:T(2,128)S(1)}, f32[2,512]{1,0:T(2,128)}, u32[]{:S(2)}) copy-start(f32[2,512]{1,0:T(2,128)} %param.9) | copy-start | bytes 12292
  6.6 30.8 %copy-start.10 = (f32[128,512]{1,0:T(8,128)S(1)}, f32[128,512]{1,0:T(8,128)}, u32[]{:S(2)}) copy-start(f32[128,512]{1,0:T(8,128)} %param.8) | copy-start | bytes 786436
  6.6 37.6 %collective-permute-start.2 = (f32[4,128,768]{2,1,0:T(8,128)}, f32[4,128,768]{2,1,0:T(8,128)S(1)}, u32[]{:S(2)}, u32[]{:S(2)}) collective-permute-start(f32[4,128,768]{2,1,0:T(8,128)} %shard_map.65), channel_id=1, source_target_pairs={{0,1},{1,0},{2,3},{3,2},{4,5},{5,4},{6,7},{7,6},{8,9},{9,8},{10,11... | collective-permute-start | bytes 4718600 | tf_op jit(solution)/shard_map/ppermute | solution.py:31
  8.2 13.3 %collective-permute-start.5 = (f32[1,128,512]{2,1,0:T(8,128)}, f32[1,128,512]{2,1,0:T(8,128)S(1)}, u32[]{:S(2)}, u32[]{:S(2)}) collective-permute-start(f32[1,128,512]{2,1,0:T(8,128)} %bitcast.20), channel_id=1, source_target_pairs={{0,2},{1,3},{2,0},{3,1},{4,6},{5,7},{6,4},{7,5},{8,10},{9,11},{10,... | collective-permute-start | bytes 786440 | tf_op jit(solution)/shard_map/ppermute | solution.py:31
  16.3 12.6 %copy-start.11 = (f32[1,128,512]{2,1,0:T(8,128)}, f32[1,128,512]{2,1,0:T(8,128)S(1)}, u32[]{:S(2)}) copy-start(f32[1,128,512]{2,1,0:T(8,128)S(1)} %collective-permute-done.refs_1_) | copy-start | bytes 786436
  16.3 12.6 %collective-permute-start.1 = (f32[1,128,512]{2,1,0:T(8,128)S(1)}, f32[1,128,512]{2,1,0:T(8,128)S(1)}, u32[]{:S(2)}, u32[]{:S(2)}) collective-permute-start(f32[1,128,512]{2,1,0:T(8,128)S(1)} %collective-permute-done.refs_1_), channel_id=1, source_target_pairs={{0,2},{1,3},{2,0},{3,1},{4,6},{5,7},{6,4},{7,5},{8,10},{9,11},{10,... | collective-permute-start | bytes 786440 | tf_op jit(solution)/shard_map/ppermute | solution.py:31
  17.1 15.4 %collective-permute-start.8 = (f32[2,512]{1,0:T(2,128)}, f32[2,512]{1,0:T(2,128)S(1)}, u32[]{:S(2)}, u32[]{:S(2)}) collective-permute-start(f32[2,512]{1,0:T(2,128)} %param.9), channel_id=1, source_target_pairs={{0,8},{8,0},{16,24},{24,16},{1,9},{9,1},{17,25},{25,17},{2,10},{10... | collective-permute-start | bytes 12296 | tf_op jit(solution)/shard_map/ppermute | solution.py:388
  17.1 15.4 %collective-permute-start.7 = (f32[2,512]{1,0:T(2,128)}, f32[2,512]{1,0:T(2,128)S(1)}, u32[]{:S(2)}, u32[]{:S(2)}) collective-permute-start(f32[2,512]{1,0:T(2,128)} %param.9), channel_id=1, source_target_pairs={{8,16},{24,0},{16,8},{0,24},{9,17},{25,1},{17,9},{1,25},{10,18},{2... | collective-permute-start | bytes 12296 | tf_op jit(solution)/shard_map/ppermute | solution.py:385
  21.5 7.5 %copy-start.13 = (f32[1,128,512]{2,1,0:T(8,128)}, f32[1,128,512]{2,1,0:T(8,128)S(1)}, u32[]{:S(2)}) copy-start(f32[1,128,512]{2,1,0:T(8,128)S(1)} %collective-permute-done.5.refs_2_) | copy-start | bytes 786436
  21.5 13.2 %collective-permute-start.3 = (f32[1,128,512]{2,1,0:T(8,128)}, f32[1,128,512]{2,1,0:T(8,128)S(1)}, u32[]{:S(2)}, u32[]{:S(2)}) collective-permute-start(f32[1,128,512]{2,1,0:T(8,128)} %bitcast.22), channel_id=1, source_target_pairs={{0,4},{1,5},{2,6},{3,7},{4,0},{5,1},{6,2},{7,3},{8,12},{9,13},{10,... | collective-permute-start | bytes 786440 | tf_op jit(solution)/shard_map/ppermute | solution.py:31
  31.9 33.4 %collective-permute-start.6 = (f32[4,128,512]{2,1,0:T(8,128)}, f32[4,128,512]{2,1,0:T(8,128)}, u32[]{:S(2)}, u32[]{:S(2)}) collective-permute-start(f32[4,128,512]{2,1,0:T(8,128)} %shard_map.68.near_ref), channel_id=1, source_target_pairs={{0,1},{1,0},{2,3},{3,2},{4,5},{5,4},{6,7},{7,6},{8,9},{9,8},{10,11... | collective-permute-start | bytes 3145736 | tf_op jit(solution)/shard_map/ppermute | solution.py:31
  32.5 26.7 %collective-permute-start.9 = (f32[4,128,512]{2,1,0:T(8,128)}, f32[4,128,512]{2,1,0:T(8,128)}, u32[]{:S(2)}, u32[]{:S(2)}) collective-permute-start(f32[4,128,512]{2,1,0:T(8,128)} %shard_map.68.near_ref), channel_id=1, source_target_pairs={{8,16},{24,0},{16,8},{0,24},{9,17},{25,1},{17,9},{1,25},{10,18},{2... | collective-permute-start | bytes 3145736 | tf_op jit(solution)/shard_map/ppermute | solution.py:385
  34.6 13.3 %copy-start.12 = (f32[1,128,512]{2,1,0:T(8,128)}, f32[1,128,512]{2,1,0:T(8,128)S(1)}, u32[]{:S(2)}) copy-start(f32[1,128,512]{2,1,0:T(8,128)S(1)} %collective-permute-done.3.refs_1_) | copy-start | bytes 786436
  34.6 13.3 %collective-permute-start.4 = (f32[1,128,512]{2,1,0:T(8,128)S(1)}, f32[1,128,512]{2,1,0:T(8,128)S(1)}, u32[]{:S(2)}, u32[]{:S(2)}) collective-permute-start(f32[1,128,512]{2,1,0:T(8,128)S(1)} %collective-permute-done.3.refs_1_), channel_id=1, source_target_pairs={{0,2},{1,3},{2,0},{3,1},{4,6},{5,7},{6,4},{7,5},{8,10},{9,11},{10,... | collective-permute-start | bytes 786440 | tf_op jit(solution)/shard_map/ppermute | solution.py:31
  37.4 19.6 %collective-permute-start.10 = (f32[1,128,512]{2,1,0:T(8,128)S(1)}, f32[1,128,512]{2,1,0:T(8,128)}, u32[]{:S(2)}, u32[]{:S(2)}) collective-permute-start(f32[1,128,512]{2,1,0:T(8,128)S(1)} %bitcast.24), channel_id=1, source_target_pairs={{0,2},{1,3},{2,0},{3,1},{4,6},{5,7},{6,4},{7,5},{8,10},{9,11},{10,... | collective-permute-start | bytes 786440 | tf_op jit(solution)/shard_map/ppermute | solution.py:31
  48.7 77.0 %all-to-all-start = ((f32[4,2,128,768]{3,2,1,0:T(8,128)}), f32[4,2,128,768]{3,2,1,0:T(8,128)S(1)}, u32[]{:S(2)}, u32[]{:S(2)}) async-start(f32[4,2,128,768]{3,2,1,0:T(8,128)} %shard_map.67), calls=%async_computation | async-start | bytes 6291456 | tf_op jit(solution)/shard_map/all_to_all | solution.py:366
  52.4 12.9 %copy-start.1 = (f32[4,128,512]{2,1,0:T(8,128)S(1)}, f32[4,128,512]{2,1,0:T(8,128)}, u32[]{:S(2)}) copy-start(f32[4,128,512]{2,1,0:T(8,128)} %shard_map.68.near_ref) | copy-start | bytes 3145732
  65.3 2.7 %collective-permute-start.11 = (f32[4,128,512]{2,1,0:T(8,128)S(1)}, f32[4,128,512]{2,1,0:T(8,128)S(1)}, u32[]{:S(2)}, u32[]{:S(2)}) collective-permute-start(f32[4,128,512]{2,1,0:T(8,128)S(1)} %copy-done.1), channel_id=1, source_target_pairs={{0,8},{8,0},{16,24},{24,16},{1,9},{9,1},{17,25},{25,17},{2,10},{10... | collective-permute-start | bytes 3145736 | tf_op jit(solution)/shard_map/ppermute | solution.py:388
  68.0 2.9 %copy-start.8 = (f32[4,128,512]{2,1,0:T(8,128)}, f32[4,128,512]{2,1,0:T(8,128)S(1)}, u32[]{:S(2)}) copy-start(f32[4,128,512]{2,1,0:T(8,128)S(1)} %collective-permute-done.11.near_ref) | copy-start | bytes 3145732
  68.0 2.9 %collective-permute-start.12 = (f32[4,128,512]{2,1,0:T(8,128)}, f32[4,128,512]{2,1,0:T(8,128)S(1)}, u32[]{:S(2)}, u32[]{:S(2)}) collective-permute-start(f32[4,128,512]{2,1,0:T(8,128)} %collective-permute-done.6.far_ref), channel_id=1, source_target_pairs={{0,8},{8,0},{16,24},{24,16},{1,9},{9,1},{17,25},{25,17},{2,10},{10... | collective-permute-start | bytes 3145736 | tf_op jit(solution)/shard_map/ppermute | solution.py:388
  70.9 27.1 %copy-start.9 = (f32[4,128,512]{2,1,0:T(8,128)}, f32[4,128,512]{2,1,0:T(8,128)S(1)}, u32[]{:S(2)}) copy-start(f32[4,128,512]{2,1,0:T(8,128)S(1)} %collective-permute-done.12.far_ref) | copy-start | bytes 3145732
  70.9 25.4 %collective-permute-start.14 = (f32[4,128,512]{2,1,0:T(8,128)}, f32[4,128,512]{2,1,0:T(8,128)S(1)}, u32[]{:S(2)}, u32[]{:S(2)}) collective-permute-start(f32[4,128,512]{2,1,0:T(8,128)} %shard_map.70.refs_8_), channel_id=1, source_target_pairs={{0,1},{1,0},{2,3},{3,2},{4,5},{5,4},{6,7},{7,6},{8,9},{9,8},{10,11... | collective-permute-start | bytes 3145736 | tf_op jit(solution)/shard_map/ppermute | solution.py:31
  72.4 25.6 %collective-permute-start.13 = (f32[4,128,512]{2,1,0:T(8,128)}, f32[4,128,512]{2,1,0:T(8,128)S(1)}, u32[]{:S(2)}, u32[]{:S(2)}) collective-permute-start(f32[4,128,512]{2,1,0:T(8,128)} %shard_map.70.refs_8_), channel_id=1, source_target_pairs={{8,16},{24,0},{16,8},{0,24},{9,17},{25,1},{17,9},{1,25},{10,18},{2... | collective-permute-start | bytes 3145736 | tf_op jit(solution)/shard_map/ppermute | solution.py:385
  96.3 28.5 %copy-start.2 = (f32[4,128,512]{2,1,0:T(8,128)}, f32[4,128,512]{2,1,0:T(8,128)S(1)}, u32[]{:S(2)}) copy-start(f32[4,128,512]{2,1,0:T(8,128)S(1)} %collective-permute-done.14.refs_9_) | copy-start | bytes 3145732
  98.0 26.8 %copy-start.3 = (f32[4,128,512]{2,1,0:T(8,128)}, f32[4,128,512]{2,1,0:T(8,128)S(1)}, u32[]{:S(2)}) copy-start(f32[4,128,512]{2,1,0:T(8,128)S(1)} %collective-permute-done.13.refs_12_) | copy-start | bytes 3145732
  98.0 25.4 %collective-permute-start.15 = (f32[4,128,512]{2,1,0:T(8,128)}, f32[4,128,512]{2,1,0:T(8,128)S(1)}, u32[]{:S(2)}, u32[]{:S(2)}) collective-permute-start(f32[4,128,512]{2,1,0:T(8,128)} %collective-permute-done.6.far_ref), channel_id=1, source_target_pairs={{8,16},{24,0},{16,8},{0,24},{9,17},{25,1},{17,9},{1,25},{10,18},{2... | collective-permute-start | bytes 3145736 | tf_op jit(solution)/shard_map/ppermute | solution.py:385
  99.2 25.5 %collective-permute-start.16 = (f32[4,128,512]{2,1,0:T(8,128)S(1)}, f32[4,128,512]{2,1,0:T(8,128)S(1)}, u32[]{:S(2)}, u32[]{:S(2)}) collective-permute-start(f32[4,128,512]{2,1,0:T(8,128)S(1)} %collective-permute-done.13.refs_12_), channel_id=1, source_target_pairs={{0,1},{1,0},{2,3},{3,2},{4,5},{5,4},{6,7},{7,6},{8,9},{9,8},{10,11... | collective-permute-start | bytes 3145736 | tf_op jit(solution)/shard_map/ppermute | solution.py:31
  125.7 4.5 %collective-permute-start.17 = (f32[4,128,512]{2,1,0:T(8,128)}, f32[4,128,512]{2,1,0:T(8,128)}, u32[]{:S(2)}, u32[]{:S(2)}) collective-permute-start(f32[4,128,512]{2,1,0:T(8,128)} %shard_map.70.refs_8_), channel_id=1, source_target_pairs={{0,8},{8,0},{16,24},{24,16},{1,9},{9,1},{17,25},{25,17},{2,10},{10... | collective-permute-start | bytes 3145736 | tf_op jit(solution)/shard_map/ppermute | solution.py:388
  125.7 8.0 %copy-start = (f32[4,2,128,768]{3,2,1,0:T(8,128)}, f32[4,2,128,768]{3,2,1,0:T(8,128)S(1)}, u32[]{:S(2)}) copy-start(f32[4,2,128,768]{3,2,1,0:T(8,128)S(1)} %all-to-all-done.refs_1_) | copy-start | bytes 9437188
  125.7 31.0 %all-to-all-start.1 = ((f32[8,128,256]{2,1,0:T(8,128)}), f32[8,128,256]{2,1,0:T(8,128)}, u32[]{:S(2)}, u32[]{:S(2)}) async-start(f32[8,128,256]{2,1,0:T(8,128)} %shard_map.64), calls=%async_computation.1 | async-start | bytes 2097152 | tf_op jit(solution)/shard_map/all_to_all | solution.py:366
  130.2 3.6 %collective-permute-start.18 = (f32[4,128,512]{2,1,0:T(8,128)}, f32[4,128,512]{2,1,0:T(8,128)S(1)}, u32[]{:S(2)}, u32[]{:S(2)}) collective-permute-start(f32[4,128,512]{2,1,0:T(8,128)} %copy-done.2), channel_id=1, source_target_pairs={{0,8},{8,0},{16,24},{24,16},{1,9},{9,1},{17,25},{25,17},{2,10},{10... | collective-permute-start | bytes 3145736 | tf_op jit(solution)/shard_map/ppermute | solution.py:388
  (6 other events, 5.9 us)
